TPU v7x, 256 devices: a whole 4x4x8 slice. The times are simulated.
256 devices in a mesh: seq: 128 (over y, z, x), head: 2 (over core).
Axes of the slice: x: 4, y: 4, z: 8, core: 2. Of those that a mesh axis runs over, the one named last changes fastest.
Arguments:
- queries: bfloat16 [256, 73728], P('seq', 'head'), may hold values from -6 to 6
- cache: bfloat16 [16, 1024, 36864], P(None, 'seq'), may hold values from -6 to 6
- selected: int32 [256, 32], replicated, may hold values from 0 to 1023, as said below
Outputs:
- attended: bfloat16 [256, 65536], P('seq')
Inputs may be any that keep to these rules, and one draw needn't show every extreme that they name: `selected`: the 32 entries of one row are different blocks. The entries of the 2 rows on one index of seq (aligned runs of 2 rows) hold together at most 1 block of any range of 8 consecutive blocks starting at a multiple of 8, and exactly 1 of some range.
All inputs are finite; a program needn't handle non-finite values.
Results may differ from a plain program's by a relative error of at most 0.004.
Values may be sent and summed in bfloat16 or wider, within the bound.
No kernel may reach another device: no remote copies, remote signals or barrier semaphores. Data moves between devices by JAX's collectives and lax.ppermute only.
A program may use at most 192 MiB of HBM per device.

v0:
```python
import math

import jax
import jax.numpy as jnp
from jax import lax
from jax.sharding import PartitionSpec as P

KL = 512
KR = 64
BLOCK = 64
TOPK = 32
REQUESTS = 16
STEPS = 8
DRAFTS = 2


score_scale = 192.0 ** (-0.5)


def slot_partials(query_slots, key_slots, valid):
    count = query_slots.shape[0]
    slab = math.gcd(count, 128)
    pieces = count // slab

    def one_slab(items):
        query_rows, key_rows, live = items
        scores = (
            jnp.einsum("shk,stk->sht", query_rows, key_rows, preferred_element_type=jnp.float32)
            * score_scale
        )
        block_top = jnp.max(scores, axis=-1)
        weights = jnp.exp(scores - block_top[:, :, None])
        block_total = jnp.sum(weights, axis=-1)
        block_out = jnp.einsum(
            "sht,stv->shv",
            weights.astype(jnp.bfloat16),
            key_rows[:, :, :KL],
            preferred_element_type=jnp.float32,
        )
        block_top = jnp.where(live[:, None], block_top, -jnp.inf)
        return (block_out, block_top, block_total)

    outputs, tops, totals = lax.map(
        one_slab,
        (
            query_slots.reshape((pieces, slab) + query_slots.shape[1:]),
            key_slots.reshape((pieces, slab) + key_slots.shape[1:]),
            valid.reshape(pieces, slab),
        ),
    )
    return (
        outputs.reshape((count,) + outputs.shape[2:]),
        tops.reshape(count, -1),
        totals.reshape(count, -1),
    )


def combine(outputs, tops, totals, pick_slot, rows_dev):
    row_slots = pick_slot.reshape(rows_dev, TOPK)

    def one_row(slots):
        row_top = tops[slots]
        row_total = totals[slots]
        peak = jnp.max(row_top, axis=0)
        factor = jnp.exp(row_top - peak[None, :])
        denominator = jnp.sum(factor * row_total, axis=0)
        numerator = jnp.sum(factor[:, :, None] * outputs[slots], axis=0)
        return numerator / denominator[:, None]

    return lax.map(one_row, row_slots)


def per_device(queries, cache, selected):
    seq_count = lax.axis_size("seq")
    seq_index = lax.axis_index("seq")
    rows_dev = queries.shape[0]
    blk_dev = cache.shape[1]
    feature_width = KL + KR
    heads_dev = queries.shape[1] // feature_width
    capacity = max(1, rows_dev * TOPK // seq_count)
    picks_dev = rows_dev * TOPK
    slot_count = seq_count * capacity
    flat = selected.reshape(seq_count, picks_dev)
    owners = flat // blk_dev
    owner_ids = jnp.arange(seq_count, dtype=jnp.int32)
    slot_ids = jnp.arange(capacity, dtype=jnp.int32)
    pick_ids = jnp.arange(picks_dev, dtype=jnp.int32)
    hits = (owners[:, :, None] == owner_ids[None, None, :]).astype(jnp.int32)
    rank = jnp.sum(jnp.cumsum(hits, axis=1) * hits, axis=2) - 1
    my_owners = lax.dynamic_index_in_dim(owners, seq_index, 0, keepdims=False)
    my_rank = lax.dynamic_index_in_dim(rank, seq_index, 0, keepdims=False)
    pick_slot = my_owners * capacity + my_rank
    mine_match = (my_owners[None, None, :] == owner_ids[:, None, None]) & (
        my_rank[None, None, :] == slot_ids[None, :, None]
    )
    mine_pick = jnp.sum(jnp.where(mine_match, pick_ids[None, None, :], 0), axis=-1).reshape(-1)
    mine_row = mine_pick // TOPK
    held_match = (owners == seq_index)[:, None, :] & (rank[:, None, :] == slot_ids[None, :, None])
    held_pick = jnp.sum(jnp.where(held_match, pick_ids[None, None, :], 0), axis=-1)
    held_live = jnp.any(held_match, axis=-1)
    held_block = jnp.take_along_axis(flat, held_pick, axis=1) - seq_index * blk_dev
    held_block = jnp.where(held_live, held_block, 0)
    held_request = (owner_ids[:, None] * rows_dev + held_pick // TOPK) // (STEPS * DRAFTS)
    cache_rows = cache.reshape(REQUESTS * blk_dev, BLOCK * feature_width)
    held_keys = cache_rows[(held_request * blk_dev + held_block).reshape(-1)]
    held_valid = held_live.reshape(-1)
    outgoing = queries[mine_row]
    arrived = lax.all_to_all(outgoing, "seq", split_axis=0, concat_axis=0, tiled=True)
    outputs, tops, totals = slot_partials(
        arrived.reshape(slot_count, heads_dev, feature_width),
        held_keys.reshape(slot_count, BLOCK, feature_width),
        held_valid,
    )
    outputs, tops, totals = (
        lax.all_to_all(
            outputs.reshape(slot_count, heads_dev * KL),
            "seq",
            split_axis=0,
            concat_axis=0,
            tiled=True,
        ),
        lax.all_to_all(tops, "seq", split_axis=0, concat_axis=0, tiled=True),
        lax.all_to_all(totals, "seq", split_axis=0, concat_axis=0, tiled=True),
    )
    outputs = outputs.reshape(slot_count, heads_dev, KL)
    attended = combine(outputs, tops, totals, pick_slot, rows_dev)
    result = attended.astype(jnp.bfloat16).reshape(rows_dev, heads_dev * KL)
    return lax.all_gather(result, "head", axis=1, tiled=True)


def solution(mesh):
    placed = (P("seq", "head"), P(None, "seq", None), P())
    return jax.shard_map(
        per_device, mesh=mesh, in_specs=placed, out_specs=P("seq", None), check_vma=False
    )
```

profile of v0, /device:TPU:1, one launch (start us, length us, event | category | flops | bytes accessed | tf_op | source)
XLA Modules:
  0.0 903.0 jit_solution(16434885738511283466)
XLA Ops:
  0.0 0.0 copy-start
  0.0 0.9 copy.33
  0.9 0.1 reshape.665
  1.0 0.1 copy.34
  1.1 3.3 select_reduce_fusion
  4.4 0.2 dynamic-slice_reduce_fusion
  4.6 0.2 compare_reduce_fusion
  4.8 0.1 reshape.666
  4.9 0.1 copy.39
  5.0 0.1 fusion.22
  5.1 0.1 select_reduce_fusion.2
  5.2 0.0 copy-done
  5.2 10.3 %gather_fusion.3 = bf16[128,36864]{1,0:T(8,128)(2,1)} fusion(bf16[2,36864]{1,0:T(2,128)(2,1)S(1)} %copy-done, s32[1024]{0:T(1024)S(1)} %pad_clamp_fusion.2), kind=kCustom, calls=%fused_computation.3 | custom fusion | bytes 18874880 | tf_op jit(solution)/shard_map/gather | solution.py:107
  15.5 0.5 broadcast.702
  16.0 12.8 %reduce.11 = bf16[128,36864]{1,0:T(8,128)(2,1)} reduce(bf16[128,1,36864]{2,0,1:T(8,128)(2,1)} %bitcast.85, bf16[]{:T(256)} %broadcast.702), dimensions={1}, to_apply=%copy.43.reduce_sub_computation | reduce | bytes 18874370 | tf_op jit(solution)/shard_map/all_to_all | solution.py:108
  28.8 15.4 %reshape.722 = bf16[128,2,18432]{2,1,0:T(2,128)(2,1)} reshape(bf16[128,36864]{1,0:T(8,128)(2,1)} %reduce.11) | data formatting | bytes 18874368
  44.3 16.8 %all-to-all-start = ((bf16[128,2,18432]{2,1,0:T(2,128)(2,1)}), bf16[128,2,18432]{2,1,0:T(2,128)(2,1)}, u32[]{:S(2)}, u32[]{:S(2)}) async-start(bf16[128,2,18432]{2,1,0:T(2,128)(2,1)} %reshape.722), calls=%async_computation | async-start | bytes 18874368 | tf_op jit(solution)/shard_map/all_to_all | solution.py:108
  61.1 1.3 gather_fusion.5
  62.4 23.3 %gather_fusion.4 = bf16[128,36864]{1,0:T(8,128)(2,1)} fusion(bf16[128,36864]{1,0:T(8,128)(2,1)} %bitcast.82, s32[1024]{0:T(1024)S(1)} %pad_clamp_fusion.1), kind=kCustom, calls=%fused_computation.4 | custom fusion | bytes 18874880 | tf_op jit(solution)/shard_map/gather | solution.py:105
  85.7 12.7 %copy.45 = bf16[128,36864]{0,1:T(8,128)(2,1)} copy(bf16[128,36864]{1,0:T(8,128)(2,1)} %gather_fusion.4) | data formatting | bytes 18874368 | tf_op jit(solution)/shard_map/gather | solution.py:105
  98.4 14.8 %copy.47 = bf16[128,64,576]{2,1,0:T(8,128)(2,1)} copy(bf16[128,64,576]{0,2,1:T(8,128)(2,1)} %bitcast.87) | data formatting | bytes 18874368 | tf_op jit(solution)/shard_map/while/body/jit(dynamic_index_in_dim)/squeeze | solution.py:43
  113.3 152.4 %all-to-all-done = bf16[128,2,18432]{2,1,0:T(2,128)(2,1)} async-done(((bf16[128,2,18432]{2,1,0:T(2,128)(2,1)}), bf16[128,2,18432]{2,1,0:T(2,128)(2,1)}, u32[]{:S(2)}, u32[]{:S(2)}) %all-to-all-start) | async-done | bytes 9437216 | tf_op jit(solution)/shard_map/all_to_all | solution.py:108
  265.7 39.2 %reshape.723 = bf16[128,1,36864]{2,1,0:T(2,128)(2,1)} reshape(bf16[128,2,18432]{2,1,0:T(2,128)(2,1)} %all-to-all-done) | data formatting | bytes 18874368
  304.9 36.9 %copy.44 = bf16[128,1,36864]{0,2,1:T(8,128)(2,1)} copy(bf16[128,1,36864]{2,1,0:T(2,128)(2,1)} %reshape.723) | data formatting | bytes 18874368 | tf_op jit(solution)/shard_map/all_to_all | solution.py:108
  341.7 14.8 %copy.46 = bf16[128,64,576]{2,1,0:T(8,128)(2,1)} copy(bf16[128,64,576]{0,2,1:T(8,128)(2,1)} %bitcast.86) | data formatting | bytes 18874368 | tf_op jit(solution)/shard_map/while/body/jit(dynamic_index_in_dim)/squeeze | solution.py:43
  356.5 12.6 %multiply_reduce_fusion.2 = (f32[128,64]{1,0:T(8,128)S(1)}, f32[128,64,64]{1,2,0:T(8,128)}) fusion(bf16[128,64,576]{2,1,0:T(8,128)(2,1)} %copy.46, bf16[128,64,576]{2,1,0:T(8,128)(2,1)} %copy.47), kind=kOutput, calls=%fused_computation.21 | convolution fusion | flops 605020160 | bytes 21004288 | tf_op jit(solution)/shard_map/while/body/eval_jaxpr/shk,stk->sht/dot_general | solution.py:28
  369.1 0.8 broadcast_select_fusion
  370.0 11.4 %all-to-all-start.1 = ((f32[128,1,64]{2,1,0:T(1,128)}), f32[128,1,64]{2,1,0:T(1,128)S(1)}, u32[]{:S(2)}, u32[]{:S(2)}) async-start(f32[128,1,64]{2,1,0:T(1,128)} %broadcast_select_fusion), calls=%async_computation.1 | async-start | bytes 131072 | tf_op jit(solution)/shard_map/all_to_all | solution.py:122
  381.4 12.8 %fusion.2 = f32[128,64,512]{2,1,0:T(8,128)} fusion(bf16[128,64,576]{2,1,0:T(8,128)(2,1)} %copy.47, f32[128,64,64]{1,2,0:T(8,128)} %get-tuple-element.78, f32[128,64]{1,0:T(8,128)S(1)} %get-tuple-element.77), kind=kOutput, calls=%fused_computation.14 | convolution fusion | flops 538443776 | bytes 29392896 | tf_op jit(solution)/shard_map/while/body/eval_jaxpr/sht,stv->shv/dot_general | solution.py:34
  394.1 25.1 %all_to_all.35 = f32[128,1,32768]{2,1,0:T(1,128)} reshape(f32[128,64,512]{2,1,0:T(8,128)} %fusion.2) | data formatting | bytes 33554432 | tf_op jit(solution)/shard_map/all_to_all | solution.py:115
  419.3 0.0 all-to-all-done.1
  419.3 13.9 %all-to-all-start.2 = ((f32[128,1,32768]{2,1,0:T(1,128)}), f32[128,1,32768]{2,1,0:T(1,128)}, u32[]{:S(2)}, u32[]{:S(2)}) async-start(f32[128,1,32768]{2,1,0:T(1,128)} %all_to_all.35), calls=%async_computation.2 | async-start | bytes 33554432 | tf_op jit(solution)/shard_map/all_to_all | solution.py:115
  433.2 3.9 fusion.6
  437.1 357.9 %all-to-all-done.2 = f32[128,1,32768]{2,1,0:T(1,128)} async-done(((f32[128,1,32768]{2,1,0:T(1,128)}), f32[128,1,32768]{2,1,0:T(1,128)}, u32[]{:S(2)}, u32[]{:S(2)}) %all-to-all-start.2) | async-done | bytes 16777248 | tf_op jit(solution)/shard_map/all_to_all | solution.py:115
  795.0 14.2 %all-to-all-start.3 = ((f32[128,1,64]{2,1,0:T(1,128)}), f32[128,1,64]{2,1,0:T(1,128)S(1)}, u32[]{:S(2)}, u32[]{:S(2)}) async-start(f32[128,1,64]{2,1,0:T(1,128)} %bitcast.19), calls=%async_computation.3 | async-start | bytes 131072 | tf_op jit(solution)/shard_map/all_to_all | solution.py:123
  809.2 0.1 add.181
  809.3 47.3 %reduce.7 = f32[128,32768]{1,0:T(8,128)} reduce(f32[128,1,32768]{2,1,0:T(1,128)} %all-to-all-done.2, f32[]{:T(128)} %constant.155), dimensions={1}, to_apply=%all_to_all.31.reduce_sub_computation | reduce | bytes 33554436 | tf_op jit(solution)/shard_map/all_to_all | solution.py:115
  856.6 17.7 %copy.52 = f32[16,8,64,512]{3,2,1,0:T(8,128)} copy(f32[16,8,64,512]{3,1,2,0:T(8,128)} %bitcast.84) | data formatting | bytes 33554432
  874.3 0.0 all-to-all-done.3
  874.3 24.8 %while.2 = (s32[]{:T(128)}, bf16[2,64,512]{2,1,0:T(8,128)(2,1)S(1)}, s32[2,32]{1,0:T(2,128)S(1)}, f32[128,64]{1,0:T(8,128)S(1)}, f32[128,64,512]{2,1,0:T(8,128)}...) while((s32[]{:T(128)}, bf16[2,64,512]{2,1,0:T(8,128)(2,1)S(1)}, s32[2,32]{1,0:T(2,128)S(1)}, ...), condition=%wide.region_11.12_spmd, body=%wide.region_7.11_spmd.sunk | while | flops 2106338 | bytes 13056105 | solution.py:70
  874.3 8.5 gather_fusion
  882.8 0.6 gather_fusion.1
  883.4 0.6 gather_fusion.2
  884.0 2.5 multiply_reduce_fusion.6
  886.6 0.1 fusion.28
  886.7 8.5 gather_fusion
  895.2 0.6 gather_fusion.1
  895.8 0.6 gather_fusion.2
  896.4 2.5 multiply_reduce_fusion.6
  899.0 0.1 fusion.28
  899.1 0.0 copy-start.1
  899.1 0.1 copy.53
  899.2 2.7 all_gather.3
  901.9 0.7 copy.65
  902.6 0.0 copy-done.1
  (19 shorter events, 0.3 us)
Async XLA Ops:
  0.0 5.2 copy-start
  44.3 221.4 %all-to-all-start = ((bf16[128,2,18432]{2,1,0:T(2,128)(2,1)}), bf16[128,2,18432]{2,1,0:T(2,128)(2,1)}, u32[]{:S(2)}, u32[]{:S(2)}) async-start(bf16[128,2,18432]{2,1,0:T(2,128)(2,1)} %reshape.722), calls=%async_computation | async-start | bytes 18874368 | tf_op jit(solution)/shard_map/all_to_all | solution.py:108
  370.0 49.3 %all-to-all-start.1 = ((f32[128,1,64]{2,1,0:T(1,128)}), f32[128,1,64]{2,1,0:T(1,128)S(1)}, u32[]{:S(2)}, u32[]{:S(2)}) async-start(f32[128,1,64]{2,1,0:T(1,128)} %broadcast_select_fusion), calls=%async_computation.1 | async-start | bytes 131072 | tf_op jit(solution)/shard_map/all_to_all | solution.py:122
  419.3 375.7 %all-to-all-start.2 = ((f32[128,1,32768]{2,1,0:T(1,128)}), f32[128,1,32768]{2,1,0:T(1,128)}, u32[]{:S(2)}, u32[]{:S(2)}) async-start(f32[128,1,32768]{2,1,0:T(1,128)} %all_to_all.35), calls=%async_computation.2 | async-start | bytes 33554432 | tf_op jit(solution)/shard_map/all_to_all | solution.py:115
  795.0 79.3 %all-to-all-start.3 = ((f32[128,1,64]{2,1,0:T(1,128)}), f32[128,1,64]{2,1,0:T(1,128)S(1)}, u32[]{:S(2)}, u32[]{:S(2)}) async-start(f32[128,1,64]{2,1,0:T(1,128)} %bitcast.19), calls=%async_computation.3 | async-start | bytes 131072 | tf_op jit(solution)/shard_map/all_to_all | solution.py:123
  899.1 3.5 copy-start.1
where the time goes:
time: 916 us; the launch traced here: 903 us
  waiting for transfers between devices  510 us (56%)
  local copies, waits for them, and re-layouts  233 us (25%)
  other arithmetic  74.2 us (8%)
  starting transfers between devices  56.3 us (6%)
  matrix products  25.4 us (3%)
    all_to_all x1, waiting for transfers between devices, per_device(): lax.all_to_all(outputs.reshape(slot_count, heads_dev * KL), 'seq', split_...  358 us
    all_to_all x1, waiting for transfers between devices, per_device(): lax.all_to_all(outgoing, 'seq', split_axis=0, concat_axis=0, tiled=True)  152 us
    unnamed x11, local copies, waits for them, and re-layouts  74 us
    all_to_all x1, other arithmetic, per_device(): lax.all_to_all(outputs.reshape(slot_count, heads_dev * KL), 'seq', split_...  47.3 us
    all_to_all x2, local copies, waits for them, and re-layouts, per_device(): lax.all_to_all(outgoing, 'seq', split_axis=0, concat_axis=0, tiled=True)  37.4 us
    gather x2, local copies, waits for them, and re-layouts, per_device(): held_keys = cache_rows[(held_request * blk_dev + held_block).reshape(-1)]  36 us
    squeeze x2, local copies, waits for them, and re-layouts, slot_partials(): lax.map(one_slab, (query_slots.reshape((pieces, slab) + query_slots.shape...  29.6 us
    all_to_all x1, local copies, waits for them, and re-layouts, per_device(): lax.all_to_all(outputs.reshape(slot_count, heads_dev * KL), 'seq', split_...  25.1 us
  transfers between devices with their start and end apart: 4, of which 2 were waited for; matrix products, arithmetic and copies ran while one was open for 15% of the time, Pallas kernels for 0%

commit v1 on v0

v1 whole, which is shorter than its diff:
```python
import functools

import jax
import jax.numpy as jnp
from jax import lax
from jax.experimental import pallas as pl
from jax.experimental.pallas import tpu as pltpu
from jax.sharding import Mesh
from jax.sharding import PartitionSpec as P

KL = 512
KR = 64
FEAT = KL + KR
WIDE = KL + 2 * KR
BLOCK = 64
PAIRS = BLOCK // 2
PAIR_WIDTH = 2 * FEAT
TOPK = 32
RDEV = 2
BLK_DEV = 8
HEADS = 64
NY, NZ, NX = 4, 8, 4
PLANE = NY * NX
SEQ = NY * NZ * NX
ROWS_LOCAL = RDEV * HEADS
TAIL = 16
EMPTY = -1e30

score_scale = 192.0 ** (-0.5)

OFFSETS = (((4, 6), (3, 5)), ((2, 0), (1, 7)))

VMEM_LIMIT = 48 * 1024 * 1024


def pick_kernel(zd_ref, inner_ref, cache_ref, out_ref):
    base = (pl.program_id(1) * NZ + zd_ref[pl.program_id(0)]) * NX
    row = lax.broadcasted_iota(jnp.int32, (NX * PAIRS, BLK_DEV * PAIRS), 0)
    col = lax.broadcasted_iota(jnp.int32, (NX * PAIRS, BLK_DEV * PAIRS), 1)
    owner = row >> 5
    block = jnp.full(row.shape, inner_ref[base], jnp.int32)
    for i in range(1, NX):
        block = jnp.where(owner == i, inner_ref[base + i], block)
    hit = ((col >> 3) == (row & (PAIRS - 1))) & ((col & (BLK_DEV - 1)) == block)
    onehot = jnp.where(hit, 1.0, 0.0).astype(jnp.bfloat16)
    pieces = [
        cache_ref[0, :, p * PAIR_WIDTH : (p + 1) * PAIR_WIDTH].astype(jnp.float32)
        for p in range(PAIRS)
    ]
    stacked = jnp.concatenate(pieces, axis=0).astype(jnp.bfloat16)
    picked = jnp.dot(onehot, stacked, preferred_element_type=jnp.float32)
    out_ref[0, :, 0] = picked.astype(jnp.bfloat16).reshape(NX, PAIRS, PAIR_WIDTH)


def pick_blocks(zds, inner, cache):
    count = zds.shape[0]
    return pl.pallas_call(
        pick_kernel,
        out_shape=jax.ShapeDtypeStruct((NY, NX, count, PAIRS, PAIR_WIDTH), jnp.bfloat16),
        grid_spec=pltpu.PrefetchScalarGridSpec(
            num_scalar_prefetch=2,
            grid=(count, NY),
            in_specs=[
                pl.BlockSpec(
                    (1, BLK_DEV, BLOCK * FEAT),
                    lambda i, y, zd, inner: (y * (NZ // 2) + zd[i] // 2, 0, 0),
                )
            ],
            out_specs=pl.BlockSpec(
                (1, NX, 1, PAIRS, PAIR_WIDTH), lambda i, y, zd, inner: (y, 0, i, 0, 0)
            ),
        ),
        compiler_params=pltpu.CompilerParams(vmem_limit_bytes=VMEM_LIMIT),
        name="pick_blocks",
    )(zds, inner, cache)


def attend_kernel(zd_ref, core_ref, blocks_ref, near_ref, far_ref, live_ref, out_ref):
    pairs = blocks_ref[:, 0].reshape(PLANE * PAIRS, PAIR_WIDTH)
    query = jnp.concatenate([near_ref[0, 0], far_ref[0, 0]], axis=0)
    shifted = pltpu.roll(query.astype(jnp.float32), KR, 1).astype(jnp.bfloat16)
    live = live_ref[0]
    width = PLANE * PAIRS
    rows = [jnp.broadcast_to(live[j : j + 1], (HEADS, width)) for j in range(RDEV)]
    valid = jnp.concatenate(rows * 2, axis=0) > 0.5
    dims = (((1,), (1,)), ((), ()))
    even_keys = pairs[:, :WIDE]
    odd_keys = pairs[:, KL:]
    even = lax.dot_general(query, even_keys, dims, preferred_element_type=jnp.float32)
    odd = lax.dot_general(shifted, odd_keys, dims, preferred_element_type=jnp.float32)
    even = jnp.where(valid, even * score_scale, EMPTY)
    odd = jnp.where(valid, odd * score_scale, EMPTY)
    top = jnp.max(jnp.maximum(even, odd), axis=1, keepdims=True)
    even = jnp.where(valid, jnp.exp(even - top), 0.0)
    odd = jnp.where(valid, jnp.exp(odd - top), 0.0)
    total = jnp.maximum(jnp.sum(even + odd, axis=1, keepdims=True), 1.0)
    value = jnp.dot(
        even.astype(jnp.bfloat16), pairs[:, :KL], preferred_element_type=jnp.float32
    )
    odd_value = jnp.dot(odd.astype(jnp.bfloat16), odd_keys, preferred_element_type=jnp.float32)
    value = (value + odd_value[:, KR : KR + KL]) * (1.0 / total)
    level = top + jnp.log(total)
    across = jnp.transpose(jnp.broadcast_to(level, (2 * ROWS_LOCAL, 128)))
    line = lax.broadcasted_iota(jnp.int32, (TAIL, ROWS_LOCAL), 0)
    for half in range(2):
        span = slice(half * ROWS_LOCAL, (half + 1) * ROWS_LOCAL)
        out_ref[0, half, :ROWS_LOCAL] = value[span].astype(jnp.bfloat16)
        wide = across[:TAIL, span]
        high = wide.astype(jnp.bfloat16).astype(jnp.float32)
        middle = (wide - high).astype(jnp.bfloat16).astype(jnp.float32)
        low = wide - high - middle
        tail = jnp.where(line == 0, high, jnp.where(line == 1, middle, jnp.where(line == 2, low, 0.0)))
        out_ref[0, half, ROWS_LOCAL:, :ROWS_LOCAL] = tail.astype(jnp.bfloat16)
        out_ref[0, half, ROWS_LOCAL:, ROWS_LOCAL:] = jnp.zeros(
            (TAIL, KL - ROWS_LOCAL), jnp.bfloat16
        )


def attend(zds, core, blocks, queries, live):
    count = zds.shape[0]
    return pl.pallas_call(
        attend_kernel,
        out_shape=jax.ShapeDtypeStruct((count, 2, ROWS_LOCAL + TAIL, KL), jnp.bfloat16),
        grid_spec=pltpu.PrefetchScalarGridSpec(
            num_scalar_prefetch=2,
            grid=(count,),
            in_specs=[
                pl.BlockSpec((PLANE, 1, PAIRS, PAIR_WIDTH), lambda i, zd, core: (0, i, 0, 0)),
                pl.BlockSpec((1, 1, ROWS_LOCAL, WIDE), lambda i, zd, core: (zd[i], core[0], 0, 0)),
                pl.BlockSpec(
                    (1, 1, ROWS_LOCAL, WIDE), lambda i, zd, core: (zd[i], 1 - core[0], 0, 0)
                ),
                pl.BlockSpec((1, RDEV, PLANE * PAIRS), lambda i, zd, core: (zd[i], 0, 0)),
            ],
            out_specs=pl.BlockSpec(
                (1, 2, ROWS_LOCAL + TAIL, KL), lambda i, zd, core: (i, 0, 0, 0)
            ),
        ),
        compiler_params=pltpu.CompilerParams(vmem_limit_bytes=VMEM_LIMIT),
        name="attend",
    )(zds, core, blocks, queries, queries, live)


def merge_kernel(*refs):
    parts, out_ref = refs[:-1], refs[-1]
    levels = []
    for part in parts:
        tail = part[ROWS_LOCAL:, :ROWS_LOCAL].astype(jnp.float32)
        levels.append(jnp.sum(tail, axis=0, keepdims=True))
    peak = functools.reduce(jnp.maximum, levels)
    weights = [jnp.exp(level - peak) for level in levels]
    scale = 1.0 / functools.reduce(jnp.add, weights)
    total = jnp.zeros((ROWS_LOCAL, KL), jnp.float32)
    for part, weight in zip(parts, weights):
        column = jnp.transpose(jnp.broadcast_to(weight * scale, (128, ROWS_LOCAL)))
        factor = jnp.concatenate([column] * (KL // 128), axis=1)
        total = total + factor * part[:ROWS_LOCAL].astype(jnp.float32)
    out_ref[...] = total.astype(jnp.bfloat16).reshape(RDEV, HEADS, KL)


def merge(parts):
    return pl.pallas_call(
        merge_kernel,
        out_shape=jax.ShapeDtypeStruct((RDEV, HEADS, KL), jnp.bfloat16),
        compiler_params=pltpu.CompilerParams(vmem_limit_bytes=VMEM_LIMIT),
        name="merge",
    )(*parts)


def per_device(queries, cache, selected):
    y, z, x = lax.axis_index("y"), lax.axis_index("z"), lax.axis_index("x")
    core = lax.axis_index("head")
    me = (y * NZ + z) * NX + x

    by_chip = selected.reshape(SEQ, RDEV * TOPK)
    inner = jnp.max(jnp.where(by_chip // BLK_DEV == me, by_chip % BLK_DEV, -1), axis=1)

    padded = jnp.pad(queries.reshape(ROWS_LOCAL, FEAT), ((0, 0), (0, KR)))
    column_queries = lax.all_gather(padded, ("z", "head"), axis=0, tiled=False)
    column_queries = column_queries.reshape(NZ, 2, ROWS_LOCAL, WIDE)

    by_place = selected.reshape(NY, NZ, NX, RDEV, TOPK) // BLK_DEV
    column_owner = lax.dynamic_index_in_dim(by_place, y, 0, keepdims=False)
    column_owner = lax.dynamic_index_in_dim(column_owner, x, 1, keepdims=False)
    slot = jnp.arange(PLANE * PAIRS, dtype=jnp.int32) // PAIRS
    holder = ((slot // NX) * NZ + z) * NX + slot % NX
    live = jnp.any(column_owner[:, :, :, None] == holder, axis=2).astype(jnp.float32)

    core_id = core.astype(jnp.int32).reshape(1)
    offsets = jnp.array(OFFSETS, jnp.int32)
    my_offsets = lax.dynamic_index_in_dim(offsets, core, 1, keepdims=False)
    targets = (z + my_offsets) % NZ

    arrived = []
    for chunk in range(len(OFFSETS)):
        picked = pick_blocks(targets[chunk], inner, cache)
        picked = picked.reshape((PLANE,) + picked.shape[2:])
        arrived.append(
            lax.all_to_all(picked, ("y", "x"), split_axis=0, concat_axis=0, tiled=True)
        )
    parts = []
    for chunk, by_core in enumerate(OFFSETS):
        partial = attend(targets[chunk], core_id, arrived[chunk], column_queries, live)
        for i in range(len(by_core[0])):
            for cross in range(2):
                route = [
                    (zz * 2 + c, ((zz + by_core[c][i]) % NZ) * 2 + (c ^ cross))
                    for zz in range(NZ)
                    for c in range(2)
                ]
                parts.append(lax.ppermute(partial[i, cross], ("z", "head"), route))
    result = merge(parts).reshape(RDEV, HEADS * KL)
    return lax.all_gather(result, "head", axis=1, tiled=True)


def solution(mesh):
    grid = Mesh(mesh.devices.reshape(NY, NZ, NX, 2), ("y", "z", "x", "head"))
    seq = ("y", "z", "x")
    placed = (P(seq, "head"), P(None, seq, None), P())
    return jax.shard_map(
        per_device, mesh=grid, in_specs=placed, out_specs=P(seq, None), check_vma=False
    )
```

time: 916 us -> 145 us (0.16); the launches traced: 903 us -> 143 us
  waiting for transfers between devices: 510 us -> 57.3 us
  local copies, waits for them, and re-layouts: 233 us -> 9.98 us
  other arithmetic: 74.2 us -> 2.1 us
  matrix products: 25.4 us -> 0 us
  Pallas kernels: 0 us -> 21.9 us
  starting transfers between devices: 56.3 us -> 35.8 us
  between operations: 0.62 us -> 13.6 us
    all_to_all x4 -> x2, waiting for transfers between devices: 510 us -> 39.9 us  [per_device(): lax.all_to_all(picked, ('y', 'x'), split_axis=0, concat_axis=0, tiled=True)]
    gather x10 -> x0, local copies, waits for them, and re-layouts: 66.9 us -> none  [the longest x2 36 us: per_device(): held_keys = cache_rows[(held_request * blk_dev + held_block).reshape(-1)]]
    unnamed x11 -> x15, local copies, waits for them, and re-layouts: 74 us -> 7.25 us
    all_to_all x3 -> x0, local copies, waits for them, and re-layouts: 62.5 us -> none  [the longest x2 37.4 us: per_device(): lax.all_to_all(outgoing, 'seq', split_axis=0, concat_axis=0, tiled=True)]
    all_to_all x2 -> x0, other arithmetic: 60.1 us -> none  [the longest x1 47.3 us: per_device(): lax.all_to_all(outputs.reshape(slot_count, heads_dev * KL), 'seq', split_...]
    all_to_all x4 -> x2, starting transfers between devices: 56.3 us -> 12 us  [per_device(): lax.all_to_all(picked, ('y', 'x'), split_axis=0, concat_axis=0, tiled=True)]
    squeeze x2 -> x3, local copies, waits for them, and re-layouts: 29.6 us -> 0.8 us  [the longest x2 0.79 us: per_device(): parts.append(lax.ppermute(partial[i, cross], ('z', 'head'), route))]
    dot_general x2 -> x0, matrix products: 25.4 us -> none  [the longest x1 12.8 us: one_slab(): jnp.einsum('sht,stv->shv', weights.astype(jnp.bfloat16), key_rows[:, :, :...]
  transfers between devices with their start and end apart: 4 -> 11, of which waited for: 2 -> 6; matrix products, arithmetic and copies ran while one was open for 15% -> 2% of each run, Pallas kernels for 0% -> 15%
where the time goes in v1:
time: 145 us; the launch traced here: 143 us
  waiting for transfers between devices  57.3 us (40%)
  starting transfers between devices  35.8 us (25%)
  Pallas kernels  21.9 us (15%)
  between operations  13.6 us (9%)
  local copies, waits for them, and re-layouts  9.98 us (7%)
  other arithmetic  2.1 us (1%)
  blocking collectives  2.03 us (1%)
    all_to_all x2, waiting for transfers between devices, per_device(): lax.all_to_all(picked, ('y', 'x'), split_axis=0, concat_axis=0, tiled=True)  39.9 us
    ppermute x8, starting transfers between devices, per_device(): parts.append(lax.ppermute(partial[i, cross], ('z', 'head'), route))  23.7 us
    ppermute x8, waiting for transfers between devices, per_device(): parts.append(lax.ppermute(partial[i, cross], ('z', 'head'), route))  17.3 us
    pallas_call x2, Pallas kernels, pick_blocks(): pl.pallas_call(pick_kernel, out_shape=jax.ShapeDtypeStruct((NY, NX, count...  14.2 us
    all_to_all x2, starting transfers between devices, per_device(): lax.all_to_all(picked, ('y', 'x'), split_axis=0, concat_axis=0, tiled=True)  12 us
    pallas_call x2, Pallas kernels, attend(): pl.pallas_call(attend_kernel, out_shape=jax.ShapeDtypeStruct((count, 2, R...  7.46 us
    unnamed x15, local copies, waits for them, and re-layouts  7.25 us
  transfers between devices with their start and end apart: 11, of which 6 were waited for; matrix products, arithmetic and copies ran while one was open for 2% of the time, Pallas kernels for 15%

profile of v1, /device:TPU:1, one launch (start us, length us, event | category | flops | bytes accessed | tf_op | source)
XLA Modules:
  0.0 142.7 jit_solution(10560947813541651481)
XLA Ops:
  6.5 0.0 all-gather.3.cloned.1.call-start
  6.5 1.1 reshape.74
  7.6 0.7 pad.4
  8.3 0.0 all-gather.3.cloned.1.call-update
  8.4 0.8 fusion.2
  9.2 0.1 reduce_max.14
  9.3 0.1 reduce_max.18.inner_ref
  9.4 0.7 and_select_fusion.1
  10.1 6.5 %pick_blocks.3 = bf16[4,4,2,32,1152]{4,3,2,1,0:T(8,128)(2,1)S(1)} custom-call(s32[2]{0:T(128)S(1)} %get-tuple-element.13.zd_ref, s32[128]{0:T(128)S(1)} %reduce_max.18.inner_ref, bf16[16,8,36864]{2,1,0:T(8,128)(2,1)} %cache_ref.3), custom_call_target="tpu_custom_call" | custom-call | tf_op jit(solution)/shard_map/pick_blocks/pallas_call | solution.py:57
  16.6 0.0 copy-start.4
  16.6 1.4 %copy-done.4 = bf16[4,4,2,32,1152]{4,3,2,1,0:T(8,128)(2,1)} copy-done((bf16[4,4,2,32,1152]{4,3,2,1,0:T(8,128)(2,1)}, bf16[4,4,2,32,1152]{4,3,2,1,0:T(8,128)(2,1)S(1)}, u32[]{:S(2)}) %copy-start.4) | copy-done | bytes 2359320
  18.1 7.6 %all-to-all-start.1 = ((bf16[16,2,32,1152]{3,2,1,0:T(8,128)(2,1)}), bf16[16,2,32,1152]{3,2,1,0:T(8,128)(2,1)S(1)}, u32[]{:S(2)}, u32[]{:S(2)}) async-start(bf16[16,2,32,1152]{3,2,1,0:T(8,128)(2,1)} %bitcast.35), calls=%async_computation.1 | async-start | bytes 4718592 | tf_op jit(solution)/shard_map/all_to_all | solution.py:199
  25.7 7.7 %pick_blocks.2 = bf16[4,4,2,32,1152]{4,3,2,1,0:T(8,128)(2,1)} custom-call(s32[2]{0:T(128)S(1)} %get-tuple-element.14.zd_ref, s32[128]{0:T(128)S(1)} %reduce_max.18.inner_ref, bf16[16,8,36864]{2,1,0:T(8,128)(2,1)} %cache_ref.3), custom_call_target="tpu_custom_call" | custom-call | tf_op jit(solution)/shard_map/pick_blocks/pallas_call | solution.py:57
  33.4 26.9 %all-to-all-done.1.blocks_ref = bf16[16,2,32,1152]{3,2,1,0:T(8,128)(2,1)S(1)} async-done(((bf16[16,2,32,1152]{3,2,1,0:T(8,128)(2,1)}), bf16[16,2,32,1152]{3,2,1,0:T(8,128)(2,1)S(1)}, u32[]{:S(2)}, u32[]{:S(2)}) %all-to-all-start.1) | async-done | bytes 2359328 | tf_op jit(solution)/shard_map/all_to_all | solution.py:199
  60.3 0.0 copy-start.2
  60.3 0.0 copy-start.5
  60.3 1.5 %copy-done.2 = bf16[16,2,32,1152]{3,2,1,0:T(8,128)(2,1)} copy-done((bf16[16,2,32,1152]{3,2,1,0:T(8,128)(2,1)}, bf16[16,2,32,1152]{3,2,1,0:T(8,128)(2,1)S(1)}, u32[]{:S(2)}) %copy-start.2) | copy-done | bytes 2359320
  61.8 4.4 %all-to-all-start = ((bf16[16,2,32,1152]{3,2,1,0:T(8,128)(2,1)}), bf16[16,2,32,1152]{3,2,1,0:T(8,128)(2,1)}, u32[]{:S(2)}, u32[]{:S(2)}) async-start(bf16[16,2,32,1152]{3,2,1,0:T(8,128)(2,1)} %bitcast.3), calls=%async_computation | async-start | bytes 4718592 | tf_op jit(solution)/shard_map/all_to_all | solution.py:199
  66.2 0.0 copy-done.5
  66.2 0.1 copy.8
  66.4 0.1 broadcast_compare_fusion
  66.4 0.1 negate_select_fusion
  66.6 0.3 compare_reduce_fusion
  66.9 0.0 all-gather.3.cloned.1.call-done
  66.9 0.0 copy-start
  66.9 1.7 %copy-done = bf16[2048,640]{1,0:T(8,128)(2,1)S(1)} copy-done((bf16[2048,640]{1,0:T(8,128)(2,1)S(1)}, bf16[2048,640]{1,0:T(8,128)(2,1)}, u32[]{:S(2)}) %copy-start) | copy-done | bytes 2621464
  68.6 0.0 copy-start.3
  68.6 1.7 %copy-done.3 = bf16[16,2,32,1152]{3,2,1,0:T(8,128)(2,1)S(1)} copy-done((bf16[16,2,32,1152]{3,2,1,0:T(8,128)(2,1)S(1)}, bf16[16,2,32,1152]{3,2,1,0:T(8,128)(2,1)}, u32[]{:S(2)}) %copy-start.3) | copy-done | bytes 2359320
  70.3 0.0 copy-start.1
  70.3 3.2 %attend.3 = bf16[2,2,144,512]{3,2,1,0:T(8,128)(2,1)S(1)} custom-call(s32[2]{0:T(128)S(1)} %get-tuple-element.13.zd_ref, s32[1]{0:T(128)} %bitcast.2.core_ref, bf16[16,2,32,1152]{3,2,1,0:T(8,128)(2,1)S(1)} %copy-done.3, bf16[8,2,128,640]{3,2,1,0:T(8,128)(2,1)S(1)} %bitcast.31, bf16[8,2,128,640]{3,2,1,0:T(8,128)(2,1)S(1)} %bitcast.32, ...), custom_call_target="tpu_custom_call" | custom-call | tf_op jit(solution)/shard_map/attend/pallas_call | solution.py:121
  73.5 0.8 slice_bitcast_fusion
  74.3 7.3 %collective-permute-start.7 = (bf16[144,512]{1,0:T(8,128)(2,1)}, bf16[144,512]{1,0:T(8,128)(2,1)S(1)}, u32[]{:S(2)}, u32[]{:S(2)}) collective-permute-start(bf16[144,512]{1,0:T(8,128)(2,1)} %get-tuple-element.5), channel_id=1, source_target_pairs={{0,1},{1,56},{8,9},{9,0},{16,17},{17,8},{24,25},{25,16},{32,33},{3... | collective-permute-start | bytes 442376 | tf_op jit(solution)/shard_map/ppermute | solution.py:211
  81.6 2.6 %collective-permute-start.6 = (bf16[144,512]{1,0:T(8,128)(2,1)}, bf16[144,512]{1,0:T(8,128)(2,1)S(1)}, u32[]{:S(2)}, u32[]{:S(2)}) collective-permute-start(bf16[144,512]{1,0:T(8,128)(2,1)} %get-tuple-element.6), channel_id=1, source_target_pairs={{0,0},{1,57},{8,8},{9,1},{16,16},{17,9},{24,24},{25,17},{32,32},{3... | collective-permute-start | bytes 442376 | tf_op jit(solution)/shard_map/ppermute | solution.py:211
  84.2 0.1 collective-permute-start.5
  84.3 0.8 collective-permute-start.4
  85.1 12.9 %all-to-all-done.blocks_ref = bf16[16,2,32,1152]{3,2,1,0:T(8,128)(2,1)} async-done(((bf16[16,2,32,1152]{3,2,1,0:T(8,128)(2,1)}), bf16[16,2,32,1152]{3,2,1,0:T(8,128)(2,1)}, u32[]{:S(2)}, u32[]{:S(2)}) %all-to-all-start) | async-done | bytes 2359328 | tf_op jit(solution)/shard_map/all_to_all | solution.py:199
  98.0 0.0 copy-done.1
  98.0 4.3 %attend.2 = bf16[2,2,144,512]{3,2,1,0:T(8,128)(2,1)S(1)} custom-call(s32[2]{0:T(128)S(1)} %get-tuple-element.14.zd_ref, s32[1]{0:T(128)} %bitcast.2.core_ref, bf16[16,2,32,1152]{3,2,1,0:T(8,128)(2,1)} %all-to-all-done.blocks_ref, bf16[8,2,128,640]{3,2,1,0:T(8,128)(2,1)S(1)} %bitcast.33, bf16[8,2,128,640]{3,2,1,0:T(8,128)(2,1)S(1)} %bitcast.34, ...), custom_call_target="tpu_custom_call" | custom-call | tf_op jit(solution)/shard_map/attend/pallas_call | solution.py:121
  102.4 9.6 %collective-permute-start.3 = (bf16[144,512]{1,0:T(8,128)(2,1)S(1)}, bf16[144,512]{1,0:T(8,128)(2,1)S(1)}, u32[]{:S(2)}, u32[]{:S(2)}) collective-permute-start(bf16[144,512]{1,0:T(8,128)(2,1)S(1)} %get-tuple-element.9), channel_id=1, source_target_pairs={{0,49},{1,40},{8,57},{9,48},{16,1},{17,56},{24,9},{25,0},{32,17},{... | collective-permute-start | bytes 442376 | tf_op jit(solution)/shard_map/ppermute | solution.py:211
  112.0 0.0 collective-permute-done.7.refs_7_
  112.0 0.0 collective-permute-start.2
  112.0 0.0 collective-permute-done.6.refs_6_
  112.0 0.1 collective-permute-start.1
  112.1 0.0 collective-permute-done.5.refs_5_
  112.1 3.2 %collective-permute-start = (bf16[144,512]{1,0:T(8,128)(2,1)S(1)}, bf16[144,512]{1,0:T(8,128)(2,1)S(1)}, u32[]{:S(2)}, u32[]{:S(2)}) collective-permute-start(bf16[144,512]{1,0:T(8,128)(2,1)S(1)} %get-tuple-element.12), channel_id=1, source_target_pairs={{0,32},{1,25},{8,40},{9,33},{16,48},{17,41},{24,56},{25,49},{32,0}... | collective-permute-start | bytes 442376 | tf_op jit(solution)/shard_map/ppermute | solution.py:211
  115.3 0.0 collective-permute-done.4.refs_4_
  115.3 4.0 %collective-permute-done.3.refs_3_ = bf16[144,512]{1,0:T(8,128)(2,1)S(1)} collective-permute-done((bf16[144,512]{1,0:T(8,128)(2,1)S(1)}, bf16[144,512]{1,0:T(8,128)(2,1)S(1)}, u32[]{:S(2)}, u32[]{:S(2)}) %collective-permute-start.3) | collective-permute-done | bytes 147488 | tf_op jit(solution)/shard_map/ppermute | solution.py:211
  119.3 5.6 %collective-permute-done.2.refs_2_ = bf16[144,512]{1,0:T(8,128)(2,1)S(1)} collective-permute-done((bf16[144,512]{1,0:T(8,128)(2,1)S(1)}, bf16[144,512]{1,0:T(8,128)(2,1)S(1)}, u32[]{:S(2)}, u32[]{:S(2)}) %collective-permute-start.2) | collective-permute-done | bytes 147488 | tf_op jit(solution)/shard_map/ppermute | solution.py:211
  124.9 3.1 %collective-permute-done.1.refs_1_ = bf16[144,512]{1,0:T(8,128)(2,1)S(1)} collective-permute-done((bf16[144,512]{1,0:T(8,128)(2,1)S(1)}, bf16[144,512]{1,0:T(8,128)(2,1)S(1)}, u32[]{:S(2)}, u32[]{:S(2)}) %collective-permute-start.1) | collective-permute-done | bytes 147488 | tf_op jit(solution)/shard_map/ppermute | solution.py:211
  128.0 4.6 %collective-permute-done.refs_0_ = bf16[144,512]{1,0:T(8,128)(2,1)S(1)} collective-permute-done((bf16[144,512]{1,0:T(8,128)(2,1)S(1)}, bf16[144,512]{1,0:T(8,128)(2,1)S(1)}, u32[]{:S(2)}, u32[]{:S(2)}) %collective-permute-start) | collective-permute-done | bytes 147488 | tf_op jit(solution)/shard_map/ppermute | solution.py:211
  132.7 0.3 merge.1
  133.0 0.1 copy.12
  133.1 2.0 %all_gather.11 = bf16[2,65536]{1,0:T(2,128)(2,1)S(1)} all-gather(bf16[2,32768]{1,0:T(2,128)(2,1)S(1)} %bitcast.40), channel_id=1, replica_groups=mesh['y'=4,'z'=8,'x'=4,'head'=2] {'head'}, dimensions={1}, use_global_device_ids=true | all-gather | bytes 393216 | tf_op jit(solution)/shard_map/all_gather | solution.py:213
  135.2 0.7 copy.14
  (5 shorter events, 0.1 us)
Async XLA Ops:
  6.5 60.4 %all-gather.3.cloned.1.call-start = ((), (), s32[]{:S(2)}) async-start(), calls=%async_computation.2 | async-start | bytes 2785280 | tf_op jit(solution)/shard_map/all_gather | solution.py:179
  16.6 1.5 %copy-start.4 = (bf16[4,4,2,32,1152]{4,3,2,1,0:T(8,128)(2,1)}, bf16[4,4,2,32,1152]{4,3,2,1,0:T(8,128)(2,1)S(1)}, u32[]{:S(2)}) copy-start(bf16[4,4,2,32,1152]{4,3,2,1,0:T(8,128)(2,1)S(1)} %pick_blocks.3) | copy-start | bytes 7077892
  18.1 42.2 %all-to-all-start.1 = ((bf16[16,2,32,1152]{3,2,1,0:T(8,128)(2,1)}), bf16[16,2,32,1152]{3,2,1,0:T(8,128)(2,1)S(1)}, u32[]{:S(2)}, u32[]{:S(2)}) async-start(bf16[16,2,32,1152]{3,2,1,0:T(8,128)(2,1)} %bitcast.35), calls=%async_computation.1 | async-start | bytes 4718592 | tf_op jit(solution)/shard_map/all_to_all | solution.py:199
  60.3 1.5 %copy-start.2 = (bf16[16,2,32,1152]{3,2,1,0:T(8,128)(2,1)}, bf16[16,2,32,1152]{3,2,1,0:T(8,128)(2,1)S(1)}, u32[]{:S(2)}) copy-start(bf16[16,2,32,1152]{3,2,1,0:T(8,128)(2,1)S(1)} %all-to-all-done.1.blocks_ref) | copy-start | bytes 7077892
  60.3 5.9 %copy-start.5 = (s32[256,32]{0,1:T(8,128)S(1)}, s32[256,32]{0,1:T(8,128)}, u32[]{:S(2)}) copy-start(s32[256,32]{0,1:T(8,128)} %param.6) | copy-start | bytes 98308
  61.8 36.3 %all-to-all-start = ((bf16[16,2,32,1152]{3,2,1,0:T(8,128)(2,1)}), bf16[16,2,32,1152]{3,2,1,0:T(8,128)(2,1)}, u32[]{:S(2)}, u32[]{:S(2)}) async-start(bf16[16,2,32,1152]{3,2,1,0:T(8,128)(2,1)} %bitcast.3), calls=%async_computation | async-start | bytes 4718592 | tf_op jit(solution)/shard_map/all_to_all | solution.py:199
  66.9 1.7 %copy-start = (bf16[2048,640]{1,0:T(8,128)(2,1)S(1)}, bf16[2048,640]{1,0:T(8,128)(2,1)}, u32[]{:S(2)}) copy-start(bf16[2048,640]{1,0:T(8,128)(2,1)} %all-gather.3.cloned.1.call-done) | copy-start | bytes 7864324
  68.6 1.7 %copy-start.3 = (bf16[16,2,32,1152]{3,2,1,0:T(8,128)(2,1)S(1)}, bf16[16,2,32,1152]{3,2,1,0:T(8,128)(2,1)}, u32[]{:S(2)}) copy-start(bf16[16,2,32,1152]{3,2,1,0:T(8,128)(2,1)} %copy-done.2) | copy-start | bytes 7077892
  70.3 27.7 %copy-start.1 = (bf16[2048,640]{1,0:T(8,128)(2,1)S(1)}, bf16[2048,640]{1,0:T(8,128)(2,1)}, u32[]{:S(2)}) copy-start(bf16[2048,640]{1,0:T(8,128)(2,1)} %all-gather.3.cloned.1.call-done) | copy-start | bytes 7864324
  74.3 37.7 %collective-permute-start.7 = (bf16[144,512]{1,0:T(8,128)(2,1)}, bf16[144,512]{1,0:T(8,128)(2,1)S(1)}, u32[]{:S(2)}, u32[]{:S(2)}) collective-permute-start(bf16[144,512]{1,0:T(8,128)(2,1)} %get-tuple-element.5), channel_id=1, source_target_pairs={{0,1},{1,56},{8,9},{9,0},{16,17},{17,8},{24,25},{25,16},{32,33},{3... | collective-permute-start | bytes 442376 | tf_op jit(solution)/shard_map/ppermute | solution.py:211
  81.6 30.4 %collective-permute-start.6 = (bf16[144,512]{1,0:T(8,128)(2,1)}, bf16[144,512]{1,0:T(8,128)(2,1)S(1)}, u32[]{:S(2)}, u32[]{:S(2)}) collective-permute-start(bf16[144,512]{1,0:T(8,128)(2,1)} %get-tuple-element.6), channel_id=1, source_target_pairs={{0,0},{1,57},{8,8},{9,1},{16,16},{17,9},{24,24},{25,17},{32,32},{3... | collective-permute-start | bytes 442376 | tf_op jit(solution)/shard_map/ppermute | solution.py:211
  84.2 27.9 %collective-permute-start.5 = (bf16[144,512]{1,0:T(8,128)(2,1)S(1)}, bf16[144,512]{1,0:T(8,128)(2,1)S(1)}, u32[]{:S(2)}, u32[]{:S(2)}) collective-permute-start(bf16[144,512]{1,0:T(8,128)(2,1)S(1)} %get-tuple-element.7), channel_id=1, source_target_pairs={{0,17},{1,8},{8,25},{9,16},{16,33},{17,24},{24,41},{25,32},{32,49}... | collective-permute-start | bytes 442376 | tf_op jit(solution)/shard_map/ppermute | solution.py:211
  84.3 31.1 %collective-permute-start.4 = (bf16[144,512]{1,0:T(8,128)(2,1)S(1)}, bf16[144,512]{1,0:T(8,128)(2,1)S(1)}, u32[]{:S(2)}, u32[]{:S(2)}) collective-permute-start(bf16[144,512]{1,0:T(8,128)(2,1)S(1)} %get-tuple-element.8), channel_id=1, source_target_pairs={{0,16},{1,9},{8,24},{9,17},{16,32},{17,25},{24,40},{25,33},{32,48}... | collective-permute-start | bytes 442376 | tf_op jit(solution)/shard_map/ppermute | solution.py:211
  102.4 16.9 %collective-permute-start.3 = (bf16[144,512]{1,0:T(8,128)(2,1)S(1)}, bf16[144,512]{1,0:T(8,128)(2,1)S(1)}, u32[]{:S(2)}, u32[]{:S(2)}) collective-permute-start(bf16[144,512]{1,0:T(8,128)(2,1)S(1)} %get-tuple-element.9), channel_id=1, source_target_pairs={{0,49},{1,40},{8,57},{9,48},{16,1},{17,56},{24,9},{25,0},{32,17},{... | collective-permute-start | bytes 442376 | tf_op jit(solution)/shard_map/ppermute | solution.py:211
  112.0 12.9 %collective-permute-start.2 = (bf16[144,512]{1,0:T(8,128)(2,1)S(1)}, bf16[144,512]{1,0:T(8,128)(2,1)S(1)}, u32[]{:S(2)}, u32[]{:S(2)}) collective-permute-start(bf16[144,512]{1,0:T(8,128)(2,1)S(1)} %get-tuple-element.10), channel_id=1, source_target_pairs={{0,48},{1,41},{8,56},{9,49},{16,0},{17,57},{24,8},{25,1},{32,16},{... | collective-permute-start | bytes 442376 | tf_op jit(solution)/shard_map/ppermute | solution.py:211
  112.0 16.1 %collective-permute-start.1 = (bf16[144,512]{1,0:T(8,128)(2,1)S(1)}, bf16[144,512]{1,0:T(8,128)(2,1)S(1)}, u32[]{:S(2)}, u32[]{:S(2)}) collective-permute-start(bf16[144,512]{1,0:T(8,128)(2,1)S(1)} %get-tuple-element.11), channel_id=1, source_target_pairs={{0,33},{1,24},{8,41},{9,32},{16,49},{17,40},{24,57},{25,48},{32,1}... | collective-permute-start | bytes 442376 | tf_op jit(solution)/shard_map/ppermute | solution.py:211
  112.1 20.6 %collective-permute-start = (bf16[144,512]{1,0:T(8,128)(2,1)S(1)}, bf16[144,512]{1,0:T(8,128)(2,1)S(1)}, u32[]{:S(2)}, u32[]{:S(2)}) collective-permute-start(bf16[144,512]{1,0:T(8,128)(2,1)S(1)} %get-tuple-element.12), channel_id=1, source_target_pairs={{0,32},{1,25},{8,40},{9,33},{16,48},{17,41},{24,56},{25,49},{32,0}... | collective-permute-start | bytes 442376 | tf_op jit(solution)/shard_map/ppermute | solution.py:211
Sparse Core Ops, SparseCore 0:
  9.2 44.5 all-gather.2

commit v2 on v1

v2 whole, which is shorter than its diff:
```python
import functools

import jax
import jax.numpy as jnp
from jax import lax
from jax.experimental import pallas as pl
from jax.experimental.pallas import tpu as pltpu
from jax.sharding import Mesh
from jax.sharding import PartitionSpec as P

KL = 512
KR = 64
FEAT = KL + KR
WIDE = KL + 2 * KR
BLOCK = 64
PAIRS = BLOCK // 2
UNIT = PAIRS // 2
PAIR_WIDTH = 2 * FEAT
SPAN = UNIT * PAIR_WIDTH
TILES = PAIR_WIDTH // 128
TOPK = 32
RDEV = 2
BLK_DEV = 8
HEADS = 64
NY, NZ, NX = 4, 8, 4
NK = NZ // 2
GROUP = NY * 2 * NX
SEQ = NY * NZ * NX
ROWS = RDEV * HEADS
TAIL = 16
EMPTY = -1e30
MIB = 1024 * 1024

score_scale = 192.0 ** (-0.5)

STEPS = ((2, 1), (0, 3))
COUNT = len(STEPS)


def owner_of(i, meta):
    step = jnp.where(meta[2 * SEQ + 1] == 0, STEPS[i][0], STEPS[i][1])
    pair = meta[2 * SEQ] // (2 * NX) % NK
    return (pair + step) % NK * (2 * NX), meta[2 * SEQ] % (2 * NX)


def pick_kernel(i, meta_ref, cache_ref, *refs):
    out_ref = refs[-1]
    base = pl.program_id(0) * (NK * 2 * NX) + owner_of(i, meta_ref)[0]
    row = lax.broadcasted_iota(jnp.int32, (2 * NX * UNIT, BLK_DEV * UNIT), 0)
    col = lax.broadcasted_iota(jnp.int32, (2 * NX * UNIT, BLK_DEV * UNIT), 1)
    slot, token, held = row >> 4, (col >> 3) == (row & (UNIT - 1)), col & (BLK_DEV - 1)
    block = jnp.full(row.shape, -1, jnp.int32)
    for j in range(2 * NX):
        inner = jnp.maximum(meta_ref[2 * (base + j)], meta_ref[2 * (base + j) + 1])
        block = jnp.where(slot == j, inner, block)
    onehot = jnp.where(token & (held == block), 1.0, 0.0).astype(jnp.bfloat16)
    for half in range(2):
        pieces = [
            cache_ref[0, :, p * PAIR_WIDTH : (p + 1) * PAIR_WIDTH].astype(jnp.float32)
            for p in range(half * UNIT, (half + 1) * UNIT)
        ]
        stacked = jnp.concatenate(pieces, axis=0).astype(jnp.bfloat16)
        picked = jnp.dot(onehot, stacked, preferred_element_type=jnp.float32)
        picked = picked.astype(jnp.bfloat16).reshape(2 * NX, UNIT, PAIR_WIDTH)
        for t in range(TILES):
            out_ref[0, :, 0, t, half * UNIT : (half + 1) * UNIT] = picked[
                :, :, t * 128 : (t + 1) * 128
            ]


def pick_blocks(i, meta, cache, into=None, earlier=()):
    anywhere = pl.BlockSpec(memory_space=pl.ANY)
    more = () if into is None else (into,) + tuple(earlier)
    return pl.pallas_call(
        functools.partial(pick_kernel, i),
        out_shape=jax.ShapeDtypeStruct((NY, 2 * NX, COUNT, TILES, PAIRS, 128), jnp.bfloat16),
        grid_spec=pltpu.PrefetchScalarGridSpec(
            num_scalar_prefetch=1,
            grid=(NY,),
            in_specs=[
                pl.BlockSpec(
                    (1, BLK_DEV, BLOCK * FEAT),
                    lambda y, meta: (y * NK + owner_of(i, meta)[0] // (2 * NX), 0, 0),
                )
            ]
            + [anywhere] * len(more),
            out_specs=pl.BlockSpec(
                (1, 2 * NX, 1, TILES, PAIRS, 128), lambda y, meta: (y, 0, i, 0, 0, 0)
            ),
        ),
        input_output_aliases={} if into is None else {2: 0},
        compiler_params=pltpu.CompilerParams(vmem_limit_bytes=12 * MIB),
        name="pick_blocks",
    )(meta, cache, *more)


def attend_kernel(i, meta_ref, blocks_ref, near_ref, far_ref, selected_ref, _, near_out, far_out):
    width = GROUP * PAIRS
    pairs = jnp.concatenate(
        [blocks_ref[:, 0, t].reshape(width, 128) for t in range(TILES)], axis=1
    )
    query = jnp.concatenate([near_ref[...], far_ref[...]], axis=0)
    shifted = pltpu.roll(query.astype(jnp.float32), KR, 1).astype(jnp.bfloat16)
    pair, within = owner_of(i, meta_ref)
    here = meta_ref[2 * SEQ]
    owner = here // (NK * 2 * NX) * (NK * 2 * NX) + pair + within
    slot = lax.broadcasted_iota(jnp.int32, (1, width), 1) >> 5
    holder = (slot >> 3) * (NK * 2 * NX) + (here // (2 * NX) % NK * (2 * NX) + (slot & 7))
    places = selected_ref[...] >> 3
    lane = lax.broadcasted_iota(jnp.int32, places.shape, 1)
    rows = []
    for j in range(RDEV):
        mine = jnp.sum(jnp.where(lane == RDEV * owner + j, places, 0), axis=1, keepdims=True)
        read = jnp.max(jnp.where(mine == holder, 1.0, 0.0), axis=0, keepdims=True)
        rows.append(jnp.broadcast_to(read, (HEADS, width)))
    valid = jnp.concatenate(rows * 2, axis=0) > 0.5
    dims = (((1,), (1,)), ((), ()))
    odd_keys = pairs[:, KL:]
    even = lax.dot_general(query, pairs[:, :WIDE], dims, preferred_element_type=jnp.float32)
    odd = lax.dot_general(shifted, odd_keys, dims, preferred_element_type=jnp.float32)
    even = jnp.where(valid, even * score_scale, EMPTY)
    odd = jnp.where(valid, odd * score_scale, EMPTY)
    top = jnp.max(jnp.maximum(even, odd), axis=1, keepdims=True)
    even = jnp.where(valid, jnp.exp(even - top), 0.0)
    odd = jnp.where(valid, jnp.exp(odd - top), 0.0)
    total = jnp.maximum(jnp.sum(even + odd, axis=1, keepdims=True), 1.0)
    value = jnp.dot(
        even.astype(jnp.bfloat16), pairs[:, :KL], preferred_element_type=jnp.float32
    )
    odd_value = jnp.dot(odd.astype(jnp.bfloat16), odd_keys, preferred_element_type=jnp.float32)
    value = (value + odd_value[:, KR : KR + KL]) * (1.0 / total)
    value = value.astype(jnp.bfloat16)
    level = top + jnp.log(total)
    across = jnp.transpose(jnp.broadcast_to(level, (2 * ROWS, 128)))[:TAIL]
    for half, out_ref in enumerate((near_out, far_out)):
        span = slice(half * ROWS, (half + 1) * ROWS)
        wide = across[:, span]
        high = wide.astype(jnp.bfloat16).astype(jnp.float32)
        middle = (wide - high).astype(jnp.bfloat16).astype(jnp.float32)
        low = wide - high - middle
        line = lax.broadcasted_iota(jnp.int32, wide.shape, 0)
        tail = jnp.where(
            line == 0, high, jnp.where(line == 1, middle, jnp.where(line == 2, low, 0.0))
        )
        out_ref[:ROWS] = value[span]
        out_ref[ROWS:, :ROWS] = tail.astype(jnp.bfloat16)
        out_ref[ROWS:, ROWS:] = jnp.zeros((TAIL, KL - ROWS), jnp.bfloat16)


def attend(i, meta, blocks, near, far, selected, earlier):
    part = jax.ShapeDtypeStruct((ROWS + TAIL, KL), jnp.bfloat16)
    query = pl.BlockSpec((ROWS, WIDE), lambda n, meta: (0, 0))
    return pl.pallas_call(
        functools.partial(attend_kernel, i),
        out_shape=[part, part],
        grid_spec=pltpu.PrefetchScalarGridSpec(
            num_scalar_prefetch=1,
            grid=(1,),
            in_specs=[
                pl.BlockSpec((GROUP, 1, TILES, PAIRS, 128), lambda n, meta: (0, i, 0, 0, 0)),
                query,
                query,
                pl.BlockSpec(selected.shape, lambda n, meta: (0, 0)),
                pl.BlockSpec(memory_space=pl.ANY),
            ],
            out_specs=[pl.BlockSpec((ROWS + TAIL, KL), lambda n, meta: (0, 0))] * 2,
        ),
        compiler_params=pltpu.CompilerParams(vmem_limit_bytes=24 * MIB),
        cost_estimate=pl.CostEstimate(flops=1, bytes_accessed=1, transcendentals=0),
        name="attend",
    )(meta, blocks, near, far, selected, earlier)


def weigh(parts, levels):
    peak = functools.reduce(jnp.maximum, levels)
    weights = [jnp.exp(level - peak) for level in levels]
    total = functools.reduce(jnp.add, weights)
    scale = 1.0 / total
    mean = jnp.zeros((ROWS, KL), jnp.float32)
    for part, weight in zip(parts, weights):
        column = jnp.transpose(jnp.broadcast_to(weight * scale, (128, ROWS)))
        factor = jnp.concatenate([column] * (KL // 128), axis=1)
        mean = mean + factor * part[:ROWS].astype(jnp.float32)
    return mean, peak + jnp.log(total)


def level_of(part):
    return jnp.sum(part[ROWS:, :ROWS].astype(jnp.float32), axis=0, keepdims=True)


def premerge_kernel(*refs):
    parts, out_ref = refs[:-1], refs[-1]
    mean, level = weigh(parts, [level_of(part) for part in parts])
    out_ref[:ROWS] = mean
    out_ref[ROWS:, :ROWS] = jnp.broadcast_to(level, (8, ROWS))
    out_ref[ROWS:, ROWS:] = jnp.zeros((8, KL - ROWS), jnp.float32)


def premerge(parts):
    return pl.pallas_call(
        premerge_kernel,
        out_shape=jax.ShapeDtypeStruct((ROWS + 8, KL), jnp.float32),
        compiler_params=pltpu.CompilerParams(vmem_limit_bytes=8 * MIB),
        name="premerge",
    )(*parts)


def merge_kernel(state, *refs):
    parts, out_ref = refs[:-1], refs[-1]
    levels = [state[ROWS : ROWS + 1, :ROWS]] + [level_of(part) for part in parts]
    mean, _ = weigh((state,) + parts, levels)
    out_ref[...] = mean.astype(jnp.bfloat16).reshape(RDEV, HEADS, KL)


def merge(parts):
    return pl.pallas_call(
        merge_kernel,
        out_shape=jax.ShapeDtypeStruct((RDEV, HEADS, KL), jnp.bfloat16),
        compiler_params=pltpu.CompilerParams(vmem_limit_bytes=8 * MIB),
        name="merge",
    )(*parts)


def per_device(queries, cache, selected):
    y, zhi, zlo, x = (lax.axis_index(name) for name in ("y", "zhi", "zlo", "x"))
    core = lax.axis_index("head")
    me = ((y * NK + zhi) * 2 + zlo) * NX + x

    extended = jnp.pad(selected, ((0, 8), (0, 0)), constant_values=-1)
    which = lax.broadcasted_iota(jnp.int32, extended.shape, 0)
    local = jnp.where(extended // BLK_DEV == me, extended % BLK_DEV, -1)
    local = jnp.where(which == 2 * SEQ, me, jnp.where(which == 2 * SEQ + 1, core, local))
    meta = jnp.max(local, axis=1)

    def route(steps, back, cross):
        pairs = [
            (zz * 2 + c, (zz + steps[c]) % NK * 2 + (c ^ cross)) for zz in range(NK) for c in range(2)
        ]
        return [pair[::-1] for pair in pairs] if back else pairs

    def move(value, *way):
        return lax.ppermute(value, ("zhi", "head"), route(*way))

    padded = jnp.pad(queries.reshape(ROWS, FEAT), ((0, 0), (0, KR)))
    asked = [move(padded, steps, True, cross) for steps in STEPS for cross in range(2)]
    picked = pick_blocks(0, meta, cache)
    picked = pick_blocks(1, meta, cache, picked, asked)
    picked = picked.reshape(GROUP, COUNT * TILES * PAIRS, 128)
    blocks = lax.all_to_all(picked, ("y", "zlo", "x"), split_axis=0, concat_axis=0, tiled=True)
    blocks = blocks.reshape(GROUP, COUNT, TILES, PAIRS, 128)

    parts, earlier = [], meta
    for i, steps in enumerate(STEPS):
        near, far = attend(i, meta, blocks, asked[2 * i], asked[2 * i + 1], selected.T, earlier)
        parts.append([move(near, steps, False, 0), move(far, steps, False, 1)])
        earlier = near
    result = merge([premerge(parts[0])] + parts[1]).reshape(RDEV, HEADS * KL)
    return lax.all_gather(result, "head", axis=1, tiled=True)


def solution(mesh):
    grid = Mesh(mesh.devices.reshape(NY, NK, 2, NX, 2), ("y", "zhi", "zlo", "x", "head"))
    seq = ("y", "zhi", "zlo", "x")
    placed = (P(seq, "head"), P(None, seq, None), P())
    return jax.shard_map(
        per_device, mesh=grid, in_specs=placed, out_specs=P(seq, None), check_vma=False
    )
```

time: 145 us -> 118 us (0.81); the launches traced: 143 us -> 118 us
  blocking collectives: 2.03 us -> 63.6 us
  waiting for transfers between devices: 57.3 us -> 10.7 us
  between operations: 13.6 us -> 0.13 us
  Pallas kernels: 21.9 us -> 10 us
  starting transfers between devices: 35.8 us -> 26.8 us
  local copies, waits for them, and re-layouts: 9.98 us -> 5.64 us
    all_to_all x0 -> x1, blocking collectives: none -> 60.4 us  [per_device(): lax.all_to_all(picked, ('y', 'zlo', 'x'), split_axis=0, concat_axis=0, ti...]
    all_to_all x2 -> x0, waiting for transfers between devices: 39.9 us -> none  [per_device(): lax.all_to_all(picked, ('y', 'x'), split_axis=0, concat_axis=0, tiled=True)]
    all_to_all x2 -> x0, starting transfers between devices: 12 us -> none  [per_device(): lax.all_to_all(picked, ('y', 'x'), split_axis=0, concat_axis=0, tiled=True)]
    pallas_call x4 -> x5, Pallas kernels: 21.6 us -> 9.85 us  [the longest x2 5.63 us: attend(): pl.pallas_call(functools.partial(attend_kernel, i), out_shape=[part, part...]
    ppermute x8, waiting for transfers between devices: 17.3 us -> 10.7 us  [move(): return lax.ppermute(value, ('zhi', 'head'), route(*way))]
    ppermute x8, starting transfers between devices: 23.7 us -> 26.8 us  [move(): return lax.ppermute(value, ('zhi', 'head'), route(*way))]
    unnamed x15 -> x6, local copies, waits for them, and re-layouts: 7.25 us -> 4.52 us
  transfers between devices with their start and end apart: 11 -> 8, of which waited for: 6 -> 4; matrix products, arithmetic and copies ran while one was open for 2% -> 1% of each run, Pallas kernels for 15% -> 4%
where the time goes in v2:
time: 118 us
  blocking collectives  63.6 us (54%)
  starting transfers between devices  26.8 us (23%)
  waiting for transfers between devices  10.7 us (9%)
  Pallas kernels  10 us (8%)
  local copies, waits for them, and re-layouts  5.64 us (5%)
    all_to_all x1, blocking collectives, per_device(): lax.all_to_all(picked, ('y', 'zlo', 'x'), split_axis=0, concat_axis=0, ti...  60.4 us
    ppermute x8, starting transfers between devices, move(): return lax.ppermute(value, ('zhi', 'head'), route(*way))  26.8 us
    ppermute x8, waiting for transfers between devices, move(): return lax.ppermute(value, ('zhi', 'head'), route(*way))  10.7 us
    pallas_call x2, Pallas kernels, attend(): pl.pallas_call(functools.partial(attend_kernel, i), out_shape=[part, part...  5.63 us
    unnamed x6, local copies, waits for them, and re-layouts  4.52 us
    pallas_call x2, Pallas kernels, pick_blocks(): pl.pallas_call(functools.partial(pick_kernel, i), out_shape=jax.ShapeDtyp...  4.09 us
    all_gather x1, blocking collectives, per_device(): return lax.all_gather(result, 'head', axis=1, tiled=True)  3.25 us
  transfers between devices with their start and end apart: 8, of which 4 were waited for; matrix products, arithmetic and copies ran while one was open for 1% of the time, Pallas kernels for 4%

profile of v2, /device:TPU:1, one launch (start us, length us, event | category | flops | bytes accessed | tf_op | source)
XLA Modules:
  0.0 117.7 jit_solution(11618026123461349998)
XLA Ops:
  0.0 1.1 reshape.12
  1.1 3.3 %collective-permute-start.3 = (bf16[128,640]{1,0:T(8,128)(2,1)S(1)}, bf16[128,640]{1,0:T(8,128)(2,1)S(1)}, u32[]{:S(2)}, u32[]{:S(2)}) collective-permute-start(bf16[128,640]{1,0:T(8,128)(2,1)S(1)} %pad.9), channel_id=1, source_target_pairs={{1,0},{48,1},{17,16},{0,17},{33,32},{16,33},{49,48},{32,49},{3,2},... | collective-permute-start | bytes 491528 | tf_op jit(solution)/shard_map/ppermute | solution.py:242
  4.5 3.2 %collective-permute-start.2 = (bf16[128,640]{1,0:T(8,128)(2,1)S(1)}, bf16[128,640]{1,0:T(8,128)(2,1)S(1)}, u32[]{:S(2)}, u32[]{:S(2)}) collective-permute-start(bf16[128,640]{1,0:T(8,128)(2,1)S(1)} %pad.9), channel_id=1, source_target_pairs={{0,0},{49,1},{16,16},{1,17},{32,32},{17,33},{48,48},{33,49},{2,2},... | collective-permute-start | bytes 491528 | tf_op jit(solution)/shard_map/ppermute | solution.py:242
  7.6 3.6 %collective-permute-start.1 = (bf16[128,640]{1,0:T(8,128)(2,1)S(1)}, bf16[128,640]{1,0:T(8,128)(2,1)S(1)}, u32[]{:S(2)}, u32[]{:S(2)}) collective-permute-start(bf16[128,640]{1,0:T(8,128)(2,1)S(1)} %pad.9), channel_id=1, source_target_pairs={{33,0},{16,1},{49,16},{32,17},{1,32},{48,33},{17,48},{0,49},{35,2}... | collective-permute-start | bytes 491528 | tf_op jit(solution)/shard_map/ppermute | solution.py:242
  11.2 2.4 %collective-permute-start = (bf16[128,640]{1,0:T(8,128)(2,1)S(1)}, bf16[128,640]{1,0:T(8,128)(2,1)S(1)}, u32[]{:S(2)}, u32[]{:S(2)}) collective-permute-start(bf16[128,640]{1,0:T(8,128)(2,1)S(1)} %pad.9), channel_id=1, source_target_pairs={{32,0},{17,1},{48,16},{33,17},{0,32},{49,33},{16,48},{1,49},{34,2}... | collective-permute-start | bytes 491528 | tf_op jit(solution)/shard_map/ppermute | solution.py:242
  13.6 0.8 fusion.5.meta_ref._
  14.4 0.0 copy-start
  14.4 3.7 %copy-done = bf16[16,8,36864]{2,1,0:T(8,128)(2,1)S(1)} copy-done((bf16[16,8,36864]{2,1,0:T(8,128)(2,1)S(1)}, bf16[16,8,36864]{2,1,0:T(8,128)(2,1)}, u32[]{:S(2)}) %copy-start) | copy-done | bytes 9437208
  18.0 2.0 %pick_blocks.2.refs_0_ = bf16[4,8,2,9,32,128]{5,4,3,2,1,0:T(8,128)(2,1)S(1)} custom-call(s32[264]{0:T(512)S(1)} %fusion.5.meta_ref._, bf16[16,8,36864]{2,1,0:T(8,128)(2,1)S(1)} %copy-done), custom_call_target="tpu_custom_call" | custom-call | tf_op jit(solution)/shard_map/pick_blocks/pallas_call | solution.py:74
  20.1 0.0 collective-permute-done.3.refs_4_.far_ref
  20.1 0.0 collective-permute-done.2.refs_3_.near_ref
  20.1 0.0 collective-permute-done.1.refs_2_.far_ref
  20.1 5.7 %collective-permute-done.refs_1_.near_ref = bf16[128,640]{1,0:T(8,128)(2,1)S(1)} collective-permute-done((bf16[128,640]{1,0:T(8,128)(2,1)S(1)}, bf16[128,640]{1,0:T(8,128)(2,1)S(1)}, u32[]{:S(2)}, u32[]{:S(2)}) %collective-permute-start) | collective-permute-done | bytes 163872 | tf_op jit(solution)/shard_map/ppermute | solution.py:242
  25.9 2.0 %pick_blocks.3 = bf16[4,8,2,9,32,128]{5,4,3,2,1,0:T(8,128)(2,1)S(1)} custom-call(s32[264]{0:T(512)S(1)} %fusion.5.meta_ref._, bf16[16,8,36864]{2,1,0:T(8,128)(2,1)S(1)} %copy-done, bf16[4,8,2,9,32,128]{5,4,3,2,1,0:T(8,128)(2,1)S(1)} %pick_blocks.2.refs_0_, ...), custom_call_target="tpu_custom_call", output_to_operand_aliasing={{}: (2, {})} | custom-call | tf_op jit(solution)/shard_map/pick_blocks/pallas_call | solution.py:74
  27.9 0.0 copy-start.1
  27.9 60.4 %all_to_all.5 = bf16[32,576,128]{2,1,0:T(8,128)(2,1)S(1)} all-to-all(bf16[32,576,128]{2,1,0:T(8,128)(2,1)S(1)} %bitcast.7), channel_id=1, replica_groups=mesh['y'=4,'zhi'=4,'zlo'=2,'x'=4,'head'=2] {'y','zlo','x'}, dimensions={0} | all-to-all | bytes 9437184 | tf_op jit(solution)/shard_map/all_to_all | solution.py:249
  88.3 0.0 copy-done.1
  88.3 2.8 %attend.2 = (bf16[144,512]{1,0:T(8,128)(2,1)S(1)}, bf16[144,512]{1,0:T(8,128)(2,1)S(1)}) custom-call(s32[264]{0:T(512)S(1)} %fusion.5.meta_ref._, bf16[32,2,9,32,128]{4,3,2,1,0:T(8,128)(2,1)S(1)} %bitcast.5, bf16[128,640]{1,0:T(8,128)(2,1)S(1)} %collective-permute-done.refs_1_.near_ref, bf16[128,640]{1,0:T(8,128)(2,1)S(1)} %collective-permute-done.1.refs_2_.far_ref, ...), custom_call_target="tpu_custom_call" | custom-call | flops 1 | bytes 1 | tf_op jit(solution)/shard_map/attend/pallas_call | solution.py:153
  91.1 6.4 %collective-permute-start.5 = (bf16[144,512]{1,0:T(8,128)(2,1)S(1)}, bf16[144,512]{1,0:T(8,128)(2,1)S(1)}, u32[]{:S(2)}, u32[]{:S(2)}) collective-permute-start(bf16[144,512]{1,0:T(8,128)(2,1)S(1)} %get-tuple-element.10), channel_id=1, source_target_pairs={{0,33},{1,16},{16,49},{17,32},{32,1},{33,48},{48,17},{49,0},{2,35}... | collective-permute-start | bytes 442376 | tf_op jit(solution)/shard_map/ppermute | solution.py:242
  97.5 2.4 %collective-permute-start.4 = (bf16[144,512]{1,0:T(8,128)(2,1)S(1)}, bf16[144,512]{1,0:T(8,128)(2,1)S(1)}, u32[]{:S(2)}, u32[]{:S(2)}) collective-permute-start(bf16[144,512]{1,0:T(8,128)(2,1)S(1)} %get-tuple-element.9._), channel_id=1, source_target_pairs={{0,32},{1,17},{16,48},{17,33},{32,0},{33,49},{48,16},{49,1},{2,34}... | collective-permute-start | bytes 442376 | tf_op jit(solution)/shard_map/ppermute | solution.py:242
  99.9 2.8 %attend.3 = (bf16[144,512]{1,0:T(8,128)(2,1)S(1)}, bf16[144,512]{1,0:T(8,128)(2,1)S(1)}) custom-call(s32[264]{0:T(512)S(1)} %fusion.5.meta_ref._, bf16[32,2,9,32,128]{4,3,2,1,0:T(8,128)(2,1)S(1)} %bitcast.6, bf16[128,640]{1,0:T(8,128)(2,1)S(1)} %collective-permute-done.2.refs_3_.near_ref, bf16[128,640]{1,0:T(8,128)(2,1)S(1)} %collective-permute-done.3.refs_4_.far_ref, ...), custom_call_target="tpu_custom_call" | custom-call | flops 1 | bytes 1 | tf_op jit(solution)/shard_map/attend/pallas_call | solution.py:153
  102.7 3.1 %collective-permute-start.6 = (bf16[144,512]{1,0:T(8,128)(2,1)S(1)}, bf16[144,512]{1,0:T(8,128)(2,1)S(1)}, u32[]{:S(2)}, u32[]{:S(2)}) collective-permute-start(bf16[144,512]{1,0:T(8,128)(2,1)S(1)} %get-tuple-element.11), channel_id=1, source_target_pairs={{0,0},{1,49},{16,16},{17,1},{32,32},{33,17},{48,48},{49,33},{2,2},... | collective-permute-start | bytes 442376 | tf_op jit(solution)/shard_map/ppermute | solution.py:242
  105.8 2.5 %collective-permute-start.7 = (bf16[144,512]{1,0:T(8,128)(2,1)S(1)}, bf16[144,512]{1,0:T(8,128)(2,1)S(1)}, u32[]{:S(2)}, u32[]{:S(2)}) collective-permute-start(bf16[144,512]{1,0:T(8,128)(2,1)S(1)} %get-tuple-element.12), channel_id=1, source_target_pairs={{0,1},{1,48},{16,17},{17,0},{32,33},{33,16},{48,49},{49,32},{2,3},... | collective-permute-start | bytes 442376 | tf_op jit(solution)/shard_map/ppermute | solution.py:242
  108.3 0.0 collective-permute-done.5.refs_1_
  108.3 3.2 %collective-permute-done.4.refs_0_ = bf16[144,512]{1,0:T(8,128)(2,1)S(1)} collective-permute-done((bf16[144,512]{1,0:T(8,128)(2,1)S(1)}, bf16[144,512]{1,0:T(8,128)(2,1)S(1)}, u32[]{:S(2)}, u32[]{:S(2)}) %collective-permute-start.4) | collective-permute-done | bytes 147488 | tf_op jit(solution)/shard_map/ppermute | solution.py:242
  111.5 0.1 premerge.1.state
  111.6 1.1 collective-permute-done.6.refs_0_
  112.7 0.6 collective-permute-done.7.refs_1_
  113.4 0.2 merge.1
  113.6 0.1 copy.5
  113.7 3.3 %all_gather.3 = bf16[2,65536]{1,0:T(2,128)(2,1)S(1)} all-gather(bf16[2,32768]{1,0:T(2,128)(2,1)S(1)} %bitcast.11), channel_id=1, replica_groups=mesh['y'=4,'zhi'=4,'zlo'=2,'x'=4,'head'=2] {'head'}, dimensions={1}, use_global_device_ids=true | all-gather | bytes 393216 | tf_op jit(solution)/shard_map/all_gather | solution.py:258
  117.0 0.7 copy.8
  (2 shorter events, 0.0 us)
Async XLA Ops:
  1.1 19.0 %collective-permute-start.3 = (bf16[128,640]{1,0:T(8,128)(2,1)S(1)}, bf16[128,640]{1,0:T(8,128)(2,1)S(1)}, u32[]{:S(2)}, u32[]{:S(2)}) collective-permute-start(bf16[128,640]{1,0:T(8,128)(2,1)S(1)} %pad.9), channel_id=1, source_target_pairs={{1,0},{48,1},{17,16},{0,17},{33,32},{16,33},{49,48},{32,49},{3,2},... | collective-permute-start | bytes 491528 | tf_op jit(solution)/shard_map/ppermute | solution.py:242
  4.5 15.7 %collective-permute-start.2 = (bf16[128,640]{1,0:T(8,128)(2,1)S(1)}, bf16[128,640]{1,0:T(8,128)(2,1)S(1)}, u32[]{:S(2)}, u32[]{:S(2)}) collective-permute-start(bf16[128,640]{1,0:T(8,128)(2,1)S(1)} %pad.9), channel_id=1, source_target_pairs={{0,0},{49,1},{16,16},{1,17},{32,32},{17,33},{48,48},{33,49},{2,2},... | collective-permute-start | bytes 491528 | tf_op jit(solution)/shard_map/ppermute | solution.py:242
  7.6 12.5 %collective-permute-start.1 = (bf16[128,640]{1,0:T(8,128)(2,1)S(1)}, bf16[128,640]{1,0:T(8,128)(2,1)S(1)}, u32[]{:S(2)}, u32[]{:S(2)}) collective-permute-start(bf16[128,640]{1,0:T(8,128)(2,1)S(1)} %pad.9), channel_id=1, source_target_pairs={{33,0},{16,1},{49,16},{32,17},{1,32},{48,33},{17,48},{0,49},{35,2}... | collective-permute-start | bytes 491528 | tf_op jit(solution)/shard_map/ppermute | solution.py:242
  11.2 14.7 %collective-permute-start = (bf16[128,640]{1,0:T(8,128)(2,1)S(1)}, bf16[128,640]{1,0:T(8,128)(2,1)S(1)}, u32[]{:S(2)}, u32[]{:S(2)}) collective-permute-start(bf16[128,640]{1,0:T(8,128)(2,1)S(1)} %pad.9), channel_id=1, source_target_pairs={{32,0},{17,1},{48,16},{33,17},{0,32},{49,33},{16,48},{1,49},{34,2}... | collective-permute-start | bytes 491528 | tf_op jit(solution)/shard_map/ppermute | solution.py:242
  14.4 3.7 %copy-start = (bf16[16,8,36864]{2,1,0:T(8,128)(2,1)S(1)}, bf16[16,8,36864]{2,1,0:T(8,128)(2,1)}, u32[]{:S(2)}) copy-start(bf16[16,8,36864]{2,1,0:T(8,128)(2,1)} %cache_ref.3) | copy-start | bytes 28311556
  27.9 60.4 %copy-start.1 = (s32[256,32]{0,1:T(8,128)S(1)}, s32[256,32]{0,1:T(8,128)}, u32[]{:S(2)}) copy-start(s32[256,32]{0,1:T(8,128)} %param.5) | copy-start | bytes 98308
  91.1 17.2 %collective-permute-start.5 = (bf16[144,512]{1,0:T(8,128)(2,1)S(1)}, bf16[144,512]{1,0:T(8,128)(2,1)S(1)}, u32[]{:S(2)}, u32[]{:S(2)}) collective-permute-start(bf16[144,512]{1,0:T(8,128)(2,1)S(1)} %get-tuple-element.10), channel_id=1, source_target_pairs={{0,33},{1,16},{16,49},{17,32},{32,1},{33,48},{48,17},{49,0},{2,35}... | collective-permute-start | bytes 442376 | tf_op jit(solution)/shard_map/ppermute | solution.py:242
  97.5 14.0 %collective-permute-start.4 = (bf16[144,512]{1,0:T(8,128)(2,1)S(1)}, bf16[144,512]{1,0:T(8,128)(2,1)S(1)}, u32[]{:S(2)}, u32[]{:S(2)}) collective-permute-start(bf16[144,512]{1,0:T(8,128)(2,1)S(1)} %get-tuple-element.9._), channel_id=1, source_target_pairs={{0,32},{1,17},{16,48},{17,33},{32,0},{33,49},{48,16},{49,1},{2,34}... | collective-permute-start | bytes 442376 | tf_op jit(solution)/shard_map/ppermute | solution.py:242
  102.7 10.0 %collective-permute-start.6 = (bf16[144,512]{1,0:T(8,128)(2,1)S(1)}, bf16[144,512]{1,0:T(8,128)(2,1)S(1)}, u32[]{:S(2)}, u32[]{:S(2)}) collective-permute-start(bf16[144,512]{1,0:T(8,128)(2,1)S(1)} %get-tuple-element.11), channel_id=1, source_target_pairs={{0,0},{1,49},{16,16},{17,1},{32,32},{33,17},{48,48},{49,33},{2,2},... | collective-permute-start | bytes 442376 | tf_op jit(solution)/shard_map/ppermute | solution.py:242
  105.8 7.6 %collective-permute-start.7 = (bf16[144,512]{1,0:T(8,128)(2,1)S(1)}, bf16[144,512]{1,0:T(8,128)(2,1)S(1)}, u32[]{:S(2)}, u32[]{:S(2)}) collective-permute-start(bf16[144,512]{1,0:T(8,128)(2,1)S(1)} %get-tuple-element.12), channel_id=1, source_target_pairs={{0,1},{1,48},{16,17},{17,0},{32,33},{33,16},{48,49},{49,32},{2,3},... | collective-permute-start | bytes 442376 | tf_op jit(solution)/shard_map/ppermute | solution.py:242

commit v3 on v2

--- a/solution.py
+++ b/solution.py
@@ -33,19 +33,29 @@
 
 score_scale = 192.0 ** (-0.5)
 
-STEPS = ((2, 1), (0, 3))
-COUNT = len(STEPS)
-
-
-def owner_of(i, meta):
-    step = jnp.where(meta[2 * SEQ + 1] == 0, STEPS[i][0], STEPS[i][1])
-    pair = meta[2 * SEQ] // (2 * NX) % NK
-    return (pair + step) % NK * (2 * NX), meta[2 * SEQ] % (2 * NX)
-
-
-def pick_kernel(i, meta_ref, cache_ref, *refs):
-    out_ref = refs[-1]
-    base = pl.program_id(0) * (NK * 2 * NX) + owner_of(i, meta_ref)[0]
+COUNT = 2
+
+
+def owner_place(zhi, zlo, core, i):
+    if core == 0:
+        return ((zhi + 2) % NK, 1 - zlo) if i == 0 else (zhi, zlo)
+    return (zhi + 3 - 2 * zlo) % NK, zlo if i == 0 else 1 - zlo
+
+
+def own_place(meta):
+    here = meta[2 * SEQ]
+    return here // (2 * NX) % NK, here // NX % 2, meta[2 * SEQ + 1]
+
+
+def pick_pair(n, meta):
+    zhi, _, core = own_place(meta)
+    return (zhi + jnp.where(core == 0, 2 - 2 * n, 3 - 2 * n)) % NK
+
+
+def pick_kernel(meta_ref, cache_ref, out_ref):
+    n = pl.program_id(1)
+    core = meta_ref[2 * SEQ + 1]
+    base = (pl.program_id(0) * NK + pick_pair(n, meta_ref)) * (2 * NX)
     row = lax.broadcasted_iota(jnp.int32, (2 * NX * UNIT, BLK_DEV * UNIT), 0)
     col = lax.broadcasted_iota(jnp.int32, (2 * NX * UNIT, BLK_DEV * UNIT), 1)
     slot, token, held = row >> 4, (col >> 3) == (row & (UNIT - 1)), col & (BLK_DEV - 1)
@@ -61,37 +71,62 @@
         ]
         stacked = jnp.concatenate(pieces, axis=0).astype(jnp.bfloat16)
         picked = jnp.dot(onehot, stacked, preferred_element_type=jnp.float32)
-        picked = picked.astype(jnp.bfloat16).reshape(2 * NX, UNIT, PAIR_WIDTH)
-        for t in range(TILES):
-            out_ref[0, :, 0, t, half * UNIT : (half + 1) * UNIT] = picked[
-                :, :, t * 128 : (t + 1) * 128
-            ]
-
-
-def pick_blocks(i, meta, cache, into=None, earlier=()):
-    anywhere = pl.BlockSpec(memory_space=pl.ANY)
-    more = () if into is None else (into,) + tuple(earlier)
-    return pl.pallas_call(
-        functools.partial(pick_kernel, i),
+        picked = picked.astype(jnp.bfloat16).reshape(2, NX, UNIT, PAIR_WIDTH)
+        for zlo in range(2):
+            chip = jnp.where(core == 0, jnp.where(n == 0, 1 - zlo, zlo), n)
+            index = jnp.where(core == 0, n, jnp.where(n == zlo, 0, 1))
+            for t in range(TILES):
+                out_ref[0, pl.ds(chip * NX, NX), index, t, half * UNIT : (half + 1) * UNIT] = picked[
+                    zlo, :, :, t * 128 : (t + 1) * 128
+                ]
+
+
+def pick_blocks(meta, cache):
+    return pl.pallas_call(
+        pick_kernel,
         out_shape=jax.ShapeDtypeStruct((NY, 2 * NX, COUNT, TILES, PAIRS, 128), jnp.bfloat16),
         grid_spec=pltpu.PrefetchScalarGridSpec(
             num_scalar_prefetch=1,
-            grid=(NY,),
+            grid=(NY, COUNT),
             in_specs=[
                 pl.BlockSpec(
                     (1, BLK_DEV, BLOCK * FEAT),
-                    lambda y, meta: (y * NK + owner_of(i, meta)[0] // (2 * NX), 0, 0),
+                    lambda y, n, meta: (y * NK + pick_pair(n, meta), 0, 0),
                 )
-            ]
-            + [anywhere] * len(more),
+            ],
             out_specs=pl.BlockSpec(
-                (1, 2 * NX, 1, TILES, PAIRS, 128), lambda y, meta: (y, 0, i, 0, 0, 0)
+                (1, 2 * NX, COUNT, TILES, PAIRS, 128), lambda y, n, meta: (y, 0, 0, 0, 0, 0)
             ),
         ),
-        input_output_aliases={} if into is None else {2: 0},
         compiler_params=pltpu.CompilerParams(vmem_limit_bytes=12 * MIB),
         name="pick_blocks",
-    )(meta, cache, *more)
+    )(meta, cache)
+
+
+def tie_kernel(*refs):
+    pass
+
+
+def tie(value, *earlier):
+    anywhere = pl.BlockSpec(memory_space=pl.ANY)
+    return pl.pallas_call(
+        tie_kernel,
+        out_shape=jax.ShapeDtypeStruct(value.shape, value.dtype),
+        in_specs=[anywhere] * (1 + len(earlier)),
+        out_specs=anywhere,
+        input_output_aliases={0: 0},
+        compiler_params=pltpu.CompilerParams(vmem_limit_bytes=MIB),
+        name="tie",
+    )(value, *earlier)
+
+
+def spread_queries(packed):
+    lane = lax.broadcasted_iota(jnp.int32, (RDEV * HEADS // 2, WIDE), 1)
+    even = jnp.where(lane < FEAT, packed[:, :WIDE].astype(jnp.float32), 0.0)
+    odd = jnp.where(lane >= KR, packed[:, KL:].astype(jnp.float32), 0.0)
+    low = [even, pltpu.roll(odd, FEAT, 1)]
+    high = [pltpu.roll(even, KR, 1), odd]
+    return low, high
 
 
 def attend_kernel(i, meta_ref, blocks_ref, near_ref, far_ref, selected_ref, _, near_out, far_out):
@@ -99,21 +134,29 @@
     pairs = jnp.concatenate(
         [blocks_ref[:, 0, t].reshape(width, 128) for t in range(TILES)], axis=1
     )
-    query = jnp.concatenate([near_ref[...], far_ref[...]], axis=0)
-    shifted = pltpu.roll(query.astype(jnp.float32), KR, 1).astype(jnp.bfloat16)
-    pair, within = owner_of(i, meta_ref)
+    low, high = [], []
+    for ref in (near_ref, far_ref):
+        parts = spread_queries(ref[...])
+        low += parts[0]
+        high += parts[1]
+    query = jnp.concatenate(low, axis=0).astype(jnp.bfloat16)
+    shifted = jnp.concatenate(high, axis=0).astype(jnp.bfloat16)
+    zhi, zlo, core = own_place(meta_ref)
     here = meta_ref[2 * SEQ]
-    owner = here // (NK * 2 * NX) * (NK * 2 * NX) + pair + within
+    first, second = (owner_place(zhi, zlo, c, i) for c in range(2))
+    pair = jnp.where(core == 0, first[0], second[0])
+    chip = jnp.where(core == 0, first[1], second[1])
+    owner = here // (NK * 2 * NX) * (NK * 2 * NX) + pair * (2 * NX) + chip * NX + here % NX
     slot = lax.broadcasted_iota(jnp.int32, (1, width), 1) >> 5
-    holder = (slot >> 3) * (NK * 2 * NX) + (here // (2 * NX) % NK * (2 * NX) + (slot & 7))
+    holder = (slot >> 3) * (NK * 2 * NX) + (zhi * (2 * NX) + (slot & 7))
     places = selected_ref[...] >> 3
     lane = lax.broadcasted_iota(jnp.int32, places.shape, 1)
     rows = []
     for j in range(RDEV):
         mine = jnp.sum(jnp.where(lane == RDEV * owner + j, places, 0), axis=1, keepdims=True)
         read = jnp.max(jnp.where(mine == holder, 1.0, 0.0), axis=0, keepdims=True)
-        rows.append(jnp.broadcast_to(read, (HEADS, width)))
-    valid = jnp.concatenate(rows * 2, axis=0) > 0.5
+        rows.append(jnp.broadcast_to(read, (HEADS // 2, width)))
+    valid = jnp.concatenate(rows * 4, axis=0) > 0.5
     dims = (((1,), (1,)), ((), ()))
     odd_keys = pairs[:, KL:]
     even = lax.dot_general(query, pairs[:, :WIDE], dims, preferred_element_type=jnp.float32)
@@ -149,7 +192,7 @@
 
 def attend(i, meta, blocks, near, far, selected, earlier):
     part = jax.ShapeDtypeStruct((ROWS + TAIL, KL), jnp.bfloat16)
-    query = pl.BlockSpec((ROWS, WIDE), lambda n, meta: (0, 0))
+    query = pl.BlockSpec((ROWS // 2, PAIR_WIDTH), lambda n, meta: (0, 0))
     return pl.pallas_call(
         functools.partial(attend_kernel, i),
         out_shape=[part, part],
@@ -209,13 +252,15 @@
     parts, out_ref = refs[:-1], refs[-1]
     levels = [state[ROWS : ROWS + 1, :ROWS]] + [level_of(part) for part in parts]
     mean, _ = weigh((state,) + parts, levels)
-    out_ref[...] = mean.astype(jnp.bfloat16).reshape(RDEV, HEADS, KL)
+    mean = mean.astype(jnp.bfloat16).reshape(2, RDEV, HEADS // 2, KL)
+    for odd in range(2):
+        out_ref[:, :, odd * KL : (odd + 1) * KL] = mean[odd]
 
 
 def merge(parts):
     return pl.pallas_call(
         merge_kernel,
-        out_shape=jax.ShapeDtypeStruct((RDEV, HEADS, KL), jnp.bfloat16),
+        out_shape=jax.ShapeDtypeStruct((RDEV, HEADS // 2, 2 * KL), jnp.bfloat16),
         compiler_params=pltpu.CompilerParams(vmem_limit_bytes=8 * MIB),
         name="merge",
     )(*parts)
@@ -232,27 +277,29 @@
     local = jnp.where(which == 2 * SEQ, me, jnp.where(which == 2 * SEQ + 1, core, local))
     meta = jnp.max(local, axis=1)
 
-    def route(steps, back, cross):
-        pairs = [
-            (zz * 2 + c, (zz + steps[c]) % NK * 2 + (c ^ cross)) for zz in range(NK) for c in range(2)
-        ]
-        return [pair[::-1] for pair in pairs] if back else pairs
-
-    def move(value, *way):
-        return lax.ppermute(value, ("zhi", "head"), route(*way))
-
-    padded = jnp.pad(queries.reshape(ROWS, FEAT), ((0, 0), (0, KR)))
-    asked = [move(padded, steps, True, cross) for steps in STEPS for cross in range(2)]
-    picked = pick_blocks(0, meta, cache)
-    picked = pick_blocks(1, meta, cache, picked, asked)
+    def move(value, i, back, cross):
+        pairs = []
+        for zz in range(NZ):
+            for c in range(2):
+                pair, chip = owner_place(zz // 2, zz % 2, c, i)
+                pairs.append((zz * 2 + c, (pair * 2 + chip) * 2 + (c ^ cross)))
+        pairs = [pair[::-1] for pair in pairs] if back else pairs
+        return lax.ppermute(value, ("zhi", "zlo", "head"), pairs)
+
+    packed = queries.reshape(ROWS // 2, PAIR_WIDTH)
+    asked = {}
+    for i in (1, 0):
+        for cross in (1, 0):
+            asked[i, cross] = move(packed, i, True, cross)
+    picked = tie(pick_blocks(meta, cache), *asked.values())
     picked = picked.reshape(GROUP, COUNT * TILES * PAIRS, 128)
     blocks = lax.all_to_all(picked, ("y", "zlo", "x"), split_axis=0, concat_axis=0, tiled=True)
     blocks = blocks.reshape(GROUP, COUNT, TILES, PAIRS, 128)
 
     parts, earlier = [], meta
-    for i, steps in enumerate(STEPS):
-        near, far = attend(i, meta, blocks, asked[2 * i], asked[2 * i + 1], selected.T, earlier)
-        parts.append([move(near, steps, False, 0), move(far, steps, False, 1)])
+    for i in range(COUNT):
+        near, far = attend(i, meta, blocks, asked[i, 0], asked[i, 1], selected.T, earlier)
+        parts.append([move(near, i, False, 0), move(far, i, False, 1)])
         earlier = near
     result = merge([premerge(parts[0])] + parts[1]).reshape(RDEV, HEADS * KL)
     return lax.all_gather(result, "head", axis=1, tiled=True)

time: 118 us -> 110 us (0.932)
  waiting for transfers between devices: 10.7 us -> 5.16 us
  starting transfers between devices: 26.8 us -> 22.6 us
  blocking collectives: 63.6 us -> 65.8 us
    ppermute x8, waiting for transfers between devices: 10.7 us -> 5.16 us  [move(): return lax.ppermute(value, ('zhi', 'zlo', 'head'), pairs)]
    ppermute x8, starting transfers between devices: 26.8 us -> 22.6 us  [move(): return lax.ppermute(value, ('zhi', 'zlo', 'head'), pairs)]
    all_to_all x1, blocking collectives: 60.4 us -> 61.9 us  [per_device(): lax.all_to_all(picked, ('y', 'zlo', 'x'), split_axis=0, concat_axis=0, ti...]
  transfers between devices with their start and end apart: 8 -> 8, of which waited for: 4 -> 2; matrix products, arithmetic and copies ran while one was open for 1% -> 1% of each run, Pallas kernels for 4% -> 6%
where the time goes in v3:
time: 110 us; the launch traced here: 109 us
  blocking collectives  65.8 us (60%)
  starting transfers between devices  22.6 us (21%)
  Pallas kernels  9.23 us (8%)
  local copies, waits for them, and re-layouts  5.52 us (5%)
  waiting for transfers between devices  5.16 us (5%)
    all_to_all x1, blocking collectives, per_device(): lax.all_to_all(picked, ('y', 'zlo', 'x'), split_axis=0, concat_axis=0, ti...  61.9 us
    ppermute x8, starting transfers between devices, move(): return lax.ppermute(value, ('zhi', 'zlo', 'head'), pairs)  22.6 us
    pallas_call x2, Pallas kernels, attend(): pl.pallas_call(functools.partial(attend_kernel, i), out_shape=[part, part...  5.65 us
    ppermute x8, waiting for transfers between devices, move(): return lax.ppermute(value, ('zhi', 'zlo', 'head'), pairs)  5.16 us
    unnamed x6, local copies, waits for them, and re-layouts  4.52 us
    all_gather x1, blocking collectives, per_device(): return lax.all_gather(result, 'head', axis=1, tiled=True)  3.9 us
    pallas_call x1, Pallas kernels, pick_blocks(): pl.pallas_call(pick_kernel, out_shape=jax.ShapeDtypeStruct((NY, 2 * NX, C...  3.28 us
  transfers between devices with their start and end apart: 8, of which 2 were waited for; matrix products, arithmetic and copies ran while one was open for 1% of the time, Pallas kernels for 6%

profile of v3, /device:TPU:1, one launch (start us, length us, event | category | flops | bytes accessed | tf_op | source)
XLA Modules:
  0.0 109.4 jit_solution(879748683375165293)
XLA Ops:
  0.0 1.0 reshape.12
  1.0 3.9 %collective-permute-start.3 = (bf16[64,1152]{1,0:T(8,128)(2,1)S(1)}, bf16[64,1152]{1,0:T(8,128)(2,1)S(1)}, u32[]{:S(2)}, u32[]{:S(2)}) collective-permute-start(bf16[64,1152]{1,0:T(8,128)(2,1)S(1)} %reshape.12), channel_id=1, source_target_pairs={{40,0},{49,1},{32,8},{25,9},{56,16},{1,17},{48,24},{41,25},{8,32},... | collective-permute-start | bytes 442376 | tf_op jit(solution)/shard_map/ppermute | solution.py:287
  4.9 4.1 %collective-permute-start.2 = (bf16[64,1152]{1,0:T(8,128)(2,1)S(1)}, bf16[64,1152]{1,0:T(8,128)(2,1)S(1)}, u32[]{:S(2)}, u32[]{:S(2)}) collective-permute-start(bf16[64,1152]{1,0:T(8,128)(2,1)S(1)} %reshape.12), channel_id=1, source_target_pairs={{41,0},{48,1},{33,8},{24,9},{57,16},{0,17},{49,24},{40,25},{9,32},... | collective-permute-start | bytes 442376 | tf_op jit(solution)/shard_map/ppermute | solution.py:287
  9.0 5.7 %collective-permute-start.1 = (bf16[64,1152]{1,0:T(8,128)(2,1)S(1)}, bf16[64,1152]{1,0:T(8,128)(2,1)S(1)}, u32[]{:S(2)}, u32[]{:S(2)}) collective-permute-start(bf16[64,1152]{1,0:T(8,128)(2,1)S(1)} %reshape.12), channel_id=1, source_target_pairs={{0,0},{57,1},{8,8},{17,9},{16,16},{9,17},{24,24},{33,25},{32,32},{... | collective-permute-start | bytes 442376 | tf_op jit(solution)/shard_map/ppermute | solution.py:287
  14.7 0.1 collective-permute-start
  14.8 0.8 fusion.5.meta_ref._
  15.6 0.0 copy-start
  15.6 3.7 %copy-done = bf16[16,8,36864]{2,1,0:T(8,128)(2,1)S(1)} copy-done((bf16[16,8,36864]{2,1,0:T(8,128)(2,1)S(1)}, bf16[16,8,36864]{2,1,0:T(8,128)(2,1)}, u32[]{:S(2)}) %copy-start) | copy-done | bytes 9437208
  19.3 3.3 %pick_blocks.1.refs_0_ = bf16[4,8,2,9,32,128]{5,4,3,2,1,0:T(8,128)(2,1)S(1)} custom-call(s32[264]{0:T(512)S(1)} %fusion.5.meta_ref._, bf16[16,8,36864]{2,1,0:T(8,128)(2,1)S(1)} %copy-done), custom_call_target="tpu_custom_call" | custom-call | tf_op jit(solution)/shard_map/pick_blocks/pallas_call | solution.py:85
  22.6 0.0 collective-permute-done.3.refs_4_.near_ref
  22.6 0.0 collective-permute-done.2.refs_3_.far_ref
  22.6 0.0 collective-permute-done.1.refs_2_.near_ref
  22.6 0.0 collective-permute-done.refs_1_.far_ref
  22.7 0.0 copy-start.1
  22.7 61.9 %all_to_all.5 = bf16[32,576,128]{2,1,0:T(8,128)(2,1)S(1)} all-to-all(bf16[32,576,128]{2,1,0:T(8,128)(2,1)S(1)} %bitcast.7), channel_id=1, replica_groups=mesh['y'=4,'zhi'=4,'zlo'=2,'x'=4,'head'=2] {'y','zlo','x'}, dimensions={0} | all-to-all | bytes 9437184 | tf_op jit(solution)/shard_map/all_to_all | solution.py:296
  84.6 0.0 copy-done.1
  84.6 2.8 %attend.2 = (bf16[144,512]{1,0:T(8,128)(2,1)S(1)}, bf16[144,512]{1,0:T(8,128)(2,1)S(1)}) custom-call(s32[264]{0:T(512)S(1)} %fusion.5.meta_ref._, bf16[32,2,9,32,128]{4,3,2,1,0:T(8,128)(2,1)S(1)} %bitcast.5, bf16[64,1152]{1,0:T(8,128)(2,1)S(1)} %collective-permute-done.3.refs_4_.near_ref, bf16[64,1152]{1,0:T(8,128)(2,1)S(1)} %collective-permute-done.2.refs_3_.far_ref, ...), custom_call_target="tpu_custom_call" | custom-call | flops 1 | bytes 1 | tf_op jit(solution)/shard_map/attend/pallas_call | solution.py:196
  87.4 5.3 %collective-permute-start.5 = (bf16[144,512]{1,0:T(8,128)(2,1)S(1)}, bf16[144,512]{1,0:T(8,128)(2,1)S(1)}, u32[]{:S(2)}, u32[]{:S(2)}) collective-permute-start(bf16[144,512]{1,0:T(8,128)(2,1)S(1)} %get-tuple-element.10), channel_id=1, source_target_pairs={{0,41},{1,48},{8,33},{9,24},{16,57},{17,0},{24,49},{25,40},{32,9},... | collective-permute-start | bytes 442376 | tf_op jit(solution)/shard_map/ppermute | solution.py:287
  92.8 0.7 collective-permute-start.4
  93.5 2.8 %attend.3 = (bf16[144,512]{1,0:T(8,128)(2,1)S(1)}, bf16[144,512]{1,0:T(8,128)(2,1)S(1)}) custom-call(s32[264]{0:T(512)S(1)} %fusion.5.meta_ref._, bf16[32,2,9,32,128]{4,3,2,1,0:T(8,128)(2,1)S(1)} %bitcast.6, bf16[64,1152]{1,0:T(8,128)(2,1)S(1)} %collective-permute-done.1.refs_2_.near_ref, bf16[64,1152]{1,0:T(8,128)(2,1)S(1)} %collective-permute-done.refs_1_.far_ref, ...), custom_call_target="tpu_custom_call" | custom-call | flops 1 | bytes 1 | tf_op jit(solution)/shard_map/attend/pallas_call | solution.py:196
  96.3 2.7 %collective-permute-start.6 = (bf16[144,512]{1,0:T(8,128)(2,1)S(1)}, bf16[144,512]{1,0:T(8,128)(2,1)S(1)}, u32[]{:S(2)}, u32[]{:S(2)}) collective-permute-start(bf16[144,512]{1,0:T(8,128)(2,1)S(1)} %get-tuple-element.11), channel_id=1, source_target_pairs={{0,0},{1,57},{8,8},{9,17},{16,16},{17,9},{24,24},{25,33},{32,32},{... | collective-permute-start | bytes 442376 | tf_op jit(solution)/shard_map/ppermute | solution.py:287
  99.1 0.1 collective-permute-start.7
  99.2 0.0 collective-permute-done.5.refs_1_
  99.2 3.1 %collective-permute-done.4.refs_0_ = bf16[144,512]{1,0:T(8,128)(2,1)S(1)} collective-permute-done((bf16[144,512]{1,0:T(8,128)(2,1)S(1)}, bf16[144,512]{1,0:T(8,128)(2,1)S(1)}, u32[]{:S(2)}, u32[]{:S(2)}) %collective-permute-start.4) | collective-permute-done | bytes 147488 | tf_op jit(solution)/shard_map/ppermute | solution.py:287
  102.3 0.1 premerge.1.state
  102.4 2.0 %collective-permute-done.6.refs_0_ = bf16[144,512]{1,0:T(8,128)(2,1)S(1)} collective-permute-done((bf16[144,512]{1,0:T(8,128)(2,1)S(1)}, bf16[144,512]{1,0:T(8,128)(2,1)S(1)}, u32[]{:S(2)}, u32[]{:S(2)}) %collective-permute-start.6) | collective-permute-done | bytes 147488 | tf_op jit(solution)/shard_map/ppermute | solution.py:287
  104.4 0.0 collective-permute-done.7.refs_1_
  104.4 0.2 merge.1
  104.6 0.1 copy.5
  104.8 3.9 %all_gather.3 = bf16[2,65536]{1,0:T(2,128)(2,1)S(1)} all-gather(bf16[2,32768]{1,0:T(2,128)(2,1)S(1)} %bitcast.11), channel_id=1, replica_groups=mesh['y'=4,'zhi'=4,'zlo'=2,'x'=4,'head'=2] {'head'}, dimensions={1}, use_global_device_ids=true | all-gather | bytes 393216 | tf_op jit(solution)/shard_map/all_gather | solution.py:305
  108.7 0.7 copy.8
  (2 shorter events, 0.0 us)
Async XLA Ops:
  1.0 21.6 %collective-permute-start.3 = (bf16[64,1152]{1,0:T(8,128)(2,1)S(1)}, bf16[64,1152]{1,0:T(8,128)(2,1)S(1)}, u32[]{:S(2)}, u32[]{:S(2)}) collective-permute-start(bf16[64,1152]{1,0:T(8,128)(2,1)S(1)} %reshape.12), channel_id=1, source_target_pairs={{40,0},{49,1},{32,8},{25,9},{56,16},{1,17},{48,24},{41,25},{8,32},... | collective-permute-start | bytes 442376 | tf_op jit(solution)/shard_map/ppermute | solution.py:287
  4.9 17.7 %collective-permute-start.2 = (bf16[64,1152]{1,0:T(8,128)(2,1)S(1)}, bf16[64,1152]{1,0:T(8,128)(2,1)S(1)}, u32[]{:S(2)}, u32[]{:S(2)}) collective-permute-start(bf16[64,1152]{1,0:T(8,128)(2,1)S(1)} %reshape.12), channel_id=1, source_target_pairs={{41,0},{48,1},{33,8},{24,9},{57,16},{0,17},{49,24},{40,25},{9,32},... | collective-permute-start | bytes 442376 | tf_op jit(solution)/shard_map/ppermute | solution.py:287
  9.0 13.6 %collective-permute-start.1 = (bf16[64,1152]{1,0:T(8,128)(2,1)S(1)}, bf16[64,1152]{1,0:T(8,128)(2,1)S(1)}, u32[]{:S(2)}, u32[]{:S(2)}) collective-permute-start(bf16[64,1152]{1,0:T(8,128)(2,1)S(1)} %reshape.12), channel_id=1, source_target_pairs={{0,0},{57,1},{8,8},{17,9},{16,16},{9,17},{24,24},{33,25},{32,32},{... | collective-permute-start | bytes 442376 | tf_op jit(solution)/shard_map/ppermute | solution.py:287
  14.7 7.9 %collective-permute-start = (bf16[64,1152]{1,0:T(8,128)(2,1)S(1)}, bf16[64,1152]{1,0:T(8,128)(2,1)S(1)}, u32[]{:S(2)}, u32[]{:S(2)}) collective-permute-start(bf16[64,1152]{1,0:T(8,128)(2,1)S(1)} %reshape.12), channel_id=1, source_target_pairs={{1,0},{56,1},{9,8},{16,9},{17,16},{8,17},{25,24},{32,25},{33,32},{... | collective-permute-start | bytes 442376 | tf_op jit(solution)/shard_map/ppermute | solution.py:287
  15.6 3.7 %copy-start = (bf16[16,8,36864]{2,1,0:T(8,128)(2,1)S(1)}, bf16[16,8,36864]{2,1,0:T(8,128)(2,1)}, u32[]{:S(2)}) copy-start(bf16[16,8,36864]{2,1,0:T(8,128)(2,1)} %cache_ref.1) | copy-start | bytes 28311556
  22.7 62.0 %copy-start.1 = (s32[256,32]{0,1:T(8,128)S(1)}, s32[256,32]{0,1:T(8,128)}, u32[]{:S(2)}) copy-start(s32[256,32]{0,1:T(8,128)} %param.5) | copy-start | bytes 98308
  87.4 11.7 %collective-permute-start.5 = (bf16[144,512]{1,0:T(8,128)(2,1)S(1)}, bf16[144,512]{1,0:T(8,128)(2,1)S(1)}, u32[]{:S(2)}, u32[]{:S(2)}) collective-permute-start(bf16[144,512]{1,0:T(8,128)(2,1)S(1)} %get-tuple-element.10), channel_id=1, source_target_pairs={{0,41},{1,48},{8,33},{9,24},{16,57},{17,0},{24,49},{25,40},{32,9},... | collective-permute-start | bytes 442376 | tf_op jit(solution)/shard_map/ppermute | solution.py:287
  92.8 9.5 %collective-permute-start.4 = (bf16[144,512]{1,0:T(8,128)(2,1)S(1)}, bf16[144,512]{1,0:T(8,128)(2,1)S(1)}, u32[]{:S(2)}, u32[]{:S(2)}) collective-permute-start(bf16[144,512]{1,0:T(8,128)(2,1)S(1)} %get-tuple-element.9._), channel_id=1, source_target_pairs={{0,40},{1,49},{8,32},{9,25},{16,56},{17,1},{24,48},{25,41},{32,8},... | collective-permute-start | bytes 442376 | tf_op jit(solution)/shard_map/ppermute | solution.py:287
  96.3 8.1 %collective-permute-start.6 = (bf16[144,512]{1,0:T(8,128)(2,1)S(1)}, bf16[144,512]{1,0:T(8,128)(2,1)S(1)}, u32[]{:S(2)}, u32[]{:S(2)}) collective-permute-start(bf16[144,512]{1,0:T(8,128)(2,1)S(1)} %get-tuple-element.11), channel_id=1, source_target_pairs={{0,0},{1,57},{8,8},{9,17},{16,16},{17,9},{24,24},{25,33},{32,32},{... | collective-permute-start | bytes 442376 | tf_op jit(solution)/shard_map/ppermute | solution.py:287
  99.1 5.4 %collective-permute-start.7 = (bf16[144,512]{1,0:T(8,128)(2,1)S(1)}, bf16[144,512]{1,0:T(8,128)(2,1)S(1)}, u32[]{:S(2)}, u32[]{:S(2)}) collective-permute-start(bf16[144,512]{1,0:T(8,128)(2,1)S(1)} %get-tuple-element.12), channel_id=1, source_target_pairs={{0,1},{1,56},{8,9},{9,16},{16,17},{17,8},{24,25},{25,32},{32,33},{... | collective-permute-start | bytes 442376 | tf_op jit(solution)/shard_map/ppermute | solution.py:287

commit v4 on v3

--- a/solution.py
+++ b/solution.py
@@ -52,10 +52,22 @@
     return (zhi + jnp.where(core == 0, 2 - 2 * n, 3 - 2 * n)) % NK
 
 
-def pick_kernel(meta_ref, cache_ref, out_ref):
-    n = pl.program_id(1)
+def pick_kernel(meta_ref, cache_ref, out_ref, held_ref, sems):
+    y, n = pl.program_id(0), pl.program_id(1)
+
+    def fetch(y, n):
+        place = y * COUNT + n
+        request = y * NK + pick_pair(n, meta_ref)
+        return pltpu.make_async_copy(cache_ref.at[request], held_ref.at[place], sems.at[place])
+
+    @pl.when((y == 0) & (n == 0))
+    def _():
+        for yy in range(NY):
+            for nn in range(COUNT):
+                fetch(yy, nn).start(priority=nn)
+
     core = meta_ref[2 * SEQ + 1]
-    base = (pl.program_id(0) * NK + pick_pair(n, meta_ref)) * (2 * NX)
+    base = (y * NK + pick_pair(n, meta_ref)) * (2 * NX)
     row = lax.broadcasted_iota(jnp.int32, (2 * NX * UNIT, BLK_DEV * UNIT), 0)
     col = lax.broadcasted_iota(jnp.int32, (2 * NX * UNIT, BLK_DEV * UNIT), 1)
     slot, token, held = row >> 4, (col >> 3) == (row & (UNIT - 1)), col & (BLK_DEV - 1)
@@ -64,9 +76,10 @@
         inner = jnp.maximum(meta_ref[2 * (base + j)], meta_ref[2 * (base + j) + 1])
         block = jnp.where(slot == j, inner, block)
     onehot = jnp.where(token & (held == block), 1.0, 0.0).astype(jnp.bfloat16)
+    fetch(y, n).wait()
     for half in range(2):
         pieces = [
-            cache_ref[0, :, p * PAIR_WIDTH : (p + 1) * PAIR_WIDTH].astype(jnp.float32)
+            held_ref[y * COUNT + n, :, p * PAIR_WIDTH : (p + 1) * PAIR_WIDTH].astype(jnp.float32)
             for p in range(half * UNIT, (half + 1) * UNIT)
         ]
         stacked = jnp.concatenate(pieces, axis=0).astype(jnp.bfloat16)
@@ -88,17 +101,16 @@
         grid_spec=pltpu.PrefetchScalarGridSpec(
             num_scalar_prefetch=1,
             grid=(NY, COUNT),
-            in_specs=[
-                pl.BlockSpec(
-                    (1, BLK_DEV, BLOCK * FEAT),
-                    lambda y, n, meta: (y * NK + pick_pair(n, meta), 0, 0),
-                )
-            ],
+            in_specs=[pl.BlockSpec(memory_space=pl.ANY)],
             out_specs=pl.BlockSpec(
                 (1, 2 * NX, COUNT, TILES, PAIRS, 128), lambda y, n, meta: (y, 0, 0, 0, 0, 0)
             ),
+            scratch_shapes=[
+                pltpu.VMEM((NY * COUNT, BLK_DEV, BLOCK * FEAT), jnp.bfloat16),
+                pltpu.SemaphoreType.DMA((NY * COUNT,)),
+            ],
         ),
-        compiler_params=pltpu.CompilerParams(vmem_limit_bytes=12 * MIB),
+        compiler_params=pltpu.CompilerParams(vmem_limit_bytes=46 * MIB),
         name="pick_blocks",
     )(meta, cache)
 
@@ -129,14 +141,14 @@
     return low, high
 
 
-def attend_kernel(i, meta_ref, blocks_ref, near_ref, far_ref, selected_ref, _, near_out, far_out):
+def attend_kernel(i, meta_ref, blocks_ref, queries_ref, selected_ref, _, out_ref):
     width = GROUP * PAIRS
     pairs = jnp.concatenate(
         [blocks_ref[:, 0, t].reshape(width, 128) for t in range(TILES)], axis=1
     )
     low, high = [], []
-    for ref in (near_ref, far_ref):
-        parts = spread_queries(ref[...])
+    for half in range(2):
+        parts = spread_queries(queries_ref[half])
         low += parts[0]
         high += parts[1]
     query = jnp.concatenate(low, axis=0).astype(jnp.bfloat16)
@@ -172,98 +184,104 @@
     )
     odd_value = jnp.dot(odd.astype(jnp.bfloat16), odd_keys, preferred_element_type=jnp.float32)
     value = (value + odd_value[:, KR : KR + KL]) * (1.0 / total)
-    value = value.astype(jnp.bfloat16)
     level = top + jnp.log(total)
-    across = jnp.transpose(jnp.broadcast_to(level, (2 * ROWS, 128)))[:TAIL]
-    for half, out_ref in enumerate((near_out, far_out)):
-        span = slice(half * ROWS, (half + 1) * ROWS)
-        wide = across[:, span]
-        high = wide.astype(jnp.bfloat16).astype(jnp.float32)
-        middle = (wide - high).astype(jnp.bfloat16).astype(jnp.float32)
-        low = wide - high - middle
-        line = lax.broadcasted_iota(jnp.int32, wide.shape, 0)
-        tail = jnp.where(
-            line == 0, high, jnp.where(line == 1, middle, jnp.where(line == 2, low, 0.0))
-        )
-        out_ref[:ROWS] = value[span]
-        out_ref[ROWS:, :ROWS] = tail.astype(jnp.bfloat16)
-        out_ref[ROWS:, ROWS:] = jnp.zeros((TAIL, KL - ROWS), jnp.bfloat16)
-
-
-def attend(i, meta, blocks, near, far, selected, earlier):
-    part = jax.ShapeDtypeStruct((ROWS + TAIL, KL), jnp.bfloat16)
-    query = pl.BlockSpec((ROWS // 2, PAIR_WIDTH), lambda n, meta: (0, 0))
+    wide = jnp.transpose(jnp.broadcast_to(level, (2 * ROWS, 128)))[:TAIL]
+    high = wide.astype(jnp.bfloat16).astype(jnp.float32)
+    middle = (wide - high).astype(jnp.bfloat16).astype(jnp.float32)
+    low = wide - high - middle
+    line = lax.broadcasted_iota(jnp.int32, wide.shape, 0)
+    tail = jnp.where(line == 0, high, jnp.where(line == 1, middle, jnp.where(line == 2, low, 0.0)))
+    out_ref[: 2 * ROWS] = value.astype(jnp.bfloat16)
+    out_ref[2 * ROWS :, : 2 * ROWS] = tail.astype(jnp.bfloat16)
+    out_ref[2 * ROWS :, 2 * ROWS :] = jnp.zeros((TAIL, KL - 2 * ROWS), jnp.bfloat16)
+
+
+def attend(i, meta, blocks, queries, selected, earlier):
+    shape = (2 * ROWS + TAIL, KL)
     return pl.pallas_call(
         functools.partial(attend_kernel, i),
-        out_shape=[part, part],
+        out_shape=jax.ShapeDtypeStruct(shape, jnp.bfloat16),
         grid_spec=pltpu.PrefetchScalarGridSpec(
             num_scalar_prefetch=1,
             grid=(1,),
             in_specs=[
                 pl.BlockSpec((GROUP, 1, TILES, PAIRS, 128), lambda n, meta: (0, i, 0, 0, 0)),
-                query,
-                query,
+                pl.BlockSpec(queries.shape, lambda n, meta: (0, 0, 0)),
                 pl.BlockSpec(selected.shape, lambda n, meta: (0, 0)),
                 pl.BlockSpec(memory_space=pl.ANY),
             ],
-            out_specs=[pl.BlockSpec((ROWS + TAIL, KL), lambda n, meta: (0, 0))] * 2,
+            out_specs=pl.BlockSpec(shape, lambda n, meta: (0, 0)),
         ),
         compiler_params=pltpu.CompilerParams(vmem_limit_bytes=24 * MIB),
         cost_estimate=pl.CostEstimate(flops=1, bytes_accessed=1, transcendentals=0),
         name="attend",
-    )(meta, blocks, near, far, selected, earlier)
-
-
-def weigh(parts, levels):
+    )(meta, blocks, queries, selected, earlier)
+
+
+def weigh(values, levels):
     peak = functools.reduce(jnp.maximum, levels)
     weights = [jnp.exp(level - peak) for level in levels]
     total = functools.reduce(jnp.add, weights)
     scale = 1.0 / total
     mean = jnp.zeros((ROWS, KL), jnp.float32)
-    for part, weight in zip(parts, weights):
+    for value, weight in zip(values, weights):
         column = jnp.transpose(jnp.broadcast_to(weight * scale, (128, ROWS)))
         factor = jnp.concatenate([column] * (KL // 128), axis=1)
-        mean = mean + factor * part[:ROWS].astype(jnp.float32)
+        mean = mean + factor * value.astype(jnp.float32)
     return mean, peak + jnp.log(total)
 
 
-def level_of(part):
-    return jnp.sum(part[ROWS:, :ROWS].astype(jnp.float32), axis=0, keepdims=True)
-
-
-def premerge_kernel(*refs):
-    parts, out_ref = refs[:-1], refs[-1]
-    mean, level = weigh(parts, [level_of(part) for part in parts])
-    out_ref[:ROWS] = mean
-    out_ref[ROWS:, :ROWS] = jnp.broadcast_to(level, (8, ROWS))
-    out_ref[ROWS:, ROWS:] = jnp.zeros((8, KL - ROWS), jnp.float32)
-
-
-def premerge(parts):
+def halves_of(ref, half):
+    tail = ref[2 * ROWS :, half * ROWS : (half + 1) * ROWS].astype(jnp.float32)
+    return ref[half * ROWS : (half + 1) * ROWS], jnp.sum(tail, axis=0, keepdims=True)
+
+
+def premerge_kernel(mine_ref, other_ref, out_ref):
+    for half in range(2):
+        views = [halves_of(mine_ref, half), halves_of(other_ref, 1 - half)]
+        mean, level = weigh([view[0] for view in views], [view[1] for view in views])
+        out_ref[half, :ROWS] = mean
+        out_ref[half, ROWS:, :ROWS] = jnp.broadcast_to(level, (8, ROWS))
+        out_ref[half, ROWS:, ROWS:] = jnp.zeros((8, KL - ROWS), jnp.float32)
+
+
+def premerge(mine, other):
     return pl.pallas_call(
         premerge_kernel,
-        out_shape=jax.ShapeDtypeStruct((ROWS + 8, KL), jnp.float32),
+        out_shape=jax.ShapeDtypeStruct((2, ROWS + 8, KL), jnp.float32),
         compiler_params=pltpu.CompilerParams(vmem_limit_bytes=8 * MIB),
         name="premerge",
-    )(*parts)
-
-
-def merge_kernel(state, *refs):
-    parts, out_ref = refs[:-1], refs[-1]
-    levels = [state[ROWS : ROWS + 1, :ROWS]] + [level_of(part) for part in parts]
-    mean, _ = weigh((state,) + parts, levels)
-    mean = mean.astype(jnp.bfloat16).reshape(2, RDEV, HEADS // 2, KL)
-    for odd in range(2):
-        out_ref[:, :, odd * KL : (odd + 1) * KL] = mean[odd]
-
-
-def merge(parts):
+    )(mine, other)
+
+
+def merge_kernel(meta_ref, state_ref, mine_ref, other_ref, out_ref):
+    core = meta_ref[2 * SEQ + 1]
+    for half in range(2):
+        state = (state_ref[half, :ROWS], state_ref[half, ROWS : ROWS + 1, :ROWS])
+        views = [state, halves_of(mine_ref, half), halves_of(other_ref, 1 - half)]
+        mean, _ = weigh([view[0] for view in views], [view[1] for view in views])
+        mean = mean.astype(jnp.bfloat16).reshape(2, RDEV, HEADS // 2, KL)
+        for odd in range(2):
+            out_ref[:, core ^ half, :, odd * KL : (odd + 1) * KL] = mean[odd]
+
+
+def merge(meta, parts):
+    shape = (RDEV, 2, HEADS // 2, 2 * KL)
     return pl.pallas_call(
         merge_kernel,
-        out_shape=jax.ShapeDtypeStruct((RDEV, HEADS // 2, 2 * KL), jnp.bfloat16),
-        compiler_params=pltpu.CompilerParams(vmem_limit_bytes=8 * MIB),
+        out_shape=jax.ShapeDtypeStruct(shape, jnp.bfloat16),
+        grid_spec=pltpu.PrefetchScalarGridSpec(
+            num_scalar_prefetch=1,
+            grid=(1,),
+            in_specs=[
+                pl.BlockSpec(part.shape, lambda n, meta, rank=part.ndim: (0,) * rank)
+                for part in parts
+            ],
+            out_specs=pl.BlockSpec(shape, lambda n, meta: (0, 0, 0, 0)),
+        ),
+        compiler_params=pltpu.CompilerParams(vmem_limit_bytes=12 * MIB),
         name="merge",
-    )(*parts)
+    )(meta, *parts)
 
 
 def per_device(queries, cache, selected):
@@ -286,23 +304,24 @@
         pairs = [pair[::-1] for pair in pairs] if back else pairs
         return lax.ppermute(value, ("zhi", "zlo", "head"), pairs)
 
+    swap = [(0, 1), (1, 0)]
     packed = queries.reshape(ROWS // 2, PAIR_WIDTH)
-    asked = {}
-    for i in (1, 0):
-        for cross in (1, 0):
-            asked[i, cross] = move(packed, i, True, cross)
-    picked = tie(pick_blocks(meta, cache), *asked.values())
+    both = jnp.stack([packed, lax.ppermute(packed, "head", swap)])
+    asked = [jnp.stack([move(packed, 0, True, cross) for cross in range(2)])]
+    picked = tie(pick_blocks(meta, cache), *asked, both)
     picked = picked.reshape(GROUP, COUNT * TILES * PAIRS, 128)
     blocks = lax.all_to_all(picked, ("y", "zlo", "x"), split_axis=0, concat_axis=0, tiled=True)
     blocks = blocks.reshape(GROUP, COUNT, TILES, PAIRS, 128)
-
-    parts, earlier = [], meta
+    asked.append(move(tie(both, blocks), 1, True, 0))
+
+    mine, other, earlier = [], [], meta
     for i in range(COUNT):
-        near, far = attend(i, meta, blocks, asked[i, 0], asked[i, 1], selected.T, earlier)
-        parts.append([move(near, i, False, 0), move(far, i, False, 1)])
-        earlier = near
-    result = merge([premerge(parts[0])] + parts[1]).reshape(RDEV, HEADS * KL)
-    return lax.all_gather(result, "head", axis=1, tiled=True)
+        part = attend(i, meta, blocks, asked[i], selected.T, earlier)
+        earlier = part
+        mine.append(move(part, i, False, 0))
+        other.append(lax.ppermute(mine[i], "head", swap))
+    state = premerge(mine[0], other[0])
+    return merge(meta, [state, mine[1], other[1]]).reshape(RDEV, 2 * HEADS * KL)
 
 
 def solution(mesh):

time: 110 us -> 105 us (0.955)
  blocking collectives: 65.8 us -> 59.9 us
  local copies, waits for them, and re-layouts: 5.52 us -> 2.98 us
  Pallas kernels: 9.23 us -> 11.7 us
  starting transfers between devices: 22.6 us -> 24.4 us
    ppermute x0 -> x3, starting transfers between devices: none -> 8.51 us  [the longest x2 5.19 us: per_device(): other.append(lax.ppermute(mine[i], 'head', swap))]
    ppermute x8 -> x5, starting transfers between devices: 22.6 us -> 15.9 us  [move(): return lax.ppermute(value, ('zhi', 'zlo', 'head'), pairs)]
    all_gather x1 -> x0, blocking collectives: 3.9 us -> none  [per_device(): return lax.all_gather(result, 'head', axis=1, tiled=True)]
    unnamed x6 -> x3, local copies, waits for them, and re-layouts: 4.52 us -> 0.98 us
    all_to_all x1, blocking collectives: 61.9 us -> 59.9 us  [per_device(): lax.all_to_all(picked, ('y', 'zlo', 'x'), split_axis=0, concat_axis=0, ti...]
    pallas_call x1, Pallas kernels: 3.28 us -> 5.02 us  [pick_blocks(): pl.pallas_call(pick_kernel, out_shape=jax.ShapeDtypeStruct((NY, 2 * NX, C...]
    ppermute x8 -> x5, waiting for transfers between devices: 5.16 us -> 3.78 us  [move(): return lax.ppermute(value, ('zhi', 'zlo', 'head'), pairs)]
    ppermute x0 -> x3, waiting for transfers between devices: none -> 1.36 us  [the longest x2 1.36 us: per_device(): other.append(lax.ppermute(mine[i], 'head', swap))]
  transfers between devices with their start and end apart: 8 -> 8, of which waited for: 2 -> 3; matrix products, arithmetic and copies ran while one was open for 1% -> 2% of each run, Pallas kernels for 6% -> 10%
where the time goes in v4:
time: 105 us
  blocking collectives  59.9 us (57%)
  starting transfers between devices  24.4 us (23%)
  Pallas kernels  11.7 us (11%)
  waiting for transfers between devices  5.14 us (5%)
  local copies, waits for them, and re-layouts  2.98 us (3%)
    all_to_all x1, blocking collectives, per_device(): lax.all_to_all(picked, ('y', 'zlo', 'x'), split_axis=0, concat_axis=0, ti...  59.9 us
    ppermute x5, starting transfers between devices, move(): return lax.ppermute(value, ('zhi', 'zlo', 'head'), pairs)  15.9 us
    pallas_call x2, Pallas kernels, attend(): pl.pallas_call(functools.partial(attend_kernel, i), out_shape=jax.ShapeDt...  5.65 us
    ppermute x2, starting transfers between devices, per_device(): other.append(lax.ppermute(mine[i], 'head', swap))  5.19 us
    pallas_call x1, Pallas kernels, pick_blocks(): pl.pallas_call(pick_kernel, out_shape=jax.ShapeDtypeStruct((NY, 2 * NX, C...  5.02 us
    ppermute x5, waiting for transfers between devices, move(): return lax.ppermute(value, ('zhi', 'zlo', 'head'), pairs)  3.78 us
    ppermute x1, starting transfers between devices, per_device(): both = jnp.stack([packed, lax.ppermute(packed, 'head', swap)])  3.33 us
  transfers between devices with their start and end apart: 8, of which 3 were waited for; matrix products, arithmetic and copies ran while one was open for 2% of the time, Pallas kernels for 10%

profile of v4, /device:TPU:1, one launch (start us, length us, event | category | flops | bytes accessed | tf_op | source)
XLA Modules:
  0.0 105.1 jit_solution(6593311251212198786)
XLA Ops:
  0.0 1.0 reshape.12
  1.0 3.3 %collective-permute-start.2 = (bf16[64,1152]{1,0:T(8,128)(2,1)S(1)}, bf16[64,1152]{1,0:T(8,128)(2,1)S(1)}, u32[]{:S(2)}, u32[]{:S(2)}) collective-permute-start(bf16[64,1152]{1,0:T(8,128)(2,1)S(1)} %reshape.12), channel_id=1, source_target_pairs={{0,1},{1,0},{2,3},{3,2},{4,5},{5,4},{6,7},{7,6},{8,9},{9,8},{10,11... | collective-permute-start | bytes 442376 | tf_op jit(solution)/shard_map/ppermute | solution.py:309
  4.3 4.7 %collective-permute-start.1 = (bf16[64,1152]{1,0:T(8,128)(2,1)S(1)}, bf16[64,1152]{1,0:T(8,128)(2,1)S(1)}, u32[]{:S(2)}, u32[]{:S(2)}) collective-permute-start(bf16[64,1152]{1,0:T(8,128)(2,1)S(1)} %reshape.12), channel_id=1, source_target_pairs={{41,0},{48,1},{33,8},{24,9},{57,16},{0,17},{49,24},{40,25},{9,32},... | collective-permute-start | bytes 442376 | tf_op jit(solution)/shard_map/ppermute | solution.py:305
  9.0 1.2 %collective-permute-start = (bf16[64,1152]{1,0:T(8,128)(2,1)S(1)}, bf16[64,1152]{1,0:T(8,128)(2,1)S(1)}, u32[]{:S(2)}, u32[]{:S(2)}) collective-permute-start(bf16[64,1152]{1,0:T(8,128)(2,1)S(1)} %reshape.12), channel_id=1, source_target_pairs={{40,0},{49,1},{32,8},{25,9},{56,16},{1,17},{48,24},{41,25},{8,32},... | collective-permute-start | bytes 442376 | tf_op jit(solution)/shard_map/ppermute | solution.py:305
  10.2 1.0 stack_reshape.3
  11.3 0.8 fusion.5.meta_ref._
  12.1 5.0 %pick_blocks.1.refs_0_ = bf16[4,8,2,9,32,128]{5,4,3,2,1,0:T(8,128)(2,1)S(1)} custom-call(s32[264]{0:T(512)S(1)} %fusion.5.meta_ref._, bf16[16,8,36864]{2,1,0:T(8,128)(2,1)} %cache_ref.1), custom_call_target="tpu_custom_call" | custom-call | tf_op jit(solution)/shard_map/pick_blocks/pallas_call | solution.py:98
  17.1 0.0 collective-permute-done.2
  17.1 1.3 %collective-permute-done.1 = bf16[64,1152]{1,0:T(8,128)(2,1)S(1)} collective-permute-done((bf16[64,1152]{1,0:T(8,128)(2,1)S(1)}, bf16[64,1152]{1,0:T(8,128)(2,1)S(1)}, u32[]{:S(2)}, u32[]{:S(2)}) %collective-permute-start.1) | collective-permute-done | bytes 147488 | tf_op jit(solution)/shard_map/ppermute | solution.py:305
  18.5 0.0 collective-permute-done
  18.5 59.9 %all_to_all.5 = bf16[32,576,128]{2,1,0:T(8,128)(2,1)S(1)} all-to-all(bf16[32,576,128]{2,1,0:T(8,128)(2,1)S(1)} %bitcast.12), channel_id=1, replica_groups=mesh['y'=4,'zhi'=4,'zlo'=2,'x'=4,'head'=2] {'y','zlo','x'}, dimensions={0} | all-to-all | bytes 9437184 | tf_op jit(solution)/shard_map/all_to_all | solution.py:313
  78.5 0.0 copy-start
  78.5 4.2 %collective-permute-start.5 = (bf16[2,64,1152]{2,1,0:T(8,128)(2,1)S(1)}, bf16[2,64,1152]{2,1,0:T(8,128)(2,1)S(1)}, u32[]{:S(2)}, u32[]{:S(2)}) collective-permute-start(bf16[2,64,1152]{2,1,0:T(8,128)(2,1)S(1)} %tie.3), channel_id=1, source_target_pairs={{0,0},{57,1},{8,8},{17,9},{16,16},{9,17},{24,24},{33,25},{32,32},{... | collective-permute-start | bytes 884744 | tf_op jit(solution)/shard_map/ppermute | solution.py:305
  82.6 0.0 copy-done
  82.7 2.8 %attend.2._ = bf16[272,512]{1,0:T(8,128)(2,1)S(1)} custom-call(s32[264]{0:T(512)S(1)} %fusion.5.meta_ref._, bf16[32,2,9,32,128]{4,3,2,1,0:T(8,128)(2,1)S(1)} %bitcast.10, bf16[2,64,1152]{2,1,0:T(8,128)(2,1)S(1)} %pad_maximum_fusion.refs_1_.queries_ref, s32[32,256]{1,0:T(8,128)S(1)} %bitcast.14, s32[264]{0:T(512)S(1)} %fusion.5.meta_ref._), custom_call_target="tpu_custom_call" | custom-call | flops 1 | bytes 1 | tf_op jit(solution)/shard_map/attend/pallas_call | solution.py:201
  85.5 2.3 %collective-permute-start.3 = (bf16[272,512]{1,0:T(8,128)(2,1)S(1)}, bf16[272,512]{1,0:T(8,128)(2,1)S(1)}, u32[]{:S(2)}, u32[]{:S(2)}) collective-permute-start(bf16[272,512]{1,0:T(8,128)(2,1)S(1)} %attend.2._), channel_id=1, source_target_pairs={{0,40},{1,49},{8,32},{9,25},{16,56},{17,1},{24,48},{25,41},{32,8},... | collective-permute-start | bytes 835592 | tf_op jit(solution)/shard_map/ppermute | solution.py:305
  87.8 0.0 collective-permute-done.5.queries_ref
  87.8 2.8 %attend.3 = bf16[272,512]{1,0:T(8,128)(2,1)S(1)} custom-call(s32[264]{0:T(512)S(1)} %fusion.5.meta_ref._, bf16[32,2,9,32,128]{4,3,2,1,0:T(8,128)(2,1)S(1)} %bitcast.11, bf16[2,64,1152]{2,1,0:T(8,128)(2,1)S(1)} %collective-permute-done.5.queries_ref, s32[32,256]{1,0:T(8,128)S(1)} %bitcast.15, bf16[272,512]{1,0:T(8,128)(2,1)S(1)} %attend.2._), custom_call_target="tpu_custom_call" | custom-call | flops 1 | bytes 1 | tf_op jit(solution)/shard_map/attend/pallas_call | solution.py:201
  90.7 3.5 %collective-permute-start.6 = (bf16[272,512]{1,0:T(8,128)(2,1)S(1)}, bf16[272,512]{1,0:T(8,128)(2,1)S(1)}, u32[]{:S(2)}, u32[]{:S(2)}) collective-permute-start(bf16[272,512]{1,0:T(8,128)(2,1)S(1)} %attend.3), channel_id=1, source_target_pairs={{0,0},{1,57},{8,8},{9,17},{16,16},{17,9},{24,24},{25,33},{32,32},{... | collective-permute-start | bytes 835592 | tf_op jit(solution)/shard_map/ppermute | solution.py:305
  94.2 0.0 collective-permute-done.3.mine_ref
  94.2 5.2 %collective-permute-start.4 = (bf16[272,512]{1,0:T(8,128)(2,1)S(1)}, bf16[272,512]{1,0:T(8,128)(2,1)S(1)}, u32[]{:S(2)}, u32[]{:S(2)}) collective-permute-start(bf16[272,512]{1,0:T(8,128)(2,1)S(1)} %collective-permute-done.3.mine_ref), channel_id=1, source_target_pairs={{0,1},{1,0},{2,3},{3,2},{4,5},{5,4},{6,7},{7,6},{8,9},{9,8},{10,11... | collective-permute-start | bytes 835592 | tf_op jit(solution)/shard_map/ppermute | solution.py:322
  99.3 2.5 %collective-permute-done.6.mine_ref = bf16[272,512]{1,0:T(8,128)(2,1)S(1)} collective-permute-done((bf16[272,512]{1,0:T(8,128)(2,1)S(1)}, bf16[272,512]{1,0:T(8,128)(2,1)S(1)}, u32[]{:S(2)}, u32[]{:S(2)}) %collective-permute-start.6) | collective-permute-done | bytes 278560 | tf_op jit(solution)/shard_map/ppermute | solution.py:305
  101.8 0.0 collective-permute-start.7
  101.8 0.0 collective-permute-done.4.other_ref
  101.8 0.2 premerge.1.state_ref
  102.0 1.4 %collective-permute-done.7.other_ref = bf16[272,512]{1,0:T(8,128)(2,1)S(1)} collective-permute-done((bf16[272,512]{1,0:T(8,128)(2,1)S(1)}, bf16[272,512]{1,0:T(8,128)(2,1)S(1)}, u32[]{:S(2)}, u32[]{:S(2)}) %collective-permute-start.7) | collective-permute-done | bytes 278560 | tf_op jit(solution)/shard_map/ppermute | solution.py:322
  103.4 0.8 merge.1
  104.2 1.0 copy.6
  (5 shorter events, 0.1 us)
Async XLA Ops:
  1.0 16.1 %collective-permute-start.2 = (bf16[64,1152]{1,0:T(8,128)(2,1)S(1)}, bf16[64,1152]{1,0:T(8,128)(2,1)S(1)}, u32[]{:S(2)}, u32[]{:S(2)}) collective-permute-start(bf16[64,1152]{1,0:T(8,128)(2,1)S(1)} %reshape.12), channel_id=1, source_target_pairs={{0,1},{1,0},{2,3},{3,2},{4,5},{5,4},{6,7},{7,6},{8,9},{9,8},{10,11... | collective-permute-start | bytes 442376 | tf_op jit(solution)/shard_map/ppermute | solution.py:309
  4.3 14.1 %collective-permute-start.1 = (bf16[64,1152]{1,0:T(8,128)(2,1)S(1)}, bf16[64,1152]{1,0:T(8,128)(2,1)S(1)}, u32[]{:S(2)}, u32[]{:S(2)}) collective-permute-start(bf16[64,1152]{1,0:T(8,128)(2,1)S(1)} %reshape.12), channel_id=1, source_target_pairs={{41,0},{48,1},{33,8},{24,9},{57,16},{0,17},{49,24},{40,25},{9,32},... | collective-permute-start | bytes 442376 | tf_op jit(solution)/shard_map/ppermute | solution.py:305
  9.0 9.4 %collective-permute-start = (bf16[64,1152]{1,0:T(8,128)(2,1)S(1)}, bf16[64,1152]{1,0:T(8,128)(2,1)S(1)}, u32[]{:S(2)}, u32[]{:S(2)}) collective-permute-start(bf16[64,1152]{1,0:T(8,128)(2,1)S(1)} %reshape.12), channel_id=1, source_target_pairs={{40,0},{49,1},{32,8},{25,9},{56,16},{1,17},{48,24},{41,25},{8,32},... | collective-permute-start | bytes 442376 | tf_op jit(solution)/shard_map/ppermute | solution.py:305
  78.5 4.2 %copy-start = (s32[256,32]{0,1:T(8,128)S(1)}, s32[256,32]{0,1:T(8,128)}, u32[]{:S(2)}) copy-start(s32[256,32]{0,1:T(8,128)} %param.5) | copy-start | bytes 98308
  78.5 9.4 %collective-permute-start.5 = (bf16[2,64,1152]{2,1,0:T(8,128)(2,1)S(1)}, bf16[2,64,1152]{2,1,0:T(8,128)(2,1)S(1)}, u32[]{:S(2)}, u32[]{:S(2)}) collective-permute-start(bf16[2,64,1152]{2,1,0:T(8,128)(2,1)S(1)} %tie.3), channel_id=1, source_target_pairs={{0,0},{57,1},{8,8},{17,9},{16,16},{9,17},{24,24},{33,25},{32,32},{... | collective-permute-start | bytes 884744 | tf_op jit(solution)/shard_map/ppermute | solution.py:305
  85.5 8.7 %collective-permute-start.3 = (bf16[272,512]{1,0:T(8,128)(2,1)S(1)}, bf16[272,512]{1,0:T(8,128)(2,1)S(1)}, u32[]{:S(2)}, u32[]{:S(2)}) collective-permute-start(bf16[272,512]{1,0:T(8,128)(2,1)S(1)} %attend.2._), channel_id=1, source_target_pairs={{0,40},{1,49},{8,32},{9,25},{16,56},{17,1},{24,48},{25,41},{32,8},... | collective-permute-start | bytes 835592 | tf_op jit(solution)/shard_map/ppermute | solution.py:305
  90.7 11.1 %collective-permute-start.6 = (bf16[272,512]{1,0:T(8,128)(2,1)S(1)}, bf16[272,512]{1,0:T(8,128)(2,1)S(1)}, u32[]{:S(2)}, u32[]{:S(2)}) collective-permute-start(bf16[272,512]{1,0:T(8,128)(2,1)S(1)} %attend.3), channel_id=1, source_target_pairs={{0,0},{1,57},{8,8},{9,17},{16,16},{17,9},{24,24},{25,33},{32,32},{... | collective-permute-start | bytes 835592 | tf_op jit(solution)/shard_map/ppermute | solution.py:305
  94.2 7.6 %collective-permute-start.4 = (bf16[272,512]{1,0:T(8,128)(2,1)S(1)}, bf16[272,512]{1,0:T(8,128)(2,1)S(1)}, u32[]{:S(2)}, u32[]{:S(2)}) collective-permute-start(bf16[272,512]{1,0:T(8,128)(2,1)S(1)} %collective-permute-done.3.mine_ref), channel_id=1, source_target_pairs={{0,1},{1,0},{2,3},{3,2},{4,5},{5,4},{6,7},{7,6},{8,9},{9,8},{10,11... | collective-permute-start | bytes 835592 | tf_op jit(solution)/shard_map/ppermute | solution.py:322
  101.8 1.6 %collective-permute-start.7 = (bf16[272,512]{1,0:T(8,128)(2,1)S(1)}, bf16[272,512]{1,0:T(8,128)(2,1)S(1)}, u32[]{:S(2)}, u32[]{:S(2)}) collective-permute-start(bf16[272,512]{1,0:T(8,128)(2,1)S(1)} %collective-permute-done.6.mine_ref), channel_id=1, source_target_pairs={{0,1},{1,0},{2,3},{3,2},{4,5},{5,4},{6,7},{7,6},{8,9},{9,8},{10,11... | collective-permute-start | bytes 835592 | tf_op jit(solution)/shard_map/ppermute | solution.py:322

commit v5 on v4

v5 whole, which is shorter than its diff:
```python
import functools

import jax
import jax.numpy as jnp
from jax import lax
from jax.experimental import pallas as pl
from jax.experimental.pallas import tpu as pltpu
from jax.sharding import Mesh
from jax.sharding import PartitionSpec as P

KL = 512
KR = 64
FEAT = KL + KR
WIDE = KL + 2 * KR
BLOCK = 64
PAIRS = BLOCK // 2
UNIT = PAIRS // 2
PAIR_WIDTH = 2 * FEAT
SPAN = UNIT * PAIR_WIDTH
TILES = PAIR_WIDTH // 128
TOPK = 32
RDEV = 2
BLK_DEV = 8
HEADS = 64
NY, NZ, NX = 4, 8, 4
NK = NZ // 2
GROUP = NY * 2 * NX
SEQ = NY * NZ * NX
ROWS = RDEV * HEADS
TAIL = 16
EMPTY = -1e30
MIB = 1024 * 1024

score_scale = 192.0 ** (-0.5)

COUNT = 2


def owner_place(zhi, zlo, core, i):
    if core == 0:
        return ((zhi + 2) % NK, 1 - zlo) if i == 0 else (zhi, zlo)
    return (zhi + 3 - 2 * zlo) % NK, zlo if i == 0 else 1 - zlo


def here():
    return tuple(lax.axis_index(name) for name in ("y", "zhi", "zlo", "x", "head"))


def pick_kernel(selected_ref, cache_ref, out_ref, held_ref, sems):
    steps = [(y, n) for y in range(NY) for n in range(COUNT)]
    y, zhi, zlo, x, core = here()
    pairs = [(zhi + jnp.where(core == 0, 2 - 2 * n, 3 - 2 * n)) % NK for n in range(COUNT)]

    def fetch(s):
        request = steps[s][0] * NK + pairs[steps[s][1]]
        return pltpu.make_async_copy(cache_ref.at[request], held_ref.at[s], sems.at[s])

    for s in range(len(steps)):
        fetch(s).start(priority=s % 2)
    me = ((y * NK + zhi) * 2 + zlo) * NX + x
    selected = selected_ref[...]
    inner = jnp.where((selected >> 3) == me, selected & (BLK_DEV - 1), -1)
    inner = jnp.max(inner, axis=0, keepdims=True)
    inner = jnp.maximum(inner, pltpu.roll(inner, SEQ * RDEV - 1, 1))
    row = lax.broadcasted_iota(jnp.int32, (2 * NX * UNIT, BLK_DEV * UNIT), 0)
    col = lax.broadcasted_iota(jnp.int32, (2 * NX * UNIT, BLK_DEV * UNIT), 1)
    token, held = (col >> 3) == (row & (UNIT - 1)), col & (BLK_DEV - 1)
    lane = lax.broadcasted_iota(jnp.int32, (2 * NX * UNIT, SEQ * RDEV), 1)
    slot = lax.broadcasted_iota(jnp.int32, (2 * NX * UNIT, SEQ * RDEV), 0) >> 4
    for s, (y, n) in enumerate(steps):
        base = (y * NK + pairs[n]) * (2 * NX)
        mine = lane == RDEV * (base + slot)
        block = jnp.sum(jnp.where(mine, inner, 0), axis=1, keepdims=True)
        onehot = jnp.where(token & (held == block), 1.0, 0.0).astype(jnp.bfloat16)
        fetch(s).wait()
        for half in range(2):
            pieces = [
                held_ref[s, :, p * PAIR_WIDTH : (p + 1) * PAIR_WIDTH].astype(jnp.float32)
                for p in range(half * UNIT, (half + 1) * UNIT)
            ]
            stacked = jnp.concatenate(pieces, axis=0).astype(jnp.bfloat16)
            picked = jnp.dot(onehot, stacked, preferred_element_type=jnp.float32)
            picked = picked.astype(jnp.bfloat16).reshape(2, NX, UNIT, PAIR_WIDTH)
            for zlo in range(2):
                chip = jnp.where(core == 0, 1 - zlo if n == 0 else zlo, n)
                index = jnp.where(core == 0, n, 0 if n == zlo else 1)
                span = slice(half * UNIT, (half + 1) * UNIT)
                for t in range(TILES):
                    tile = picked[zlo, :, :, t * 128 : (t + 1) * 128]
                    out_ref[y, pl.ds(chip * NX, NX), index, t, span] = tile


def pick_blocks(selected, cache):
    count = NY * COUNT
    return pl.pallas_call(
        pick_kernel,
        out_shape=jax.ShapeDtypeStruct((NY, 2 * NX, COUNT, TILES, PAIRS, 128), jnp.bfloat16),
        in_specs=[pl.BlockSpec(memory_space=pltpu.VMEM), pl.BlockSpec(memory_space=pl.ANY)],
        out_specs=pl.BlockSpec(memory_space=pltpu.VMEM),
        scratch_shapes=[
            pltpu.VMEM((count, BLK_DEV, BLOCK * FEAT), jnp.bfloat16),
            pltpu.SemaphoreType.DMA((count,)),
        ],
        compiler_params=pltpu.CompilerParams(vmem_limit_bytes=46 * MIB),
        name="pick_blocks",
    )(selected, cache)


def tie_kernel(*refs):
    pass


def tie(value, *earlier):
    anywhere = pl.BlockSpec(memory_space=pl.ANY)
    return pl.pallas_call(
        tie_kernel,
        out_shape=jax.ShapeDtypeStruct(value.shape, value.dtype),
        in_specs=[anywhere] * (1 + len(earlier)),
        out_specs=anywhere,
        input_output_aliases={0: 0},
        compiler_params=pltpu.CompilerParams(vmem_limit_bytes=MIB),
        name="tie",
    )(value, *earlier)


def spread_queries(packed):
    lane = lax.broadcasted_iota(jnp.int32, (RDEV * HEADS // 2, WIDE), 1)
    even = jnp.where(lane < FEAT, packed[:, :WIDE].astype(jnp.float32), 0.0)
    odd = jnp.where(lane >= KR, packed[:, KL:].astype(jnp.float32), 0.0)
    low = [even, pltpu.roll(odd, FEAT, 1)]
    high = [pltpu.roll(even, KR, 1), odd]
    return low, high


def attend_kernel(i, blocks_ref, selected_ref, _, *refs):
    width = GROUP * PAIRS
    pairs = jnp.concatenate(
        [blocks_ref[:, i, t].reshape(width, 128) for t in range(TILES)], axis=1
    )
    low, high = [], []
    views = [refs[0].at[0], refs[0].at[1]] if i else refs[:-1]
    for query_ref in views:
        parts = spread_queries(query_ref[...])
        low += parts[0]
        high += parts[1]
    query = jnp.concatenate(low, axis=0).astype(jnp.bfloat16)
    shifted = jnp.concatenate(high, axis=0).astype(jnp.bfloat16)
    out_ref = refs[-1]
    y, zhi, zlo, x, core = here()
    first, second = (owner_place(zhi, zlo, c, i) for c in range(2))
    pair = jnp.where(core == 0, first[0], second[0])
    chip = jnp.where(core == 0, first[1], second[1])
    owner = (y * NK + pair) * (2 * NX) + chip * NX + x
    slot = lax.broadcasted_iota(jnp.int32, (1, width), 1) >> 5
    holder = (slot >> 3) * (NK * 2 * NX) + (zhi * (2 * NX) + (slot & 7))
    places = selected_ref[...] >> 3
    lane = lax.broadcasted_iota(jnp.int32, places.shape, 1)
    rows = []
    for j in range(RDEV):
        mine = jnp.sum(jnp.where(lane == RDEV * owner + j, places, 0), axis=1, keepdims=True)
        read = jnp.max(jnp.where(mine == holder, 1.0, 0.0), axis=0, keepdims=True)
        rows.append(jnp.broadcast_to(read, (HEADS // 2, width)))
    valid = jnp.concatenate(rows * 4, axis=0) > 0.5
    dims = (((1,), (1,)), ((), ()))
    odd_keys = pairs[:, KL:]
    even = lax.dot_general(query, pairs[:, :WIDE], dims, preferred_element_type=jnp.float32)
    odd = lax.dot_general(shifted, odd_keys, dims, preferred_element_type=jnp.float32)
    even = jnp.where(valid, even * score_scale, EMPTY)
    odd = jnp.where(valid, odd * score_scale, EMPTY)
    top = jnp.max(jnp.maximum(even, odd), axis=1, keepdims=True)
    even = jnp.where(valid, jnp.exp(even - top), 0.0)
    odd = jnp.where(valid, jnp.exp(odd - top), 0.0)
    total = jnp.maximum(jnp.sum(even + odd, axis=1, keepdims=True), 1.0)
    value = jnp.dot(
        even.astype(jnp.bfloat16), pairs[:, :KL], preferred_element_type=jnp.float32
    )
    odd_value = jnp.dot(odd.astype(jnp.bfloat16), odd_keys, preferred_element_type=jnp.float32)
    value = (value + odd_value[:, KR : KR + KL]) * (1.0 / total)
    level = top + jnp.log(total)
    wide = jnp.transpose(jnp.broadcast_to(level, (2 * ROWS, 128)))[:TAIL]
    high = wide.astype(jnp.bfloat16).astype(jnp.float32)
    middle = (wide - high).astype(jnp.bfloat16).astype(jnp.float32)
    low = wide - high - middle
    line = lax.broadcasted_iota(jnp.int32, wide.shape, 0)
    tail = jnp.where(line == 0, high, jnp.where(line == 1, middle, jnp.where(line == 2, low, 0.0)))
    out_ref[: 2 * ROWS] = value.astype(jnp.bfloat16)
    out_ref[2 * ROWS :, : 2 * ROWS] = tail.astype(jnp.bfloat16)
    out_ref[2 * ROWS :, 2 * ROWS :] = jnp.zeros((TAIL, KL - 2 * ROWS), jnp.bfloat16)


def attend(i, blocks, selected, earlier, *queries):
    local = pl.BlockSpec(memory_space=pltpu.VMEM)
    return pl.pallas_call(
        functools.partial(attend_kernel, i),
        out_shape=jax.ShapeDtypeStruct((2 * ROWS + TAIL, KL), jnp.bfloat16),
        in_specs=[local, local, pl.BlockSpec(memory_space=pl.ANY)] + [local] * len(queries),
        out_specs=local,
        compiler_params=pltpu.CompilerParams(vmem_limit_bytes=24 * MIB),
        cost_estimate=pl.CostEstimate(flops=1, bytes_accessed=1, transcendentals=0),
        name="attend",
    )(blocks, selected, earlier, *queries)


def weigh(values, levels):
    peak = functools.reduce(jnp.maximum, levels)
    weights = [jnp.exp(level - peak) for level in levels]
    total = functools.reduce(jnp.add, weights)
    scale = 1.0 / total
    mean = jnp.zeros((ROWS, KL), jnp.float32)
    for value, weight in zip(values, weights):
        column = jnp.transpose(jnp.broadcast_to(weight * scale, (128, ROWS)))
        factor = jnp.concatenate([column] * (KL // 128), axis=1)
        mean = mean + factor * value.astype(jnp.float32)
    return mean, peak + jnp.log(total)


def halves_of(ref, half):
    tail = ref[2 * ROWS :, half * ROWS : (half + 1) * ROWS].astype(jnp.float32)
    return ref[half * ROWS : (half + 1) * ROWS], jnp.sum(tail, axis=0, keepdims=True)


def premerge_kernel(mine_ref, other_ref, out_ref):
    for half in range(2):
        views = [halves_of(mine_ref, half), halves_of(other_ref, 1 - half)]
        mean, level = weigh([view[0] for view in views], [view[1] for view in views])
        out_ref[half, :ROWS] = mean
        out_ref[half, ROWS:, :ROWS] = jnp.broadcast_to(level, (8, ROWS))
        out_ref[half, ROWS:, ROWS:] = jnp.zeros((8, KL - ROWS), jnp.float32)


def premerge(mine, other):
    return pl.pallas_call(
        premerge_kernel,
        out_shape=jax.ShapeDtypeStruct((2, ROWS + 8, KL), jnp.float32),
        compiler_params=pltpu.CompilerParams(vmem_limit_bytes=8 * MIB),
        name="premerge",
    )(mine, other)


def merge_kernel(state_ref, mine_ref, other_ref, out_ref):
    core = lax.axis_index("head")
    for half in range(2):
        state = (state_ref[half, :ROWS], state_ref[half, ROWS : ROWS + 1, :ROWS])
        views = [state, halves_of(mine_ref, half), halves_of(other_ref, 1 - half)]
        mean, _ = weigh([view[0] for view in views], [view[1] for view in views])
        mean = mean.astype(jnp.bfloat16).reshape(2, RDEV, HEADS // 2, KL)
        for odd in range(2):
            out_ref[:, core ^ half, :, odd * KL : (odd + 1) * KL] = mean[odd]


def merge(parts):
    return pl.pallas_call(
        merge_kernel,
        out_shape=jax.ShapeDtypeStruct((RDEV, 2, HEADS // 2, 2 * KL), jnp.bfloat16),
        compiler_params=pltpu.CompilerParams(vmem_limit_bytes=12 * MIB),
        name="merge",
    )(*parts)


def per_device(queries, cache, selected):
    def move(value, i, back, cross):
        pairs = []
        for zz in range(NZ):
            for c in range(2):
                pair, chip = owner_place(zz // 2, zz % 2, c, i)
                pairs.append((zz * 2 + c, (pair * 2 + chip) * 2 + (c ^ cross)))
        pairs = [pair[::-1] for pair in pairs] if back else pairs
        return lax.ppermute(value, ("zhi", "zlo", "head"), pairs)

    swap = [(0, 1), (1, 0)]
    packed = queries.reshape(ROWS // 2, PAIR_WIDTH)
    asked = [[move(packed, 0, True, cross) for cross in range(2)]]
    both = jnp.stack([packed, lax.ppermute(packed, "head", swap)])
    picked = tie(pick_blocks(selected.T, cache), *asked[0], both)
    picked = picked.reshape(GROUP, COUNT * TILES * PAIRS, 128)
    blocks = lax.all_to_all(picked, ("y", "zlo", "x"), split_axis=0, concat_axis=0, tiled=True)
    blocks = blocks.reshape(GROUP, COUNT, TILES, PAIRS, 128)
    asked.append([move(tie(both, blocks), 1, True, 0)])

    mine, other, earlier = [], [], packed
    for i in range(COUNT):
        part = attend(i, blocks, selected.T, earlier, *asked[i])
        earlier = part
        mine.append(move(part, i, False, 0))
        other.append(lax.ppermute(mine[i], "head", swap))
    state = premerge(mine[0], other[0])
    return merge([state, mine[1], other[1]]).reshape(RDEV, 2 * HEADS * KL)


def solution(mesh):
    grid = Mesh(mesh.devices.reshape(NY, NK, 2, NX, 2), ("y", "zhi", "zlo", "x", "head"))
    seq = ("y", "zhi", "zlo", "x")
    placed = (P(seq, "head"), P(None, seq, None), P())
    return jax.shard_map(
        per_device, mesh=grid, in_specs=placed, out_specs=P(seq, None), check_vma=False
    )
```

time: 105 us -> 104 us (level)
  Pallas kernels: 11.7 us -> 8.89 us
    pallas_call x2, Pallas kernels: 5.65 us -> 4.48 us  [attend(): pl.pallas_call(functools.partial(attend_kernel, i), out_shape=jax.ShapeDt...]
  transfers between devices with their start and end apart: 8 -> 8, of which waited for: 3 -> 3; matrix products, arithmetic and copies ran while one was open for 2% -> 1% of each run, Pallas kernels for 10% -> 8%
where the time goes in v5:
time: 104 us
  blocking collectives  59.9 us (58%)
  starting transfers between devices  25.1 us (24%)
  Pallas kernels  8.89 us (9%)
  waiting for transfers between devices  6.02 us (6%)
  local copies, waits for them, and re-layouts  3.73 us (4%)
    all_to_all x1, blocking collectives, per_device(): lax.all_to_all(picked, ('y', 'zlo', 'x'), split_axis=0, concat_axis=0, ti...  59.9 us
    ppermute x5, starting transfers between devices, move(): return lax.ppermute(value, ('zhi', 'zlo', 'head'), pairs)  16.4 us
    ppermute x2, starting transfers between devices, per_device(): other.append(lax.ppermute(mine[i], 'head', swap))  5.4 us
    ppermute x5, waiting for transfers between devices, move(): return lax.ppermute(value, ('zhi', 'zlo', 'head'), pairs)  4.66 us
    pallas_call x2, Pallas kernels, attend(): pl.pallas_call(functools.partial(attend_kernel, i), out_shape=jax.ShapeDt...  4.48 us
    pallas_call x1, Pallas kernels, pick_blocks(): pl.pallas_call(pick_kernel, out_shape=jax.ShapeDtypeStruct((NY, 2 * NX, C...  3.98 us
    ppermute x1, starting transfers between devices, per_device(): both = jnp.stack([packed, lax.ppermute(packed, 'head', swap)])  3.33 us
  transfers between devices with their start and end apart: 8, of which 3 were waited for; matrix products, arithmetic and copies ran while one was open for 1% of the time, Pallas kernels for 8%

profile of v5, /device:TPU:1, one launch (start us, length us, event | category | flops | bytes accessed | tf_op | source)
XLA Modules:
  0.0 103.8 jit_solution(16670289951190736323)
XLA Ops:
  0.0 1.0 reshape.12._
  1.0 3.3 %collective-permute-start.2 = (bf16[64,1152]{1,0:T(8,128)(2,1)S(1)}, bf16[64,1152]{1,0:T(8,128)(2,1)S(1)}, u32[]{:S(2)}, u32[]{:S(2)}) collective-permute-start(bf16[64,1152]{1,0:T(8,128)(2,1)S(1)} %reshape.12._), channel_id=1, source_target_pairs={{0,1},{1,0},{2,3},{3,2},{4,5},{5,4},{6,7},{7,6},{8,9},{9,8},{10,11... | collective-permute-start | bytes 442376 | tf_op jit(solution)/shard_map/ppermute | solution.py:273
  4.3 4.7 %collective-permute-start.1 = (bf16[64,1152]{1,0:T(8,128)(2,1)S(1)}, bf16[64,1152]{1,0:T(8,128)(2,1)S(1)}, u32[]{:S(2)}, u32[]{:S(2)}) collective-permute-start(bf16[64,1152]{1,0:T(8,128)(2,1)S(1)} %reshape.12._), channel_id=1, source_target_pairs={{41,0},{48,1},{33,8},{24,9},{57,16},{0,17},{49,24},{40,25},{9,32},... | collective-permute-start | bytes 442376 | tf_op jit(solution)/shard_map/ppermute | solution.py:268
  9.0 1.2 %collective-permute-start = (bf16[64,1152]{1,0:T(8,128)(2,1)S(1)}, bf16[64,1152]{1,0:T(8,128)(2,1)S(1)}, u32[]{:S(2)}, u32[]{:S(2)}) collective-permute-start(bf16[64,1152]{1,0:T(8,128)(2,1)S(1)} %reshape.12._), channel_id=1, source_target_pairs={{40,0},{49,1},{32,8},{25,9},{56,16},{1,17},{48,24},{41,25},{8,32},... | collective-permute-start | bytes 442376 | tf_op jit(solution)/shard_map/ppermute | solution.py:268
  10.2 1.0 stack_reshape.3
  11.2 0.0 copy-start
  11.3 0.7 copy-done
  12.0 4.0 %pick_blocks.1.refs_0_ = bf16[4,8,2,9,32,128]{5,4,3,2,1,0:T(8,128)(2,1)S(1)} custom-call(s32[32,256]{1,0:T(8,128)S(1)} %bitcast.12, bf16[16,8,36864]{2,1,0:T(8,128)(2,1)} %cache_ref.1), custom_call_target="tpu_custom_call" | custom-call | tf_op jit(solution)/shard_map/pick_blocks/pallas_call | solution.py:95
  16.0 0.0 collective-permute-done.2
  16.0 2.4 %collective-permute-done.1.refs_2_.refs_1_ = bf16[64,1152]{1,0:T(8,128)(2,1)S(1)} collective-permute-done((bf16[64,1152]{1,0:T(8,128)(2,1)S(1)}, bf16[64,1152]{1,0:T(8,128)(2,1)S(1)}, u32[]{:S(2)}, u32[]{:S(2)}) %collective-permute-start.1) | collective-permute-done | bytes 147488 | tf_op jit(solution)/shard_map/ppermute | solution.py:268
  18.5 0.0 collective-permute-done.refs_1_.refs_0_
  18.5 59.9 %all_to_all.5 = bf16[32,576,128]{2,1,0:T(8,128)(2,1)S(1)} all-to-all(bf16[32,576,128]{2,1,0:T(8,128)(2,1)S(1)} %bitcast.10), channel_id=1, replica_groups=mesh['y'=4,'zhi'=4,'zlo'=2,'x'=4,'head'=2] {'y','zlo','x'}, dimensions={0} | all-to-all | bytes 9437184 | tf_op jit(solution)/shard_map/all_to_all | solution.py:276
  78.4 4.0 %collective-permute-start.5 = (bf16[2,64,1152]{2,1,0:T(8,128)(2,1)S(1)}, bf16[2,64,1152]{2,1,0:T(8,128)(2,1)S(1)}, u32[]{:S(2)}, u32[]{:S(2)}) collective-permute-start(bf16[2,64,1152]{2,1,0:T(8,128)(2,1)S(1)} %tie.3), channel_id=1, source_target_pairs={{0,0},{57,1},{8,8},{17,9},{16,16},{9,17},{24,24},{33,25},{32,32},{... | collective-permute-start | bytes 884744 | tf_op jit(solution)/shard_map/ppermute | solution.py:268
  82.5 2.2 %attend.2._ = bf16[272,512]{1,0:T(8,128)(2,1)S(1)} custom-call(bf16[32,2,9,32,128]{4,3,2,1,0:T(8,128)(2,1)S(1)} %bitcast.8, s32[32,256]{1,0:T(8,128)S(1)} %bitcast.13, bf16[64,1152]{1,0:T(8,128)(2,1)S(1)} %reshape.12._, bf16[64,1152]{1,0:T(8,128)(2,1)S(1)} %collective-permute-done.refs_1_.refs_0_, bf16[64,1152]{1,0:T(8,128)(2,1)S(1)} %collective-permute-done.1.refs_2_.refs_1_), custom_call_target="tpu_custom_call" | custom-call | flops 1 | bytes 1 | tf_op jit(solution)/shard_map/attend/pallas_call | solution.py:193
  84.7 2.4 %collective-permute-start.3 = (bf16[272,512]{1,0:T(8,128)(2,1)S(1)}, bf16[272,512]{1,0:T(8,128)(2,1)S(1)}, u32[]{:S(2)}, u32[]{:S(2)}) collective-permute-start(bf16[272,512]{1,0:T(8,128)(2,1)S(1)} %attend.2._), channel_id=1, source_target_pairs={{0,40},{1,49},{8,32},{9,25},{16,56},{17,1},{24,48},{25,41},{32,8},... | collective-permute-start | bytes 835592 | tf_op jit(solution)/shard_map/ppermute | solution.py:268
  87.1 0.0 collective-permute-done.5.refs_0_
  87.1 2.2 %attend.3 = bf16[272,512]{1,0:T(8,128)(2,1)S(1)} custom-call(bf16[32,2,9,32,128]{4,3,2,1,0:T(8,128)(2,1)S(1)} %bitcast.9, s32[32,256]{1,0:T(8,128)S(1)} %bitcast.14, bf16[272,512]{1,0:T(8,128)(2,1)S(1)} %attend.2._, bf16[2,64,1152]{2,1,0:T(8,128)(2,1)S(1)} %collective-permute-done.5.refs_0_), custom_call_target="tpu_custom_call" | custom-call | flops 1 | bytes 1 | tf_op jit(solution)/shard_map/attend/pallas_call | solution.py:193
  89.4 4.0 %collective-permute-start.6 = (bf16[272,512]{1,0:T(8,128)(2,1)S(1)}, bf16[272,512]{1,0:T(8,128)(2,1)S(1)}, u32[]{:S(2)}, u32[]{:S(2)}) collective-permute-start(bf16[272,512]{1,0:T(8,128)(2,1)S(1)} %attend.3), channel_id=1, source_target_pairs={{0,0},{1,57},{8,8},{9,17},{16,16},{17,9},{24,24},{25,33},{32,32},{... | collective-permute-start | bytes 835592 | tf_op jit(solution)/shard_map/ppermute | solution.py:268
  93.4 0.0 collective-permute-done.3.mine_ref
  93.4 5.4 %collective-permute-start.4 = (bf16[272,512]{1,0:T(8,128)(2,1)S(1)}, bf16[272,512]{1,0:T(8,128)(2,1)S(1)}, u32[]{:S(2)}, u32[]{:S(2)}) collective-permute-start(bf16[272,512]{1,0:T(8,128)(2,1)S(1)} %collective-permute-done.3.mine_ref), channel_id=1, source_target_pairs={{0,1},{1,0},{2,3},{3,2},{4,5},{5,4},{6,7},{7,6},{8,9},{9,8},{10,11... | collective-permute-start | bytes 835592 | tf_op jit(solution)/shard_map/ppermute | solution.py:285
  98.8 2.2 %collective-permute-done.6.mine_ref = bf16[272,512]{1,0:T(8,128)(2,1)S(1)} collective-permute-done((bf16[272,512]{1,0:T(8,128)(2,1)S(1)}, bf16[272,512]{1,0:T(8,128)(2,1)S(1)}, u32[]{:S(2)}, u32[]{:S(2)}) %collective-permute-start.6) | collective-permute-done | bytes 278560 | tf_op jit(solution)/shard_map/ppermute | solution.py:268
  101.0 0.0 collective-permute-start.7
  101.0 0.0 collective-permute-done.4.other_ref
  101.0 0.2 premerge.1.state_ref
  101.2 1.4 %collective-permute-done.7.other_ref = bf16[272,512]{1,0:T(8,128)(2,1)S(1)} collective-permute-done((bf16[272,512]{1,0:T(8,128)(2,1)S(1)}, bf16[272,512]{1,0:T(8,128)(2,1)S(1)}, u32[]{:S(2)}, u32[]{:S(2)}) %collective-permute-start.7) | collective-permute-done | bytes 278560 | tf_op jit(solution)/shard_map/ppermute | solution.py:285
  102.6 0.2 merge.1
  102.8 1.0 copy.6
  (3 shorter events, 0.0 us)
Async XLA Ops:
  1.0 15.0 %collective-permute-start.2 = (bf16[64,1152]{1,0:T(8,128)(2,1)S(1)}, bf16[64,1152]{1,0:T(8,128)(2,1)S(1)}, u32[]{:S(2)}, u32[]{:S(2)}) collective-permute-start(bf16[64,1152]{1,0:T(8,128)(2,1)S(1)} %reshape.12._), channel_id=1, source_target_pairs={{0,1},{1,0},{2,3},{3,2},{4,5},{5,4},{6,7},{7,6},{8,9},{9,8},{10,11... | collective-permute-start | bytes 442376 | tf_op jit(solution)/shard_map/ppermute | solution.py:273
  4.3 14.1 %collective-permute-start.1 = (bf16[64,1152]{1,0:T(8,128)(2,1)S(1)}, bf16[64,1152]{1,0:T(8,128)(2,1)S(1)}, u32[]{:S(2)}, u32[]{:S(2)}) collective-permute-start(bf16[64,1152]{1,0:T(8,128)(2,1)S(1)} %reshape.12._), channel_id=1, source_target_pairs={{41,0},{48,1},{33,8},{24,9},{57,16},{0,17},{49,24},{40,25},{9,32},... | collective-permute-start | bytes 442376 | tf_op jit(solution)/shard_map/ppermute | solution.py:268
  9.0 9.4 %collective-permute-start = (bf16[64,1152]{1,0:T(8,128)(2,1)S(1)}, bf16[64,1152]{1,0:T(8,128)(2,1)S(1)}, u32[]{:S(2)}, u32[]{:S(2)}) collective-permute-start(bf16[64,1152]{1,0:T(8,128)(2,1)S(1)} %reshape.12._), channel_id=1, source_target_pairs={{40,0},{49,1},{32,8},{25,9},{56,16},{1,17},{48,24},{41,25},{8,32},... | collective-permute-start | bytes 442376 | tf_op jit(solution)/shard_map/ppermute | solution.py:268
  11.2 0.8 copy-start
  78.4 8.7 %collective-permute-start.5 = (bf16[2,64,1152]{2,1,0:T(8,128)(2,1)S(1)}, bf16[2,64,1152]{2,1,0:T(8,128)(2,1)S(1)}, u32[]{:S(2)}, u32[]{:S(2)}) collective-permute-start(bf16[2,64,1152]{2,1,0:T(8,128)(2,1)S(1)} %tie.3), channel_id=1, source_target_pairs={{0,0},{57,1},{8,8},{17,9},{16,16},{9,17},{24,24},{33,25},{32,32},{... | collective-permute-start | bytes 884744 | tf_op jit(solution)/shard_map/ppermute | solution.py:268
  84.7 8.7 %collective-permute-start.3 = (bf16[272,512]{1,0:T(8,128)(2,1)S(1)}, bf16[272,512]{1,0:T(8,128)(2,1)S(1)}, u32[]{:S(2)}, u32[]{:S(2)}) collective-permute-start(bf16[272,512]{1,0:T(8,128)(2,1)S(1)} %attend.2._), channel_id=1, source_target_pairs={{0,40},{1,49},{8,32},{9,25},{16,56},{17,1},{24,48},{25,41},{32,8},... | collective-permute-start | bytes 835592 | tf_op jit(solution)/shard_map/ppermute | solution.py:268
  89.4 11.7 %collective-permute-start.6 = (bf16[272,512]{1,0:T(8,128)(2,1)S(1)}, bf16[272,512]{1,0:T(8,128)(2,1)S(1)}, u32[]{:S(2)}, u32[]{:S(2)}) collective-permute-start(bf16[272,512]{1,0:T(8,128)(2,1)S(1)} %attend.3), channel_id=1, source_target_pairs={{0,0},{1,57},{8,8},{9,17},{16,16},{17,9},{24,24},{25,33},{32,32},{... | collective-permute-start | bytes 835592 | tf_op jit(solution)/shard_map/ppermute | solution.py:268
  93.4 7.6 %collective-permute-start.4 = (bf16[272,512]{1,0:T(8,128)(2,1)S(1)}, bf16[272,512]{1,0:T(8,128)(2,1)S(1)}, u32[]{:S(2)}, u32[]{:S(2)}) collective-permute-start(bf16[272,512]{1,0:T(8,128)(2,1)S(1)} %collective-permute-done.3.mine_ref), channel_id=1, source_target_pairs={{0,1},{1,0},{2,3},{3,2},{4,5},{5,4},{6,7},{7,6},{8,9},{9,8},{10,11... | collective-permute-start | bytes 835592 | tf_op jit(solution)/shard_map/ppermute | solution.py:285
  101.0 1.6 %collective-permute-start.7 = (bf16[272,512]{1,0:T(8,128)(2,1)S(1)}, bf16[272,512]{1,0:T(8,128)(2,1)S(1)}, u32[]{:S(2)}, u32[]{:S(2)}) collective-permute-start(bf16[272,512]{1,0:T(8,128)(2,1)S(1)} %collective-permute-done.6.mine_ref), channel_id=1, source_target_pairs={{0,1},{1,0},{2,3},{3,2},{4,5},{5,4},{6,7},{7,6},{8,9},{9,8},{10,11... | collective-permute-start | bytes 835592 | tf_op jit(solution)/shard_map/ppermute | solution.py:285

commit v6 on v5

--- a/solution.py
+++ b/solution.py
@@ -46,7 +46,9 @@
     return tuple(lax.axis_index(name) for name in ("y", "zhi", "zlo", "x", "head"))
 
 
-def pick_kernel(selected_ref, cache_ref, out_ref, held_ref, sems):
+def pick_kernel(
+    selected_ref, cache_ref, packed_ref, swapped_ref, out_ref, both_ref, held_ref, table_ref, sems
+):
     steps = [(y, n) for y in range(NY) for n in range(COUNT)]
     y, zhi, zlo, x, core = here()
     pairs = [(zhi + jnp.where(core == 0, 2 - 2 * n, 3 - 2 * n)) % NK for n in range(COUNT)]
@@ -55,10 +57,15 @@
         request = steps[s][0] * NK + pairs[steps[s][1]]
         return pltpu.make_async_copy(cache_ref.at[request], held_ref.at[s], sems.at[s])
 
+    table = pltpu.make_async_copy(selected_ref, table_ref, sems.at[len(steps)])
+    table.start(priority=1)
     for s in range(len(steps)):
         fetch(s).start(priority=s % 2)
+    both_ref[0] = packed_ref[...]
+    both_ref[1] = swapped_ref[...]
+    table.wait()
     me = ((y * NK + zhi) * 2 + zlo) * NX + x
-    selected = selected_ref[...]
+    selected = table_ref[...]
     inner = jnp.where((selected >> 3) == me, selected & (BLK_DEV - 1), -1)
     inner = jnp.max(inner, axis=0, keepdims=True)
     inner = jnp.maximum(inner, pltpu.roll(inner, SEQ * RDEV - 1, 1))
@@ -90,20 +97,25 @@
                     out_ref[y, pl.ds(chip * NX, NX), index, t, span] = tile
 
 
-def pick_blocks(selected, cache):
+def pick_blocks(selected, cache, packed, swapped):
     count = NY * COUNT
+    local, anywhere = (pl.BlockSpec(memory_space=space) for space in (pltpu.VMEM, pl.ANY))
     return pl.pallas_call(
         pick_kernel,
-        out_shape=jax.ShapeDtypeStruct((NY, 2 * NX, COUNT, TILES, PAIRS, 128), jnp.bfloat16),
-        in_specs=[pl.BlockSpec(memory_space=pltpu.VMEM), pl.BlockSpec(memory_space=pl.ANY)],
-        out_specs=pl.BlockSpec(memory_space=pltpu.VMEM),
+        out_shape=[
+            jax.ShapeDtypeStruct((NY, 2 * NX, COUNT, TILES, PAIRS, 128), jnp.bfloat16),
+            jax.ShapeDtypeStruct((2,) + packed.shape, jnp.bfloat16),
+        ],
+        in_specs=[anywhere, anywhere, local, local],
+        out_specs=[local, local],
         scratch_shapes=[
             pltpu.VMEM((count, BLK_DEV, BLOCK * FEAT), jnp.bfloat16),
-            pltpu.SemaphoreType.DMA((count,)),
+            pltpu.VMEM(selected.shape, jnp.int32),
+            pltpu.SemaphoreType.DMA((count + 1,)),
         ],
         compiler_params=pltpu.CompilerParams(vmem_limit_bytes=46 * MIB),
         name="pick_blocks",
-    )(selected, cache)
+    )(selected, cache, packed, swapped)
 
 
 def tie_kernel(*refs):
@@ -168,9 +180,9 @@
     even = jnp.where(valid, even * score_scale, EMPTY)
     odd = jnp.where(valid, odd * score_scale, EMPTY)
     top = jnp.max(jnp.maximum(even, odd), axis=1, keepdims=True)
-    even = jnp.where(valid, jnp.exp(even - top), 0.0)
-    odd = jnp.where(valid, jnp.exp(odd - top), 0.0)
-    total = jnp.maximum(jnp.sum(even + odd, axis=1, keepdims=True), 1.0)
+    even = jnp.exp(even - top)
+    odd = jnp.exp(odd - top)
+    total = jnp.sum(even + odd, axis=1, keepdims=True)
     value = jnp.dot(
         even.astype(jnp.bfloat16), pairs[:, :KL], preferred_element_type=jnp.float32
     )
@@ -270,8 +282,8 @@
     swap = [(0, 1), (1, 0)]
     packed = queries.reshape(ROWS // 2, PAIR_WIDTH)
     asked = [[move(packed, 0, True, cross) for cross in range(2)]]
-    both = jnp.stack([packed, lax.ppermute(packed, "head", swap)])
-    picked = tie(pick_blocks(selected.T, cache), *asked[0], both)
+    picked, both = pick_blocks(selected.T, cache, packed, lax.ppermute(packed, "head", swap))
+    picked = tie(picked, *asked[0])
     picked = picked.reshape(GROUP, COUNT * TILES * PAIRS, 128)
     blocks = lax.all_to_all(picked, ("y", "zlo", "x"), split_axis=0, concat_axis=0, tiled=True)
     blocks = blocks.reshape(GROUP, COUNT, TILES, PAIRS, 128)

time: 104 us -> 104 us (level)
  waiting for transfers between devices: 6.02 us -> 7.11 us
    ppermute x5, waiting for transfers between devices: 4.66 us -> 5.74 us  [move(): return lax.ppermute(value, ('zhi', 'zlo', 'head'), pairs)]
  transfers between devices with their start and end apart: 8 -> 8, of which waited for: 3 -> 4; matrix products, arithmetic and copies ran while one was open for 1% -> 0% of each run, Pallas kernels for 8% -> 8%
where the time goes in v6:
time: 104 us
  blocking collectives  59.9 us (58%)
  starting transfers between devices  25.2 us (24%)
  Pallas kernels  8.69 us (8%)
  waiting for transfers between devices  7.11 us (7%)
  local copies, waits for them, and re-layouts  2.74 us (3%)
    all_to_all x1, blocking collectives, per_device(): lax.all_to_all(picked, ('y', 'zlo', 'x'), split_axis=0, concat_axis=0, ti...  59.9 us
    ppermute x5, starting transfers between devices, move(): return lax.ppermute(value, ('zhi', 'zlo', 'head'), pairs)  16.4 us
    ppermute x5, waiting for transfers between devices, move(): return lax.ppermute(value, ('zhi', 'zlo', 'head'), pairs)  5.74 us
    ppermute x2, starting transfers between devices, per_device(): other.append(lax.ppermute(mine[i], 'head', swap))  5.43 us
    pallas_call x2, Pallas kernels, attend(): pl.pallas_call(functools.partial(attend_kernel, i), out_shape=jax.ShapeDt...  4.29 us
    pallas_call x1, Pallas kernels, pick_blocks(): pl.pallas_call(pick_kernel, out_shape=[jax.ShapeDtypeStruct((NY, 2 * NX,...  3.99 us
    ppermute x1, starting transfers between devices, per_device(): lax.ppermute(packed, 'head', swap)  3.33 us
  transfers between devices with their start and end apart: 8, of which 4 were waited for; matrix products, arithmetic and copies ran while one was open for 0% of the time, Pallas kernels for 8%

profile of v6, /device:TPU:1, one launch (start us, length us, event | category | flops | bytes accessed | tf_op | source)
XLA Modules:
  0.0 103.7 jit_solution(15008854185854064738)
XLA Ops:
  0.0 1.0 reshape.12.packed_ref._
  1.0 3.3 %collective-permute-start = (bf16[64,1152]{1,0:T(8,128)(2,1)S(1)}, bf16[64,1152]{1,0:T(8,128)(2,1)S(1)}, u32[]{:S(2)}, u32[]{:S(2)}) collective-permute-start(bf16[64,1152]{1,0:T(8,128)(2,1)S(1)} %reshape.12.packed_ref._), channel_id=1, source_target_pairs={{0,1},{1,0},{2,3},{3,2},{4,5},{5,4},{6,7},{7,6},{8,9},{9,8},{10,11... | collective-permute-start | bytes 442376 | tf_op jit(solution)/shard_map/ppermute | solution.py:285
  4.3 4.7 %collective-permute-start.2 = (bf16[64,1152]{1,0:T(8,128)(2,1)S(1)}, bf16[64,1152]{1,0:T(8,128)(2,1)S(1)}, u32[]{:S(2)}, u32[]{:S(2)}) collective-permute-start(bf16[64,1152]{1,0:T(8,128)(2,1)S(1)} %reshape.12.packed_ref._), channel_id=1, source_target_pairs={{41,0},{48,1},{33,8},{24,9},{57,16},{0,17},{49,24},{40,25},{9,32},... | collective-permute-start | bytes 442376 | tf_op jit(solution)/shard_map/ppermute | solution.py:280
  9.0 1.2 %collective-permute-start.1 = (bf16[64,1152]{1,0:T(8,128)(2,1)S(1)}, bf16[64,1152]{1,0:T(8,128)(2,1)S(1)}, u32[]{:S(2)}, u32[]{:S(2)}) collective-permute-start(bf16[64,1152]{1,0:T(8,128)(2,1)S(1)} %reshape.12.packed_ref._), channel_id=1, source_target_pairs={{40,0},{49,1},{32,8},{25,9},{56,16},{1,17},{48,24},{41,25},{8,32},... | collective-permute-start | bytes 442376 | tf_op jit(solution)/shard_map/ppermute | solution.py:280
  10.2 0.0 collective-permute-done.swapped_ref
  10.2 0.0 copy-start
  10.2 0.8 copy-done
  11.0 4.0 %pick_blocks.1 = (bf16[4,8,2,9,32,128]{5,4,3,2,1,0:T(8,128)(2,1)S(1)}, bf16[2,64,1152]{2,1,0:T(8,128)(2,1)S(1)}) custom-call(s32[32,256]{1,0:T(8,128)S(1)} %bitcast.11, bf16[16,8,36864]{2,1,0:T(8,128)(2,1)} %cache_ref.1, bf16[64,1152]{1,0:T(8,128)(2,1)S(1)} %reshape.12.packed_ref._, bf16[64,1152]{1,0:T(8,128)(2,1)S(1)} %collective-permute-done.swapped_ref), custom_call_target="tpu_custom_call" | custom-call | tf_op jit(solution)/shard_map/pick_blocks/pallas_call | solution.py:103
  15.0 3.5 %collective-permute-done.2.refs_2_.refs_1_ = bf16[64,1152]{1,0:T(8,128)(2,1)S(1)} collective-permute-done((bf16[64,1152]{1,0:T(8,128)(2,1)S(1)}, bf16[64,1152]{1,0:T(8,128)(2,1)S(1)}, u32[]{:S(2)}, u32[]{:S(2)}) %collective-permute-start.2) | collective-permute-done | bytes 147488 | tf_op jit(solution)/shard_map/ppermute | solution.py:280
  18.5 0.0 collective-permute-done.1.refs_1_.refs_0_
  18.5 59.9 %all_to_all.5 = bf16[32,576,128]{2,1,0:T(8,128)(2,1)S(1)} all-to-all(bf16[32,576,128]{2,1,0:T(8,128)(2,1)S(1)} %bitcast.9), channel_id=1, replica_groups=mesh['y'=4,'zhi'=4,'zlo'=2,'x'=4,'head'=2] {'y','zlo','x'}, dimensions={0} | all-to-all | bytes 9437184 | tf_op jit(solution)/shard_map/all_to_all | solution.py:288
  78.4 4.0 %collective-permute-start.5 = (bf16[2,64,1152]{2,1,0:T(8,128)(2,1)S(1)}, bf16[2,64,1152]{2,1,0:T(8,128)(2,1)S(1)}, u32[]{:S(2)}, u32[]{:S(2)}) collective-permute-start(bf16[2,64,1152]{2,1,0:T(8,128)(2,1)S(1)} %tie.3), channel_id=1, source_target_pairs={{0,0},{57,1},{8,8},{17,9},{16,16},{9,17},{24,24},{33,25},{32,32},{... | collective-permute-start | bytes 884744 | tf_op jit(solution)/shard_map/ppermute | solution.py:280
  82.5 2.1 %attend.2._ = bf16[272,512]{1,0:T(8,128)(2,1)S(1)} custom-call(bf16[32,2,9,32,128]{4,3,2,1,0:T(8,128)(2,1)S(1)} %bitcast.7, s32[32,256]{1,0:T(8,128)S(1)} %bitcast.12, bf16[64,1152]{1,0:T(8,128)(2,1)S(1)} %reshape.12.packed_ref._, bf16[64,1152]{1,0:T(8,128)(2,1)S(1)} %collective-permute-done.1.refs_1_.refs_0_, ...), custom_call_target="tpu_custom_call" | custom-call | flops 1 | bytes 1 | tf_op jit(solution)/shard_map/attend/pallas_call | solution.py:205
  84.6 2.4 %collective-permute-start.3 = (bf16[272,512]{1,0:T(8,128)(2,1)S(1)}, bf16[272,512]{1,0:T(8,128)(2,1)S(1)}, u32[]{:S(2)}, u32[]{:S(2)}) collective-permute-start(bf16[272,512]{1,0:T(8,128)(2,1)S(1)} %attend.2._), channel_id=1, source_target_pairs={{0,40},{1,49},{8,32},{9,25},{16,56},{17,1},{24,48},{25,41},{32,8},... | collective-permute-start | bytes 835592 | tf_op jit(solution)/shard_map/ppermute | solution.py:280
  87.0 0.1 collective-permute-done.5.refs_0_
  87.1 2.1 %attend.3 = bf16[272,512]{1,0:T(8,128)(2,1)S(1)} custom-call(bf16[32,2,9,32,128]{4,3,2,1,0:T(8,128)(2,1)S(1)} %bitcast.8, s32[32,256]{1,0:T(8,128)S(1)} %bitcast.13, bf16[272,512]{1,0:T(8,128)(2,1)S(1)} %attend.2._, bf16[2,64,1152]{2,1,0:T(8,128)(2,1)S(1)} %collective-permute-done.5.refs_0_), custom_call_target="tpu_custom_call" | custom-call | flops 1 | bytes 1 | tf_op jit(solution)/shard_map/attend/pallas_call | solution.py:205
  89.2 4.1 %collective-permute-start.6 = (bf16[272,512]{1,0:T(8,128)(2,1)S(1)}, bf16[272,512]{1,0:T(8,128)(2,1)S(1)}, u32[]{:S(2)}, u32[]{:S(2)}) collective-permute-start(bf16[272,512]{1,0:T(8,128)(2,1)S(1)} %attend.3), channel_id=1, source_target_pairs={{0,0},{1,57},{8,8},{9,17},{16,16},{17,9},{24,24},{25,33},{32,32},{... | collective-permute-start | bytes 835592 | tf_op jit(solution)/shard_map/ppermute | solution.py:280
  93.3 0.0 collective-permute-done.3.mine_ref
  93.3 5.4 %collective-permute-start.4 = (bf16[272,512]{1,0:T(8,128)(2,1)S(1)}, bf16[272,512]{1,0:T(8,128)(2,1)S(1)}, u32[]{:S(2)}, u32[]{:S(2)}) collective-permute-start(bf16[272,512]{1,0:T(8,128)(2,1)S(1)} %collective-permute-done.3.mine_ref), channel_id=1, source_target_pairs={{0,1},{1,0},{2,3},{3,2},{4,5},{5,4},{6,7},{7,6},{8,9},{9,8},{10,11... | collective-permute-start | bytes 835592 | tf_op jit(solution)/shard_map/ppermute | solution.py:297
  98.7 2.2 %collective-permute-done.6.mine_ref = bf16[272,512]{1,0:T(8,128)(2,1)S(1)} collective-permute-done((bf16[272,512]{1,0:T(8,128)(2,1)S(1)}, bf16[272,512]{1,0:T(8,128)(2,1)S(1)}, u32[]{:S(2)}, u32[]{:S(2)}) %collective-permute-start.6) | collective-permute-done | bytes 278560 | tf_op jit(solution)/shard_map/ppermute | solution.py:280
  100.9 0.0 collective-permute-start.7
  100.9 0.0 collective-permute-done.4.other_ref
  100.9 0.2 premerge.1.state_ref
  101.1 1.4 %collective-permute-done.7.other_ref = bf16[272,512]{1,0:T(8,128)(2,1)S(1)} collective-permute-done((bf16[272,512]{1,0:T(8,128)(2,1)S(1)}, bf16[272,512]{1,0:T(8,128)(2,1)S(1)}, u32[]{:S(2)}, u32[]{:S(2)}) %collective-permute-start.7) | collective-permute-done | bytes 278560 | tf_op jit(solution)/shard_map/ppermute | solution.py:297
  102.5 0.2 merge.1
  102.7 1.0 copy.6
  (2 shorter events, 0.0 us)
Async XLA Ops:
  1.0 9.2 %collective-permute-start = (bf16[64,1152]{1,0:T(8,128)(2,1)S(1)}, bf16[64,1152]{1,0:T(8,128)(2,1)S(1)}, u32[]{:S(2)}, u32[]{:S(2)}) collective-permute-start(bf16[64,1152]{1,0:T(8,128)(2,1)S(1)} %reshape.12.packed_ref._), channel_id=1, source_target_pairs={{0,1},{1,0},{2,3},{3,2},{4,5},{5,4},{6,7},{7,6},{8,9},{9,8},{10,11... | collective-permute-start | bytes 442376 | tf_op jit(solution)/shard_map/ppermute | solution.py:285
  4.3 14.1 %collective-permute-start.2 = (bf16[64,1152]{1,0:T(8,128)(2,1)S(1)}, bf16[64,1152]{1,0:T(8,128)(2,1)S(1)}, u32[]{:S(2)}, u32[]{:S(2)}) collective-permute-start(bf16[64,1152]{1,0:T(8,128)(2,1)S(1)} %reshape.12.packed_ref._), channel_id=1, source_target_pairs={{41,0},{48,1},{33,8},{24,9},{57,16},{0,17},{49,24},{40,25},{9,32},... | collective-permute-start | bytes 442376 | tf_op jit(solution)/shard_map/ppermute | solution.py:280
  9.0 9.4 %collective-permute-start.1 = (bf16[64,1152]{1,0:T(8,128)(2,1)S(1)}, bf16[64,1152]{1,0:T(8,128)(2,1)S(1)}, u32[]{:S(2)}, u32[]{:S(2)}) collective-permute-start(bf16[64,1152]{1,0:T(8,128)(2,1)S(1)} %reshape.12.packed_ref._), channel_id=1, source_target_pairs={{40,0},{49,1},{32,8},{25,9},{56,16},{1,17},{48,24},{41,25},{8,32},... | collective-permute-start | bytes 442376 | tf_op jit(solution)/shard_map/ppermute | solution.py:280
  10.2 0.8 copy-start
  78.4 8.7 %collective-permute-start.5 = (bf16[2,64,1152]{2,1,0:T(8,128)(2,1)S(1)}, bf16[2,64,1152]{2,1,0:T(8,128)(2,1)S(1)}, u32[]{:S(2)}, u32[]{:S(2)}) collective-permute-start(bf16[2,64,1152]{2,1,0:T(8,128)(2,1)S(1)} %tie.3), channel_id=1, source_target_pairs={{0,0},{57,1},{8,8},{17,9},{16,16},{9,17},{24,24},{33,25},{32,32},{... | collective-permute-start | bytes 884744 | tf_op jit(solution)/shard_map/ppermute | solution.py:280
  84.6 8.7 %collective-permute-start.3 = (bf16[272,512]{1,0:T(8,128)(2,1)S(1)}, bf16[272,512]{1,0:T(8,128)(2,1)S(1)}, u32[]{:S(2)}, u32[]{:S(2)}) collective-permute-start(bf16[272,512]{1,0:T(8,128)(2,1)S(1)} %attend.2._), channel_id=1, source_target_pairs={{0,40},{1,49},{8,32},{9,25},{16,56},{17,1},{24,48},{25,41},{32,8},... | collective-permute-start | bytes 835592 | tf_op jit(solution)/shard_map/ppermute | solution.py:280
  89.2 11.7 %collective-permute-start.6 = (bf16[272,512]{1,0:T(8,128)(2,1)S(1)}, bf16[272,512]{1,0:T(8,128)(2,1)S(1)}, u32[]{:S(2)}, u32[]{:S(2)}) collective-permute-start(bf16[272,512]{1,0:T(8,128)(2,1)S(1)} %attend.3), channel_id=1, source_target_pairs={{0,0},{1,57},{8,8},{9,17},{16,16},{17,9},{24,24},{25,33},{32,32},{... | collective-permute-start | bytes 835592 | tf_op jit(solution)/shard_map/ppermute | solution.py:280
  93.3 7.6 %collective-permute-start.4 = (bf16[272,512]{1,0:T(8,128)(2,1)S(1)}, bf16[272,512]{1,0:T(8,128)(2,1)S(1)}, u32[]{:S(2)}, u32[]{:S(2)}) collective-permute-start(bf16[272,512]{1,0:T(8,128)(2,1)S(1)} %collective-permute-done.3.mine_ref), channel_id=1, source_target_pairs={{0,1},{1,0},{2,3},{3,2},{4,5},{5,4},{6,7},{7,6},{8,9},{9,8},{10,11... | collective-permute-start | bytes 835592 | tf_op jit(solution)/shard_map/ppermute | solution.py:297
  100.9 1.6 %collective-permute-start.7 = (bf16[272,512]{1,0:T(8,128)(2,1)S(1)}, bf16[272,512]{1,0:T(8,128)(2,1)S(1)}, u32[]{:S(2)}, u32[]{:S(2)}) collective-permute-start(bf16[272,512]{1,0:T(8,128)(2,1)S(1)} %collective-permute-done.6.mine_ref), channel_id=1, source_target_pairs={{0,1},{1,0},{2,3},{3,2},{4,5},{5,4},{6,7},{7,6},{8,9},{9,8},{10,11... | collective-permute-start | bytes 835592 | tf_op jit(solution)/shard_map/ppermute | solution.py:297

commit v7 on v5

--- a/solution.py
+++ b/solution.py
@@ -87,14 +87,14 @@
                 span = slice(half * UNIT, (half + 1) * UNIT)
                 for t in range(TILES):
                     tile = picked[zlo, :, :, t * 128 : (t + 1) * 128]
-                    out_ref[y, pl.ds(chip * NX, NX), index, t, span] = tile
+                    out_ref[:, chip, y, index, t, span] = tile
 
 
 def pick_blocks(selected, cache):
     count = NY * COUNT
     return pl.pallas_call(
         pick_kernel,
-        out_shape=jax.ShapeDtypeStruct((NY, 2 * NX, COUNT, TILES, PAIRS, 128), jnp.bfloat16),
+        out_shape=jax.ShapeDtypeStruct((NX, 2, NY, COUNT, TILES, PAIRS, 128), jnp.bfloat16),
         in_specs=[pl.BlockSpec(memory_space=pltpu.VMEM), pl.BlockSpec(memory_space=pl.ANY)],
         out_specs=pl.BlockSpec(memory_space=pltpu.VMEM),
         scratch_shapes=[
@@ -152,7 +152,7 @@
     chip = jnp.where(core == 0, first[1], second[1])
     owner = (y * NK + pair) * (2 * NX) + chip * NX + x
     slot = lax.broadcasted_iota(jnp.int32, (1, width), 1) >> 5
-    holder = (slot >> 3) * (NK * 2 * NX) + (zhi * (2 * NX) + (slot & 7))
+    holder = (slot & 3) * (NK * 2 * NX) + (zhi * (2 * NX) + ((slot >> 2) & 1) * NX + (slot >> 3))
     places = selected_ref[...] >> 3
     lane = lax.broadcasted_iota(jnp.int32, places.shape, 1)
     rows = []
@@ -273,7 +273,7 @@
     both = jnp.stack([packed, lax.ppermute(packed, "head", swap)])
     picked = tie(pick_blocks(selected.T, cache), *asked[0], both)
     picked = picked.reshape(GROUP, COUNT * TILES * PAIRS, 128)
-    blocks = lax.all_to_all(picked, ("y", "zlo", "x"), split_axis=0, concat_axis=0, tiled=True)
+    blocks = lax.all_to_all(picked, ("x", "zlo", "y"), split_axis=0, concat_axis=0, tiled=True)
     blocks = blocks.reshape(GROUP, COUNT, TILES, PAIRS, 128)
     asked.append([move(tie(both, blocks), 1, True, 0)])
 

time: 104 us -> 104 us (level)
  starting transfers between devices: 25.1 us -> 21.7 us
  waiting for transfers between devices: 6.02 us -> 8.47 us
    ppermute x5, starting transfers between devices: 16.4 us -> 10.5 us  [move(): return lax.ppermute(value, ('zhi', 'zlo', 'head'), pairs)]
    ppermute x2, starting transfers between devices: 5.4 us -> 7.89 us  [per_device(): other.append(lax.ppermute(mine[i], 'head', swap))]
    ppermute x5, waiting for transfers between devices: 4.66 us -> 7.1 us  [move(): return lax.ppermute(value, ('zhi', 'zlo', 'head'), pairs)]
  transfers between devices with their start and end apart: 8 -> 8, of which waited for: 3 -> 5; matrix products, arithmetic and copies ran while one was open for 1% -> 1% of each run, Pallas kernels for 8% -> 8%
where the time goes in v7:
time: 104 us
  blocking collectives  60.9 us (59%)
  starting transfers between devices  21.7 us (21%)
  Pallas kernels  8.9 us (9%)
  waiting for transfers between devices  8.47 us (8%)
  local copies, waits for them, and re-layouts  3.73 us (4%)
    all_to_all x1, blocking collectives, per_device(): lax.all_to_all(picked, ('x', 'zlo', 'y'), split_axis=0, concat_axis=0, ti...  60.9 us
    ppermute x5, starting transfers between devices, move(): return lax.ppermute(value, ('zhi', 'zlo', 'head'), pairs)  10.5 us
    ppermute x2, starting transfers between devices, per_device(): other.append(lax.ppermute(mine[i], 'head', swap))  7.89 us
    ppermute x5, waiting for transfers between devices, move(): return lax.ppermute(value, ('zhi', 'zlo', 'head'), pairs)  7.1 us
    pallas_call x2, Pallas kernels, attend(): pl.pallas_call(functools.partial(attend_kernel, i), out_shape=jax.ShapeDt...  4.5 us
    pallas_call x1, Pallas kernels, pick_blocks(): pl.pallas_call(pick_kernel, out_shape=jax.ShapeDtypeStruct((NX, 2, NY, CO...  3.98 us
    ppermute x1, starting transfers between devices, per_device(): both = jnp.stack([packed, lax.ppermute(packed, 'head', swap)])  3.33 us
  transfers between devices with their start and end apart: 8, of which 5 were waited for; matrix products, arithmetic and copies ran while one was open for 1% of the time, Pallas kernels for 8%

profile of v7, /device:TPU:1, one launch (start us, length us, event | category | flops | bytes accessed | tf_op | source)
XLA Modules:
  0.0 103.8 jit_solution(4502948651329789190)
XLA Ops:
  0.0 1.0 reshape.12._
  1.0 3.3 %collective-permute-start.2 = (bf16[64,1152]{1,0:T(8,128)(2,1)S(1)}, bf16[64,1152]{1,0:T(8,128)(2,1)S(1)}, u32[]{:S(2)}, u32[]{:S(2)}) collective-permute-start(bf16[64,1152]{1,0:T(8,128)(2,1)S(1)} %reshape.12._), channel_id=1, source_target_pairs={{0,1},{1,0},{2,3},{3,2},{4,5},{5,4},{6,7},{7,6},{8,9},{9,8},{10,11... | collective-permute-start | bytes 442376 | tf_op jit(solution)/shard_map/ppermute | solution.py:273
  4.3 4.7 %collective-permute-start.1 = (bf16[64,1152]{1,0:T(8,128)(2,1)S(1)}, bf16[64,1152]{1,0:T(8,128)(2,1)S(1)}, u32[]{:S(2)}, u32[]{:S(2)}) collective-permute-start(bf16[64,1152]{1,0:T(8,128)(2,1)S(1)} %reshape.12._), channel_id=1, source_target_pairs={{41,0},{48,1},{33,8},{24,9},{57,16},{0,17},{49,24},{40,25},{9,32},... | collective-permute-start | bytes 442376 | tf_op jit(solution)/shard_map/ppermute | solution.py:268
  9.0 1.2 %collective-permute-start = (bf16[64,1152]{1,0:T(8,128)(2,1)S(1)}, bf16[64,1152]{1,0:T(8,128)(2,1)S(1)}, u32[]{:S(2)}, u32[]{:S(2)}) collective-permute-start(bf16[64,1152]{1,0:T(8,128)(2,1)S(1)} %reshape.12._), channel_id=1, source_target_pairs={{40,0},{49,1},{32,8},{25,9},{56,16},{1,17},{48,24},{41,25},{8,32},... | collective-permute-start | bytes 442376 | tf_op jit(solution)/shard_map/ppermute | solution.py:268
  10.2 1.0 stack_reshape.3
  11.2 0.0 copy-start
  11.3 0.7 copy-done
  12.0 4.0 %pick_blocks.1.refs_0_ = bf16[4,2,4,2,9,32,128]{6,5,4,3,2,1,0:T(8,128)(2,1)S(1)} custom-call(s32[32,256]{1,0:T(8,128)S(1)} %bitcast.12, bf16[16,8,36864]{2,1,0:T(8,128)(2,1)} %cache_ref.1), custom_call_target="tpu_custom_call" | custom-call | tf_op jit(solution)/shard_map/pick_blocks/pallas_call | solution.py:95
  16.0 0.0 collective-permute-done.2
  16.0 2.4 %collective-permute-done.1.refs_2_.refs_1_ = bf16[64,1152]{1,0:T(8,128)(2,1)S(1)} collective-permute-done((bf16[64,1152]{1,0:T(8,128)(2,1)S(1)}, bf16[64,1152]{1,0:T(8,128)(2,1)S(1)}, u32[]{:S(2)}, u32[]{:S(2)}) %collective-permute-start.1) | collective-permute-done | bytes 147488 | tf_op jit(solution)/shard_map/ppermute | solution.py:268
  18.5 0.0 collective-permute-done.refs_1_.refs_0_
  18.5 60.9 %all_to_all.5 = bf16[32,576,128]{2,1,0:T(8,128)(2,1)S(1)} all-to-all(bf16[32,576,128]{2,1,0:T(8,128)(2,1)S(1)} %bitcast.10), channel_id=1, replica_groups=mesh['y'=4,'zhi'=4,'zlo'=2,'x'=4,'head'=2] {'x','zlo','y'}, dimensions={0} | all-to-all | bytes 9437184 | tf_op jit(solution)/shard_map/all_to_all | solution.py:276
  79.3 1.9 %collective-permute-start.5 = (bf16[2,64,1152]{2,1,0:T(8,128)(2,1)S(1)}, bf16[2,64,1152]{2,1,0:T(8,128)(2,1)S(1)}, u32[]{:S(2)}, u32[]{:S(2)}) collective-permute-start(bf16[2,64,1152]{2,1,0:T(8,128)(2,1)S(1)} %tie.3), channel_id=1, source_target_pairs={{0,0},{57,1},{8,8},{17,9},{16,16},{9,17},{24,24},{33,25},{32,32},{... | collective-permute-start | bytes 884744 | tf_op jit(solution)/shard_map/ppermute | solution.py:268
  81.2 2.2 %attend.2._ = bf16[272,512]{1,0:T(8,128)(2,1)S(1)} custom-call(bf16[32,2,9,32,128]{4,3,2,1,0:T(8,128)(2,1)S(1)} %bitcast.8, s32[32,256]{1,0:T(8,128)S(1)} %bitcast.13, bf16[64,1152]{1,0:T(8,128)(2,1)S(1)} %reshape.12._, bf16[64,1152]{1,0:T(8,128)(2,1)S(1)} %collective-permute-done.refs_1_.refs_0_, bf16[64,1152]{1,0:T(8,128)(2,1)S(1)} %collective-permute-done.1.refs_2_.refs_1_), custom_call_target="tpu_custom_call" | custom-call | flops 1 | bytes 1 | tf_op jit(solution)/shard_map/attend/pallas_call | solution.py:193
  83.5 0.6 collective-permute-start.3
  84.1 3.9 %collective-permute-done.5.refs_0_ = bf16[2,64,1152]{2,1,0:T(8,128)(2,1)S(1)} collective-permute-done((bf16[2,64,1152]{2,1,0:T(8,128)(2,1)S(1)}, bf16[2,64,1152]{2,1,0:T(8,128)(2,1)S(1)}, u32[]{:S(2)}, u32[]{:S(2)}) %collective-permute-start.5) | collective-permute-done | bytes 294944 | tf_op jit(solution)/shard_map/ppermute | solution.py:268
  88.0 2.3 %attend.3 = bf16[272,512]{1,0:T(8,128)(2,1)S(1)} custom-call(bf16[32,2,9,32,128]{4,3,2,1,0:T(8,128)(2,1)S(1)} %bitcast.9, s32[32,256]{1,0:T(8,128)S(1)} %bitcast.14, bf16[272,512]{1,0:T(8,128)(2,1)S(1)} %attend.2._, bf16[2,64,1152]{2,1,0:T(8,128)(2,1)S(1)} %collective-permute-done.5.refs_0_), custom_call_target="tpu_custom_call" | custom-call | flops 1 | bytes 1 | tf_op jit(solution)/shard_map/attend/pallas_call | solution.py:193
  90.3 2.0 %collective-permute-start.6 = (bf16[272,512]{1,0:T(8,128)(2,1)S(1)}, bf16[272,512]{1,0:T(8,128)(2,1)S(1)}, u32[]{:S(2)}, u32[]{:S(2)}) collective-permute-start(bf16[272,512]{1,0:T(8,128)(2,1)S(1)} %attend.3), channel_id=1, source_target_pairs={{0,0},{1,57},{8,8},{9,17},{16,16},{17,9},{24,24},{25,33},{32,32},{... | collective-permute-start | bytes 835592 | tf_op jit(solution)/shard_map/ppermute | solution.py:268
  92.3 0.0 collective-permute-done.3.mine_ref
  92.3 7.9 %collective-permute-start.4 = (bf16[272,512]{1,0:T(8,128)(2,1)S(1)}, bf16[272,512]{1,0:T(8,128)(2,1)S(1)}, u32[]{:S(2)}, u32[]{:S(2)}) collective-permute-start(bf16[272,512]{1,0:T(8,128)(2,1)S(1)} %collective-permute-done.3.mine_ref), channel_id=1, source_target_pairs={{0,1},{1,0},{2,3},{3,2},{4,5},{5,4},{6,7},{7,6},{8,9},{9,8},{10,11... | collective-permute-start | bytes 835592 | tf_op jit(solution)/shard_map/ppermute | solution.py:285
  100.2 0.8 collective-permute-done.6.mine_ref
  101.0 0.0 collective-permute-start.7
  101.0 0.4 collective-permute-done.4.other_ref
  101.4 0.2 premerge.1.state_ref
  101.6 1.0 collective-permute-done.7.other_ref
  102.6 0.2 merge.1
  102.8 1.0 copy.6
  (3 shorter events, 0.0 us)
Async XLA Ops:
  1.0 15.0 %collective-permute-start.2 = (bf16[64,1152]{1,0:T(8,128)(2,1)S(1)}, bf16[64,1152]{1,0:T(8,128)(2,1)S(1)}, u32[]{:S(2)}, u32[]{:S(2)}) collective-permute-start(bf16[64,1152]{1,0:T(8,128)(2,1)S(1)} %reshape.12._), channel_id=1, source_target_pairs={{0,1},{1,0},{2,3},{3,2},{4,5},{5,4},{6,7},{7,6},{8,9},{9,8},{10,11... | collective-permute-start | bytes 442376 | tf_op jit(solution)/shard_map/ppermute | solution.py:273
  4.3 14.1 %collective-permute-start.1 = (bf16[64,1152]{1,0:T(8,128)(2,1)S(1)}, bf16[64,1152]{1,0:T(8,128)(2,1)S(1)}, u32[]{:S(2)}, u32[]{:S(2)}) collective-permute-start(bf16[64,1152]{1,0:T(8,128)(2,1)S(1)} %reshape.12._), channel_id=1, source_target_pairs={{41,0},{48,1},{33,8},{24,9},{57,16},{0,17},{49,24},{40,25},{9,32},... | collective-permute-start | bytes 442376 | tf_op jit(solution)/shard_map/ppermute | solution.py:268
  9.0 9.4 %collective-permute-start = (bf16[64,1152]{1,0:T(8,128)(2,1)S(1)}, bf16[64,1152]{1,0:T(8,128)(2,1)S(1)}, u32[]{:S(2)}, u32[]{:S(2)}) collective-permute-start(bf16[64,1152]{1,0:T(8,128)(2,1)S(1)} %reshape.12._), channel_id=1, source_target_pairs={{40,0},{49,1},{32,8},{25,9},{56,16},{1,17},{48,24},{41,25},{8,32},... | collective-permute-start | bytes 442376 | tf_op jit(solution)/shard_map/ppermute | solution.py:268
  11.2 0.8 copy-start
  79.3 8.7 %collective-permute-start.5 = (bf16[2,64,1152]{2,1,0:T(8,128)(2,1)S(1)}, bf16[2,64,1152]{2,1,0:T(8,128)(2,1)S(1)}, u32[]{:S(2)}, u32[]{:S(2)}) collective-permute-start(bf16[2,64,1152]{2,1,0:T(8,128)(2,1)S(1)} %tie.3), channel_id=1, source_target_pairs={{0,0},{57,1},{8,8},{17,9},{16,16},{9,17},{24,24},{33,25},{32,32},{... | collective-permute-start | bytes 884744 | tf_op jit(solution)/shard_map/ppermute | solution.py:268
  83.5 8.8 %collective-permute-start.3 = (bf16[272,512]{1,0:T(8,128)(2,1)S(1)}, bf16[272,512]{1,0:T(8,128)(2,1)S(1)}, u32[]{:S(2)}, u32[]{:S(2)}) collective-permute-start(bf16[272,512]{1,0:T(8,128)(2,1)S(1)} %attend.2._), channel_id=1, source_target_pairs={{0,40},{1,49},{8,32},{9,25},{16,56},{17,1},{24,48},{25,41},{32,8},... | collective-permute-start | bytes 835592 | tf_op jit(solution)/shard_map/ppermute | solution.py:268
  90.3 10.8 %collective-permute-start.6 = (bf16[272,512]{1,0:T(8,128)(2,1)S(1)}, bf16[272,512]{1,0:T(8,128)(2,1)S(1)}, u32[]{:S(2)}, u32[]{:S(2)}) collective-permute-start(bf16[272,512]{1,0:T(8,128)(2,1)S(1)} %attend.3), channel_id=1, source_target_pairs={{0,0},{1,57},{8,8},{9,17},{16,16},{17,9},{24,24},{25,33},{32,32},{... | collective-permute-start | bytes 835592 | tf_op jit(solution)/shard_map/ppermute | solution.py:268
  92.3 9.1 %collective-permute-start.4 = (bf16[272,512]{1,0:T(8,128)(2,1)S(1)}, bf16[272,512]{1,0:T(8,128)(2,1)S(1)}, u32[]{:S(2)}, u32[]{:S(2)}) collective-permute-start(bf16[272,512]{1,0:T(8,128)(2,1)S(1)} %collective-permute-done.3.mine_ref), channel_id=1, source_target_pairs={{0,1},{1,0},{2,3},{3,2},{4,5},{5,4},{6,7},{7,6},{8,9},{9,8},{10,11... | collective-permute-start | bytes 835592 | tf_op jit(solution)/shard_map/ppermute | solution.py:285
  101.0 1.6 %collective-permute-start.7 = (bf16[272,512]{1,0:T(8,128)(2,1)S(1)}, bf16[272,512]{1,0:T(8,128)(2,1)S(1)}, u32[]{:S(2)}, u32[]{:S(2)}) collective-permute-start(bf16[272,512]{1,0:T(8,128)(2,1)S(1)} %collective-permute-done.6.mine_ref), channel_id=1, source_target_pairs={{0,1},{1,0},{2,3},{3,2},{4,5},{5,4},{6,7},{7,6},{8,9},{9,8},{10,11... | collective-permute-start | bytes 835592 | tf_op jit(solution)/shard_map/ppermute | solution.py:285

commit v8 on v6

--- a/solution.py
+++ b/solution.py
@@ -94,7 +94,7 @@
                 span = slice(half * UNIT, (half + 1) * UNIT)
                 for t in range(TILES):
                     tile = picked[zlo, :, :, t * 128 : (t + 1) * 128]
-                    out_ref[y, pl.ds(chip * NX, NX), index, t, span] = tile
+                    out_ref[:, chip, y, index, t, span] = tile
 
 
 def pick_blocks(selected, cache, packed, swapped):
@@ -103,7 +103,7 @@
     return pl.pallas_call(
         pick_kernel,
         out_shape=[
-            jax.ShapeDtypeStruct((NY, 2 * NX, COUNT, TILES, PAIRS, 128), jnp.bfloat16),
+            jax.ShapeDtypeStruct((NX, 2, NY, COUNT, TILES, PAIRS, 128), jnp.bfloat16),
             jax.ShapeDtypeStruct((2,) + packed.shape, jnp.bfloat16),
         ],
         in_specs=[anywhere, anywhere, local, local],
@@ -164,7 +164,7 @@
     chip = jnp.where(core == 0, first[1], second[1])
     owner = (y * NK + pair) * (2 * NX) + chip * NX + x
     slot = lax.broadcasted_iota(jnp.int32, (1, width), 1) >> 5
-    holder = (slot >> 3) * (NK * 2 * NX) + (zhi * (2 * NX) + (slot & 7))
+    holder = (slot & 3) * (NK * 2 * NX) + (zhi * (2 * NX) + ((slot >> 2) & 1) * NX + (slot >> 3))
     places = selected_ref[...] >> 3
     lane = lax.broadcasted_iota(jnp.int32, places.shape, 1)
     rows = []
@@ -255,15 +255,18 @@
         state = (state_ref[half, :ROWS], state_ref[half, ROWS : ROWS + 1, :ROWS])
         views = [state, halves_of(mine_ref, half), halves_of(other_ref, 1 - half)]
         mean, _ = weigh([view[0] for view in views], [view[1] for view in views])
-        mean = mean.astype(jnp.bfloat16).reshape(2, RDEV, HEADS // 2, KL)
-        for odd in range(2):
-            out_ref[:, core ^ half, :, odd * KL : (odd + 1) * KL] = mean[odd]
+        mean = mean.reshape(2, RDEV, HEADS // 2, KL)
+        for head in range(HEADS):
+            pair, odd = head // 2, head % 2
+            lines = [mean[odd, j, pair : pair + 1] for j in range(RDEV)]
+            lane = pl.multiple_of((core ^ half) * HEADS * KL + head * KL, KL)
+            out_ref[:, pl.ds(lane, KL)] = jnp.concatenate(lines, axis=0).astype(jnp.bfloat16)
 
 
 def merge(parts):
     return pl.pallas_call(
         merge_kernel,
-        out_shape=jax.ShapeDtypeStruct((RDEV, 2, HEADS // 2, 2 * KL), jnp.bfloat16),
+        out_shape=jax.ShapeDtypeStruct((RDEV, 2 * HEADS * KL), jnp.bfloat16),
         compiler_params=pltpu.CompilerParams(vmem_limit_bytes=12 * MIB),
         name="merge",
     )(*parts)
@@ -285,7 +288,7 @@
     picked, both = pick_blocks(selected.T, cache, packed, lax.ppermute(packed, "head", swap))
     picked = tie(picked, *asked[0])
     picked = picked.reshape(GROUP, COUNT * TILES * PAIRS, 128)
-    blocks = lax.all_to_all(picked, ("y", "zlo", "x"), split_axis=0, concat_axis=0, tiled=True)
+    blocks = lax.all_to_all(picked, ("x", "zlo", "y"), split_axis=0, concat_axis=0, tiled=True)
     blocks = blocks.reshape(GROUP, COUNT, TILES, PAIRS, 128)
     asked.append([move(tie(both, blocks), 1, True, 0)])
 
@@ -296,7 +299,7 @@
         mine.append(move(part, i, False, 0))
         other.append(lax.ppermute(mine[i], "head", swap))
     state = premerge(mine[0], other[0])
-    return merge([state, mine[1], other[1]]).reshape(RDEV, 2 * HEADS * KL)
+    return merge([state, mine[1], other[1]])
 
 
 def solution(mesh):

time: 104 us -> 104 us (level)
  starting transfers between devices: 25.2 us -> 21.7 us
  waiting for transfers between devices: 7.11 us -> 9.62 us
    ppermute x5, starting transfers between devices: 16.4 us -> 10.4 us  [move(): return lax.ppermute(value, ('zhi', 'zlo', 'head'), pairs)]
    ppermute x2, starting transfers between devices: 5.43 us -> 7.99 us  [per_device(): other.append(lax.ppermute(mine[i], 'head', swap))]
    ppermute x5, waiting for transfers between devices: 5.74 us -> 8.25 us  [move(): return lax.ppermute(value, ('zhi', 'zlo', 'head'), pairs)]
  transfers between devices with their start and end apart: 8 -> 8, of which waited for: 4 -> 5; matrix products, arithmetic and copies ran while one was open for 0% -> 0% of each run, Pallas kernels for 8% -> 8%
where the time goes in v8:
time: 104 us
  blocking collectives  60.9 us (59%)
  starting transfers between devices  21.7 us (21%)
  Pallas kernels  9.66 us (9%)
  waiting for transfers between devices  9.62 us (9%)
  local copies, waits for them, and re-layouts  1.76 us (2%)
    all_to_all x1, blocking collectives, per_device(): lax.all_to_all(picked, ('x', 'zlo', 'y'), split_axis=0, concat_axis=0, ti...  60.9 us
    ppermute x5, starting transfers between devices, move(): return lax.ppermute(value, ('zhi', 'zlo', 'head'), pairs)  10.4 us
    ppermute x5, waiting for transfers between devices, move(): return lax.ppermute(value, ('zhi', 'zlo', 'head'), pairs)  8.25 us
    ppermute x2, starting transfers between devices, per_device(): other.append(lax.ppermute(mine[i], 'head', swap))  7.99 us
    pallas_call x2, Pallas kernels, attend(): pl.pallas_call(functools.partial(attend_kernel, i), out_shape=jax.ShapeDt...  4.29 us
    pallas_call x1, Pallas kernels, pick_blocks(): pl.pallas_call(pick_kernel, out_shape=[jax.ShapeDtypeStruct((NX, 2, NY, C...  3.99 us
    ppermute x1, starting transfers between devices, per_device(): lax.ppermute(packed, 'head', swap)  3.33 us
  transfers between devices with their start and end apart: 8, of which 5 were waited for; matrix products, arithmetic and copies ran while one was open for 0% of the time, Pallas kernels for 8%

profile of v8, /device:TPU:1, one launch (start us, length us, event | category | flops | bytes accessed | tf_op | source)
XLA Modules:
  0.0 103.7 jit_solution(11069421233595307909)
XLA Ops:
  0.0 1.0 reshape.9.packed_ref._
  1.0 3.3 %collective-permute-start = (bf16[64,1152]{1,0:T(8,128)(2,1)S(1)}, bf16[64,1152]{1,0:T(8,128)(2,1)S(1)}, u32[]{:S(2)}, u32[]{:S(2)}) collective-permute-start(bf16[64,1152]{1,0:T(8,128)(2,1)S(1)} %reshape.9.packed_ref._), channel_id=1, source_target_pairs={{0,1},{1,0},{2,3},{3,2},{4,5},{5,4},{6,7},{7,6},{8,9},{9,8},{10,11... | collective-permute-start | bytes 442376 | tf_op jit(solution)/shard_map/ppermute | solution.py:288
  4.3 4.7 %collective-permute-start.2 = (bf16[64,1152]{1,0:T(8,128)(2,1)S(1)}, bf16[64,1152]{1,0:T(8,128)(2,1)S(1)}, u32[]{:S(2)}, u32[]{:S(2)}) collective-permute-start(bf16[64,1152]{1,0:T(8,128)(2,1)S(1)} %reshape.9.packed_ref._), channel_id=1, source_target_pairs={{41,0},{48,1},{33,8},{24,9},{57,16},{0,17},{49,24},{40,25},{9,32},... | collective-permute-start | bytes 442376 | tf_op jit(solution)/shard_map/ppermute | solution.py:283
  9.0 1.2 %collective-permute-start.1 = (bf16[64,1152]{1,0:T(8,128)(2,1)S(1)}, bf16[64,1152]{1,0:T(8,128)(2,1)S(1)}, u32[]{:S(2)}, u32[]{:S(2)}) collective-permute-start(bf16[64,1152]{1,0:T(8,128)(2,1)S(1)} %reshape.9.packed_ref._), channel_id=1, source_target_pairs={{40,0},{49,1},{32,8},{25,9},{56,16},{1,17},{48,24},{41,25},{8,32},... | collective-permute-start | bytes 442376 | tf_op jit(solution)/shard_map/ppermute | solution.py:283
  10.2 0.0 collective-permute-done.swapped_ref
  10.2 0.0 copy-start
  10.2 0.8 copy-done
  11.0 4.0 %pick_blocks.1 = (bf16[4,2,4,2,9,32,128]{6,5,4,3,2,1,0:T(8,128)(2,1)S(1)}, bf16[2,64,1152]{2,1,0:T(8,128)(2,1)S(1)}) custom-call(s32[32,256]{1,0:T(8,128)S(1)} %bitcast.7, bf16[16,8,36864]{2,1,0:T(8,128)(2,1)} %cache_ref.1, bf16[64,1152]{1,0:T(8,128)(2,1)S(1)} %reshape.9.packed_ref._, bf16[64,1152]{1,0:T(8,128)(2,1)S(1)} %collective-permute-done.swapped_ref), custom_call_target="tpu_custom_call" | custom-call | tf_op jit(solution)/shard_map/pick_blocks/pallas_call | solution.py:103
  15.0 3.5 %collective-permute-done.2.refs_2_.refs_1_ = bf16[64,1152]{1,0:T(8,128)(2,1)S(1)} collective-permute-done((bf16[64,1152]{1,0:T(8,128)(2,1)S(1)}, bf16[64,1152]{1,0:T(8,128)(2,1)S(1)}, u32[]{:S(2)}, u32[]{:S(2)}) %collective-permute-start.2) | collective-permute-done | bytes 147488 | tf_op jit(solution)/shard_map/ppermute | solution.py:283
  18.5 0.0 collective-permute-done.1.refs_1_.refs_0_
  18.5 60.9 %all_to_all.5 = bf16[32,576,128]{2,1,0:T(8,128)(2,1)S(1)} all-to-all(bf16[32,576,128]{2,1,0:T(8,128)(2,1)S(1)} %bitcast.6), channel_id=1, replica_groups=mesh['y'=4,'zhi'=4,'zlo'=2,'x'=4,'head'=2] {'x','zlo','y'}, dimensions={0} | all-to-all | bytes 9437184 | tf_op jit(solution)/shard_map/all_to_all | solution.py:291
  79.3 1.9 %collective-permute-start.5 = (bf16[2,64,1152]{2,1,0:T(8,128)(2,1)S(1)}, bf16[2,64,1152]{2,1,0:T(8,128)(2,1)S(1)}, u32[]{:S(2)}, u32[]{:S(2)}) collective-permute-start(bf16[2,64,1152]{2,1,0:T(8,128)(2,1)S(1)} %tie.3), channel_id=1, source_target_pairs={{0,0},{57,1},{8,8},{17,9},{16,16},{9,17},{24,24},{33,25},{32,32},{... | collective-permute-start | bytes 884744 | tf_op jit(solution)/shard_map/ppermute | solution.py:283
  81.2 2.1 %attend.2._ = bf16[272,512]{1,0:T(8,128)(2,1)S(1)} custom-call(bf16[32,2,9,32,128]{4,3,2,1,0:T(8,128)(2,1)S(1)} %bitcast.4, s32[32,256]{1,0:T(8,128)S(1)} %bitcast.8, bf16[64,1152]{1,0:T(8,128)(2,1)S(1)} %reshape.9.packed_ref._, bf16[64,1152]{1,0:T(8,128)(2,1)S(1)} %collective-permute-done.1.refs_1_.refs_0_, ...), custom_call_target="tpu_custom_call" | custom-call | flops 1 | bytes 1 | tf_op jit(solution)/shard_map/attend/pallas_call | solution.py:205
  83.4 0.6 collective-permute-start.3
  84.0 4.0 %collective-permute-done.5.refs_0_ = bf16[2,64,1152]{2,1,0:T(8,128)(2,1)S(1)} collective-permute-done((bf16[2,64,1152]{2,1,0:T(8,128)(2,1)S(1)}, bf16[2,64,1152]{2,1,0:T(8,128)(2,1)S(1)}, u32[]{:S(2)}, u32[]{:S(2)}) %collective-permute-start.5) | collective-permute-done | bytes 294944 | tf_op jit(solution)/shard_map/ppermute | solution.py:283
  88.0 2.1 %attend.3 = bf16[272,512]{1,0:T(8,128)(2,1)S(1)} custom-call(bf16[32,2,9,32,128]{4,3,2,1,0:T(8,128)(2,1)S(1)} %bitcast.5, s32[32,256]{1,0:T(8,128)S(1)} %bitcast.9, bf16[272,512]{1,0:T(8,128)(2,1)S(1)} %attend.2._, bf16[2,64,1152]{2,1,0:T(8,128)(2,1)S(1)} %collective-permute-done.5.refs_0_), custom_call_target="tpu_custom_call" | custom-call | flops 1 | bytes 1 | tf_op jit(solution)/shard_map/attend/pallas_call | solution.py:205
  90.1 2.0 %collective-permute-start.6 = (bf16[272,512]{1,0:T(8,128)(2,1)S(1)}, bf16[272,512]{1,0:T(8,128)(2,1)S(1)}, u32[]{:S(2)}, u32[]{:S(2)}) collective-permute-start(bf16[272,512]{1,0:T(8,128)(2,1)S(1)} %attend.3), channel_id=1, source_target_pairs={{0,0},{1,57},{8,8},{9,17},{16,16},{17,9},{24,24},{25,33},{32,32},{... | collective-permute-start | bytes 835592 | tf_op jit(solution)/shard_map/ppermute | solution.py:283
  92.1 0.0 collective-permute-done.3.mine_ref
  92.1 8.0 %collective-permute-start.4 = (bf16[272,512]{1,0:T(8,128)(2,1)S(1)}, bf16[272,512]{1,0:T(8,128)(2,1)S(1)}, u32[]{:S(2)}, u32[]{:S(2)}) collective-permute-start(bf16[272,512]{1,0:T(8,128)(2,1)S(1)} %collective-permute-done.3.mine_ref), channel_id=1, source_target_pairs={{0,1},{1,0},{2,3},{3,2},{4,5},{5,4},{6,7},{7,6},{8,9},{9,8},{10,11... | collective-permute-start | bytes 835592 | tf_op jit(solution)/shard_map/ppermute | solution.py:300
  100.1 0.8 collective-permute-done.6.mine_ref
  100.9 0.0 collective-permute-start.7
  100.9 0.4 collective-permute-done.4.other_ref
  101.3 0.2 premerge.1.state_ref
  101.5 1.0 collective-permute-done.7.other_ref
  102.5 1.2 %merge.1 = bf16[2,65536]{1,0:T(2,128)(2,1)} custom-call(f32[2,136,512]{2,1,0:T(8,128)S(1)} %premerge.1.state_ref, bf16[272,512]{1,0:T(8,128)(2,1)S(1)} %collective-permute-done.6.mine_ref, bf16[272,512]{1,0:T(8,128)(2,1)S(1)} %collective-permute-done.7.other_ref), custom_call_target="tpu_custom_call" | custom-call | tf_op jit(solution)/shard_map/merge/pallas_call | solution.py:267
  (2 shorter events, 0.0 us)
Async XLA Ops:
  1.0 9.2 %collective-permute-start = (bf16[64,1152]{1,0:T(8,128)(2,1)S(1)}, bf16[64,1152]{1,0:T(8,128)(2,1)S(1)}, u32[]{:S(2)}, u32[]{:S(2)}) collective-permute-start(bf16[64,1152]{1,0:T(8,128)(2,1)S(1)} %reshape.9.packed_ref._), channel_id=1, source_target_pairs={{0,1},{1,0},{2,3},{3,2},{4,5},{5,4},{6,7},{7,6},{8,9},{9,8},{10,11... | collective-permute-start | bytes 442376 | tf_op jit(solution)/shard_map/ppermute | solution.py:288
  4.3 14.1 %collective-permute-start.2 = (bf16[64,1152]{1,0:T(8,128)(2,1)S(1)}, bf16[64,1152]{1,0:T(8,128)(2,1)S(1)}, u32[]{:S(2)}, u32[]{:S(2)}) collective-permute-start(bf16[64,1152]{1,0:T(8,128)(2,1)S(1)} %reshape.9.packed_ref._), channel_id=1, source_target_pairs={{41,0},{48,1},{33,8},{24,9},{57,16},{0,17},{49,24},{40,25},{9,32},... | collective-permute-start | bytes 442376 | tf_op jit(solution)/shard_map/ppermute | solution.py:283
  9.0 9.4 %collective-permute-start.1 = (bf16[64,1152]{1,0:T(8,128)(2,1)S(1)}, bf16[64,1152]{1,0:T(8,128)(2,1)S(1)}, u32[]{:S(2)}, u32[]{:S(2)}) collective-permute-start(bf16[64,1152]{1,0:T(8,128)(2,1)S(1)} %reshape.9.packed_ref._), channel_id=1, source_target_pairs={{40,0},{49,1},{32,8},{25,9},{56,16},{1,17},{48,24},{41,25},{8,32},... | collective-permute-start | bytes 442376 | tf_op jit(solution)/shard_map/ppermute | solution.py:283
  10.2 0.8 copy-start
  79.3 8.7 %collective-permute-start.5 = (bf16[2,64,1152]{2,1,0:T(8,128)(2,1)S(1)}, bf16[2,64,1152]{2,1,0:T(8,128)(2,1)S(1)}, u32[]{:S(2)}, u32[]{:S(2)}) collective-permute-start(bf16[2,64,1152]{2,1,0:T(8,128)(2,1)S(1)} %tie.3), channel_id=1, source_target_pairs={{0,0},{57,1},{8,8},{17,9},{16,16},{9,17},{24,24},{33,25},{32,32},{... | collective-permute-start | bytes 884744 | tf_op jit(solution)/shard_map/ppermute | solution.py:283
  83.4 8.7 %collective-permute-start.3 = (bf16[272,512]{1,0:T(8,128)(2,1)S(1)}, bf16[272,512]{1,0:T(8,128)(2,1)S(1)}, u32[]{:S(2)}, u32[]{:S(2)}) collective-permute-start(bf16[272,512]{1,0:T(8,128)(2,1)S(1)} %attend.2._), channel_id=1, source_target_pairs={{0,40},{1,49},{8,32},{9,25},{16,56},{17,1},{24,48},{25,41},{32,8},... | collective-permute-start | bytes 835592 | tf_op jit(solution)/shard_map/ppermute | solution.py:283
  90.1 10.8 %collective-permute-start.6 = (bf16[272,512]{1,0:T(8,128)(2,1)S(1)}, bf16[272,512]{1,0:T(8,128)(2,1)S(1)}, u32[]{:S(2)}, u32[]{:S(2)}) collective-permute-start(bf16[272,512]{1,0:T(8,128)(2,1)S(1)} %attend.3), channel_id=1, source_target_pairs={{0,0},{1,57},{8,8},{9,17},{16,16},{17,9},{24,24},{25,33},{32,32},{... | collective-permute-start | bytes 835592 | tf_op jit(solution)/shard_map/ppermute | solution.py:283
  92.1 9.2 %collective-permute-start.4 = (bf16[272,512]{1,0:T(8,128)(2,1)S(1)}, bf16[272,512]{1,0:T(8,128)(2,1)S(1)}, u32[]{:S(2)}, u32[]{:S(2)}) collective-permute-start(bf16[272,512]{1,0:T(8,128)(2,1)S(1)} %collective-permute-done.3.mine_ref), channel_id=1, source_target_pairs={{0,1},{1,0},{2,3},{3,2},{4,5},{5,4},{6,7},{7,6},{8,9},{9,8},{10,11... | collective-permute-start | bytes 835592 | tf_op jit(solution)/shard_map/ppermute | solution.py:300
  100.9 1.6 %collective-permute-start.7 = (bf16[272,512]{1,0:T(8,128)(2,1)S(1)}, bf16[272,512]{1,0:T(8,128)(2,1)S(1)}, u32[]{:S(2)}, u32[]{:S(2)}) collective-permute-start(bf16[272,512]{1,0:T(8,128)(2,1)S(1)} %collective-permute-done.6.mine_ref), channel_id=1, source_target_pairs={{0,1},{1,0},{2,3},{3,2},{4,5},{5,4},{6,7},{7,6},{8,9},{9,8},{10,11... | collective-permute-start | bytes 835592 | tf_op jit(solution)/shard_map/ppermute | solution.py:300

commit v9 on v7

--- a/solution.py
+++ b/solution.py
@@ -270,7 +270,7 @@
     swap = [(0, 1), (1, 0)]
     packed = queries.reshape(ROWS // 2, PAIR_WIDTH)
     asked = [[move(packed, 0, True, cross) for cross in range(2)]]
-    both = jnp.stack([packed, lax.ppermute(packed, "head", swap)])
+    both = jnp.stack([packed, lax.ppermute(tie(packed, asked[0][0]), "head", swap)])
     picked = tie(pick_blocks(selected.T, cache), *asked[0], both)
     picked = picked.reshape(GROUP, COUNT * TILES * PAIRS, 128)
     blocks = lax.all_to_all(picked, ("x", "zlo", "y"), split_axis=0, concat_axis=0, tiled=True)

time: 104 us -> 112 us (1.077)
  waiting for transfers between devices: 8.47 us -> 13.4 us
  blocking collectives: 60.9 us -> 62.7 us
    ppermute x5, waiting for transfers between devices: 7.1 us -> 12 us  [move(): return lax.ppermute(value, ('zhi', 'zlo', 'head'), pairs)]
    ppermute x5, starting transfers between devices: 10.5 us -> 14.1 us  [move(): return lax.ppermute(value, ('zhi', 'zlo', 'head'), pairs)]
    all_to_all x1, blocking collectives: 60.9 us -> 62.7 us  [per_device(): lax.all_to_all(picked, ('x', 'zlo', 'y'), split_axis=0, concat_axis=0, ti...]
    ppermute x2, starting transfers between devices: 7.89 us -> 6.21 us  [per_device(): other.append(lax.ppermute(mine[i], 'head', swap))]
  transfers between devices with their start and end apart: 8 -> 8, of which waited for: 5 -> 4; matrix products, arithmetic and copies ran while one was open for 1% -> 1% of each run, Pallas kernels for 8% -> 8%
where the time goes in v9:
time: 112 us
  blocking collectives  62.7 us (56%)
  starting transfers between devices  22.8 us (20%)
  waiting for transfers between devices  13.4 us (12%)
  Pallas kernels  8.91 us (8%)
  local copies, waits for them, and re-layouts  3.75 us (3%)
    all_to_all x1, blocking collectives, per_device(): lax.all_to_all(picked, ('x', 'zlo', 'y'), split_axis=0, concat_axis=0, ti...  62.7 us
    ppermute x5, starting transfers between devices, move(): return lax.ppermute(value, ('zhi', 'zlo', 'head'), pairs)  14.1 us
    ppermute x5, waiting for transfers between devices, move(): return lax.ppermute(value, ('zhi', 'zlo', 'head'), pairs)  12 us
    ppermute x2, starting transfers between devices, per_device(): other.append(lax.ppermute(mine[i], 'head', swap))  6.21 us
    pallas_call x2, Pallas kernels, attend(): pl.pallas_call(functools.partial(attend_kernel, i), out_shape=jax.ShapeDt...  4.49 us
    pallas_call x1, Pallas kernels, pick_blocks(): pl.pallas_call(pick_kernel, out_shape=jax.ShapeDtypeStruct((NX, 2, NY, CO...  4 us
    ppermute x1, starting transfers between devices, per_device(): lax.ppermute(tie(packed, asked[0][0]), 'head', swap)  2.5 us
  transfers between devices with their start and end apart: 8, of which 4 were waited for; matrix products, arithmetic and copies ran while one was open for 1% of the time, Pallas kernels for 8%

profile of v9, /device:TPU:1, one launch (start us, length us, event | category | flops | bytes accessed | tf_op | source)
XLA Modules:
  0.0 111.6 jit_solution(4357820563960725766)
XLA Ops:
  0.0 1.0 reshape.12._
  1.0 3.9 %collective-permute-start = (bf16[64,1152]{1,0:T(8,128)(2,1)S(1)}, bf16[64,1152]{1,0:T(8,128)(2,1)S(1)}, u32[]{:S(2)}, u32[]{:S(2)}) collective-permute-start(bf16[64,1152]{1,0:T(8,128)(2,1)S(1)} %reshape.12._), channel_id=1, source_target_pairs={{40,0},{49,1},{32,8},{25,9},{56,16},{1,17},{48,24},{41,25},{8,32},... | collective-permute-start | bytes 442376 | tf_op jit(solution)/shard_map/ppermute | solution.py:268
  4.9 6.7 %collective-permute-done.refs_1_.refs_0_ = bf16[64,1152]{1,0:T(8,128)(2,1)S(1)} collective-permute-done((bf16[64,1152]{1,0:T(8,128)(2,1)S(1)}, bf16[64,1152]{1,0:T(8,128)(2,1)S(1)}, u32[]{:S(2)}, u32[]{:S(2)}) %collective-permute-start) | collective-permute-done | bytes 147488 | tf_op jit(solution)/shard_map/ppermute | solution.py:268
  11.7 2.5 %collective-permute-start.2 = (bf16[64,1152]{1,0:T(8,128)(2,1)S(1)}, bf16[64,1152]{1,0:T(8,128)(2,1)S(1)}, u32[]{:S(2)}, u32[]{:S(2)}) collective-permute-start(bf16[64,1152]{1,0:T(8,128)(2,1)S(1)} %tie.3), channel_id=1, source_target_pairs={{0,1},{1,0},{2,3},{3,2},{4,5},{5,4},{6,7},{7,6},{8,9},{9,8},{10,11... | collective-permute-start | bytes 442376 | tf_op jit(solution)/shard_map/ppermute | solution.py:273
  14.2 4.0 %collective-permute-start.1 = (bf16[64,1152]{1,0:T(8,128)(2,1)S(1)}, bf16[64,1152]{1,0:T(8,128)(2,1)S(1)}, u32[]{:S(2)}, u32[]{:S(2)}) collective-permute-start(bf16[64,1152]{1,0:T(8,128)(2,1)S(1)} %reshape.12._), channel_id=1, source_target_pairs={{41,0},{48,1},{33,8},{24,9},{57,16},{0,17},{49,24},{40,25},{9,32},... | collective-permute-start | bytes 442376 | tf_op jit(solution)/shard_map/ppermute | solution.py:268
  18.2 1.0 stack_reshape.3
  19.2 0.0 copy-start
  19.2 0.7 copy-done
  19.9 4.0 %pick_blocks.1.refs_0_ = bf16[4,2,4,2,9,32,128]{6,5,4,3,2,1,0:T(8,128)(2,1)S(1)} custom-call(s32[32,256]{1,0:T(8,128)S(1)} %bitcast.12, bf16[16,8,36864]{2,1,0:T(8,128)(2,1)} %cache_ref.1), custom_call_target="tpu_custom_call" | custom-call | tf_op jit(solution)/shard_map/pick_blocks/pallas_call | solution.py:95
  23.9 0.0 collective-permute-done.2
  24.0 0.0 collective-permute-done.1.refs_2_.refs_1_
  24.0 62.7 %all_to_all.5 = bf16[32,576,128]{2,1,0:T(8,128)(2,1)S(1)} all-to-all(bf16[32,576,128]{2,1,0:T(8,128)(2,1)S(1)} %bitcast.10), channel_id=1, replica_groups=mesh['y'=4,'zhi'=4,'zlo'=2,'x'=4,'head'=2] {'x','zlo','y'}, dimensions={0} | all-to-all | bytes 9437184 | tf_op jit(solution)/shard_map/all_to_all | solution.py:276
  86.7 2.7 %collective-permute-start.5 = (bf16[2,64,1152]{2,1,0:T(8,128)(2,1)S(1)}, bf16[2,64,1152]{2,1,0:T(8,128)(2,1)S(1)}, u32[]{:S(2)}, u32[]{:S(2)}) collective-permute-start(bf16[2,64,1152]{2,1,0:T(8,128)(2,1)S(1)} %tie.5), channel_id=1, source_target_pairs={{0,0},{57,1},{8,8},{17,9},{16,16},{9,17},{24,24},{33,25},{32,32},{... | collective-permute-start | bytes 884744 | tf_op jit(solution)/shard_map/ppermute | solution.py:268
  89.4 2.2 %attend.2._ = bf16[272,512]{1,0:T(8,128)(2,1)S(1)} custom-call(bf16[32,2,9,32,128]{4,3,2,1,0:T(8,128)(2,1)S(1)} %bitcast.8, s32[32,256]{1,0:T(8,128)S(1)} %bitcast.13, bf16[64,1152]{1,0:T(8,128)(2,1)S(1)} %reshape.12._, bf16[64,1152]{1,0:T(8,128)(2,1)S(1)} %collective-permute-done.refs_1_.refs_0_, bf16[64,1152]{1,0:T(8,128)(2,1)S(1)} %collective-permute-done.1.refs_2_.refs_1_), custom_call_target="tpu_custom_call" | custom-call | flops 1 | bytes 1 | tf_op jit(solution)/shard_map/attend/pallas_call | solution.py:193
  91.7 0.7 collective-permute-start.3
  92.4 3.0 %collective-permute-done.5.refs_0_ = bf16[2,64,1152]{2,1,0:T(8,128)(2,1)S(1)} collective-permute-done((bf16[2,64,1152]{2,1,0:T(8,128)(2,1)S(1)}, bf16[2,64,1152]{2,1,0:T(8,128)(2,1)S(1)}, u32[]{:S(2)}, u32[]{:S(2)}) %collective-permute-start.5) | collective-permute-done | bytes 294944 | tf_op jit(solution)/shard_map/ppermute | solution.py:268
  95.4 2.2 %attend.3 = bf16[272,512]{1,0:T(8,128)(2,1)S(1)} custom-call(bf16[32,2,9,32,128]{4,3,2,1,0:T(8,128)(2,1)S(1)} %bitcast.9, s32[32,256]{1,0:T(8,128)S(1)} %bitcast.14, bf16[272,512]{1,0:T(8,128)(2,1)S(1)} %attend.2._, bf16[2,64,1152]{2,1,0:T(8,128)(2,1)S(1)} %collective-permute-done.5.refs_0_), custom_call_target="tpu_custom_call" | custom-call | flops 1 | bytes 1 | tf_op jit(solution)/shard_map/attend/pallas_call | solution.py:193
  97.6 2.7 %collective-permute-start.6 = (bf16[272,512]{1,0:T(8,128)(2,1)S(1)}, bf16[272,512]{1,0:T(8,128)(2,1)S(1)}, u32[]{:S(2)}, u32[]{:S(2)}) collective-permute-start(bf16[272,512]{1,0:T(8,128)(2,1)S(1)} %attend.3), channel_id=1, source_target_pairs={{0,0},{1,57},{8,8},{9,17},{16,16},{17,9},{24,24},{25,33},{32,32},{... | collective-permute-start | bytes 835592 | tf_op jit(solution)/shard_map/ppermute | solution.py:268
  100.3 0.0 collective-permute-done.3.mine_ref
  100.4 6.2 %collective-permute-start.4 = (bf16[272,512]{1,0:T(8,128)(2,1)S(1)}, bf16[272,512]{1,0:T(8,128)(2,1)S(1)}, u32[]{:S(2)}, u32[]{:S(2)}) collective-permute-start(bf16[272,512]{1,0:T(8,128)(2,1)S(1)} %collective-permute-done.3.mine_ref), channel_id=1, source_target_pairs={{0,1},{1,0},{2,3},{3,2},{4,5},{5,4},{6,7},{7,6},{8,9},{9,8},{10,11... | collective-permute-start | bytes 835592 | tf_op jit(solution)/shard_map/ppermute | solution.py:285
  106.6 2.3 %collective-permute-done.6.mine_ref = bf16[272,512]{1,0:T(8,128)(2,1)S(1)} collective-permute-done((bf16[272,512]{1,0:T(8,128)(2,1)S(1)}, bf16[272,512]{1,0:T(8,128)(2,1)S(1)}, u32[]{:S(2)}, u32[]{:S(2)}) %collective-permute-start.6) | collective-permute-done | bytes 278560 | tf_op jit(solution)/shard_map/ppermute | solution.py:268
  108.9 0.0 collective-permute-start.7
  108.9 0.0 collective-permute-done.4.other_ref
  108.9 0.2 premerge.1.state_ref
  109.1 1.4 %collective-permute-done.7.other_ref = bf16[272,512]{1,0:T(8,128)(2,1)S(1)} collective-permute-done((bf16[272,512]{1,0:T(8,128)(2,1)S(1)}, bf16[272,512]{1,0:T(8,128)(2,1)S(1)}, u32[]{:S(2)}, u32[]{:S(2)}) %collective-permute-start.7) | collective-permute-done | bytes 278560 | tf_op jit(solution)/shard_map/ppermute | solution.py:285
  110.4 0.2 merge.1
  110.7 1.0 copy.7
  (5 shorter events, 0.0 us)
Async XLA Ops:
  1.0 10.7 %collective-permute-start = (bf16[64,1152]{1,0:T(8,128)(2,1)S(1)}, bf16[64,1152]{1,0:T(8,128)(2,1)S(1)}, u32[]{:S(2)}, u32[]{:S(2)}) collective-permute-start(bf16[64,1152]{1,0:T(8,128)(2,1)S(1)} %reshape.12._), channel_id=1, source_target_pairs={{40,0},{49,1},{32,8},{25,9},{56,16},{1,17},{48,24},{41,25},{8,32},... | collective-permute-start | bytes 442376 | tf_op jit(solution)/shard_map/ppermute | solution.py:268
  11.7 12.3 %collective-permute-start.2 = (bf16[64,1152]{1,0:T(8,128)(2,1)S(1)}, bf16[64,1152]{1,0:T(8,128)(2,1)S(1)}, u32[]{:S(2)}, u32[]{:S(2)}) collective-permute-start(bf16[64,1152]{1,0:T(8,128)(2,1)S(1)} %tie.3), channel_id=1, source_target_pairs={{0,1},{1,0},{2,3},{3,2},{4,5},{5,4},{6,7},{7,6},{8,9},{9,8},{10,11... | collective-permute-start | bytes 442376 | tf_op jit(solution)/shard_map/ppermute | solution.py:273
  14.2 9.8 %collective-permute-start.1 = (bf16[64,1152]{1,0:T(8,128)(2,1)S(1)}, bf16[64,1152]{1,0:T(8,128)(2,1)S(1)}, u32[]{:S(2)}, u32[]{:S(2)}) collective-permute-start(bf16[64,1152]{1,0:T(8,128)(2,1)S(1)} %reshape.12._), channel_id=1, source_target_pairs={{41,0},{48,1},{33,8},{24,9},{57,16},{0,17},{49,24},{40,25},{9,32},... | collective-permute-start | bytes 442376 | tf_op jit(solution)/shard_map/ppermute | solution.py:268
  19.2 0.8 copy-start
  86.7 8.7 %collective-permute-start.5 = (bf16[2,64,1152]{2,1,0:T(8,128)(2,1)S(1)}, bf16[2,64,1152]{2,1,0:T(8,128)(2,1)S(1)}, u32[]{:S(2)}, u32[]{:S(2)}) collective-permute-start(bf16[2,64,1152]{2,1,0:T(8,128)(2,1)S(1)} %tie.5), channel_id=1, source_target_pairs={{0,0},{57,1},{8,8},{17,9},{16,16},{9,17},{24,24},{33,25},{32,32},{... | collective-permute-start | bytes 884744 | tf_op jit(solution)/shard_map/ppermute | solution.py:268
  91.7 8.7 %collective-permute-start.3 = (bf16[272,512]{1,0:T(8,128)(2,1)S(1)}, bf16[272,512]{1,0:T(8,128)(2,1)S(1)}, u32[]{:S(2)}, u32[]{:S(2)}) collective-permute-start(bf16[272,512]{1,0:T(8,128)(2,1)S(1)} %attend.2._), channel_id=1, source_target_pairs={{0,40},{1,49},{8,32},{9,25},{16,56},{17,1},{24,48},{25,41},{32,8},... | collective-permute-start | bytes 835592 | tf_op jit(solution)/shard_map/ppermute | solution.py:268
  97.6 11.2 %collective-permute-start.6 = (bf16[272,512]{1,0:T(8,128)(2,1)S(1)}, bf16[272,512]{1,0:T(8,128)(2,1)S(1)}, u32[]{:S(2)}, u32[]{:S(2)}) collective-permute-start(bf16[272,512]{1,0:T(8,128)(2,1)S(1)} %attend.3), channel_id=1, source_target_pairs={{0,0},{1,57},{8,8},{9,17},{16,16},{17,9},{24,24},{25,33},{32,32},{... | collective-permute-start | bytes 835592 | tf_op jit(solution)/shard_map/ppermute | solution.py:268
  100.4 8.5 %collective-permute-start.4 = (bf16[272,512]{1,0:T(8,128)(2,1)S(1)}, bf16[272,512]{1,0:T(8,128)(2,1)S(1)}, u32[]{:S(2)}, u32[]{:S(2)}) collective-permute-start(bf16[272,512]{1,0:T(8,128)(2,1)S(1)} %collective-permute-done.3.mine_ref), channel_id=1, source_target_pairs={{0,1},{1,0},{2,3},{3,2},{4,5},{5,4},{6,7},{7,6},{8,9},{9,8},{10,11... | collective-permute-start | bytes 835592 | tf_op jit(solution)/shard_map/ppermute | solution.py:285
  108.9 1.6 %collective-permute-start.7 = (bf16[272,512]{1,0:T(8,128)(2,1)S(1)}, bf16[272,512]{1,0:T(8,128)(2,1)S(1)}, u32[]{:S(2)}, u32[]{:S(2)}) collective-permute-start(bf16[272,512]{1,0:T(8,128)(2,1)S(1)} %collective-permute-done.6.mine_ref), channel_id=1, source_target_pairs={{0,1},{1,0},{2,3},{3,2},{4,5},{5,4},{6,7},{7,6},{8,9},{9,8},{10,11... | collective-permute-start | bytes 835592 | tf_op jit(solution)/shard_map/ppermute | solution.py:285
